TPU v7x, 256 devices: a whole 4x4x8 slice. The times are simulated.
256 devices in a mesh: wide: 32 (over z, y), narrow: 8 (over x, core).
Axes of the slice: x: 4, y: 4, z: 8, core: 2. Of those that a mesh axis runs over, the one named last changes fastest.
Arguments:
- thermal_correction: float32 [1024, 32, 1024], P(('wide', 'narrow')), may hold values from -6 to 6
- forcing_vector: float32 [1024, 32, 1024], P(('wide', 'narrow')), may hold values from -6 to 6
- thermal_transfer_factor: float32 [1024, 32, 1024], P(('wide', 'narrow')), may hold values from 0.3 to 30
- heat_storage_factor: float32 [1024, 32, 1024], P(('wide', 'narrow')), may hold values from 0.1 to 1
- wall_status_code: int32 [1024, 32, 1024], P(('wide', 'narrow')), may hold values from 0 to 2
- block_holder_chip: int32 [768], replicated, may hold values from 0 to 255, as said below
Outputs:
- relaxed_heat_level: float32 [1024, 32, 1024], P(('wide', 'narrow'))
- defect_restricted_grid: float32 [256, 32, 1024], P(('wide', 'narrow'))
Inputs may be any that keep to these rules, and one draw needn't show every extreme that they name: block_holder_chip never falls along the patches; every device owns a run of 2 to 4 consecutive patches, one device exactly 4; the devices' counts come in pairs that sum to 6.
All inputs are finite; a program needn't handle non-finite values.
Results may differ from a plain program's by a relative error of at most 0.0003.
Values sent between devices are 32-bit elements; how exact they have to be, the bound alone decides.
No kernel may reach another device: no remote copies, remote signals or barrier semaphores. Data moves between devices by JAX's collectives and lax.ppermute only.
A program may use at most 192 MiB of HBM per device.

v0:
```python
import functools

import jax
import jax.numpy as jnp
from jax import lax
from jax.experimental import pallas as pl
from jax.experimental.pallas import tpu as pltpu
from jax.sharding import PartitionSpec as P

COLLECT_LIMIT = 56
AXES = ("wide", "narrow")
SPAN = 32
LAYER = 1024
SLOTS = 4
TILES = 4
F32 = jnp.float32
VMEM = pl.BlockSpec(memory_space=pltpu.VMEM)
SMEM = pl.BlockSpec(memory_space=pltpu.SMEM)
HBM = pl.BlockSpec(memory_space=pl.ANY)
FACES = jax.ShapeDtypeStruct((4, SPAN, 128), F32)
FIELD = jax.ShapeDtypeStruct((LAYER, 128), F32)
GHOSTS = pltpu.VMEM((4, SPAN, 128), F32)
PADDED = pltpu.VMEM((SPAN + 2, 48, 128), F32)


def lanes():
    return lax.broadcasted_iota(jnp.int32, (8, 128), 1)


def pick(tile, index):
    return jnp.take_along_axis(tile, index, axis=1, mode="promise_in_bounds")


def turned(tile, by):
    return pltpu.roll(tile, by, axis=1)


def part(xt):
    return pl.ds(8 * xt, 8)


def tile_row(y, zt):
    return pl.ds(pl.multiple_of(SPAN * y + 8 * zt, 8), 8)


def whereabouts(scalars):
    core = scalars[4]
    first, last = scalars[0], scalars[2]
    return core, jnp.where(core == 0, first, last - 4), last - first - 4


def positions(base):
    patch = base + lanes() // 32
    return patch % 2, (patch // 2) % 2, patch // 4


def put_faces(base, ref, faces):
    ix, iy, _ = positions(base)
    lane = lanes()
    for t in range(TILES):
        faces[0, part(t), :] = ref[pl.ds(256 * t, 8, stride=SPAN), :]
        faces[1, part(t), :] = ref[pl.ds(256 * t + 31, 8, stride=SPAN), :]
        faces[2, part(t), :] = jnp.where(iy == 1, ref[part(t), :], ref[pl.ds(31 * SPAN + 8 * t, 8), :])
    index = 32 * (lane // 32) + jnp.where(ix == 1, 0, 31)
    for t in range(TILES):
        found = pick(ref[part(t), :], index)
        for y in range(1, SPAN):
            found = jnp.where(lane % 32 == y, pick(ref[pl.ds(SPAN * y + 8 * t, 8), :], index), found)
        faces[3, part(t), :] = found


def ghosts(where, own, oth, far, post, out):
    core, base, extra = where
    lane = lanes()
    ix, iy, _ = positions(base)
    low = core == 0
    start = jnp.where(low, 4 - extra, extra)
    moved = (lane + 32 * start) % 128
    cut = 128 - 32 * start

    def window(face, slab, rows):
        a, b = oth[face, rows, :], post[slab, rows, :]
        lead = pick(jnp.where(low, a, b), moved)
        tail = pick(jnp.where(low, b, a), moved)
        return jnp.where(lane < cut, lead, tail)

    def sides(face, slab, rows):
        mid = window(face, slab, rows)
        edge = far[slab, rows, :]
        return jnp.where(low, edge, mid), jnp.where(low, mid, edge)

    for t in range(TILES):
        rows = part(t)
        out[0, rows, :], out[1, rows, :] = sides(core, 0, rows)
        below, above = sides(2, 1, rows)
        inner = turned(own[2, rows, :], 64)
        out[2, rows, :] = jnp.where(
            iy == 1,
            jnp.where(lane < 64, turned(below, 64), inner),
            jnp.where(lane < 64, inner, turned(above, 64)),
        )
        below, above = sides(3, 2, rows)
        inner = own[3, rows, :]
        out[3, rows, :] = jnp.where(
            ix == 1,
            turned(jnp.where(lane < 96, inner, below), 32),
            turned(jnp.where(lane < 32, above, inner), 96),
        )


def pad(base, ref, ghost, padded, outside):
    _, iy, iz = positions(base)
    for t in range(TILES):
        rows = part(t)
        low_own, high_own = ref[rows, :], ref[pl.ds(31 * SPAN + 8 * t, 8), :]
        padded[0, 8 + 8 * t : 16 + 8 * t, :] = jnp.where(iy == 1, ghost[2, rows, :], outside(low_own))
        padded[SPAN + 1, 8 + 8 * t : 16 + 8 * t, :] = jnp.where(iy == 0, ghost[2, rows, :], outside(high_own))

    def layer(y, carry):
        for t in range(TILES):
            padded[y + 1, 8 + 8 * t : 16 + 8 * t, :] = ref[tile_row(y, t), :]
        padded[y + 1, 7:8, :] = ghost[0, pl.ds(y, 1), :]
        padded[y + 1, 40:41, :] = ghost[1, pl.ds(y, 1), :]
        return carry

    lax.fori_loop(0, SPAN, layer, 0, unroll=4)


def around(y, t, padded, ghost):
    lane = lanes()
    rows = slice(8 + 8 * t, 16 + 8 * t)
    own = padded[y + 1, rows, :]
    beyond = pick(ghost[3, part(t), :], 32 * (lane // 32) + y)
    return own, (
        jnp.where(lane % 32 == 0, beyond, turned(own, 1)),
        jnp.where(lane % 32 == 31, beyond, turned(own, 127)),
        padded[y, rows, :],
        padded[y + 2, rows, :],
        padded[y + 1, 7 + 8 * t : 15 + 8 * t, :],
        padded[y + 1, 9 + 8 * t : 17 + 8 * t, :],
    )


def parity(y):
    return (lax.broadcasted_iota(jnp.int32, (8, 128), 0) + lanes() + y) % 2


def inverted(x):
    guess = pl.reciprocal(x, approx=True)
    return guess * (2.0 - x * guess)


def zero(own):
    return 0.0


def collect_kernel(holder, v, f, k, c, kind, scalars, own, faces, bounds, hv, hf, hk, hc, hkind, sems):
    device = lax.axis_index(AXES)
    core = lax.rem(device, 2)
    source = (v, f, k, c, kind)
    landed = (hv, hf, hk, hc, hkind)
    copies = [pltpu.make_async_copy(source[i], landed[i], sems.at[i]) for i in range(5)]
    counting = pltpu.make_async_copy(holder, bounds, sems.at[5])
    order = (0, 2, 4, 1, 3)
    counting.start()
    for i in order:
        copies[i].start()
    counting.wait()
    count = []
    for bound in (0, 1, 2, 4):
        count.append(jnp.sum((bounds[...] < device - core + bound).astype(jnp.int32)))
        scalars[len(count) - 1] = count[-1]
    scalars[4] = core
    base = jnp.where(core == 0, count[0], count[1])
    for i in order:
        copies[i].wait()
        for j in range(8):
            block = landed[i][:, pl.ds(128 * j, 128)].T
            if i == 4:
                block = 1.0 - 0.5 * block.astype(F32)
            own[i, pl.ds(128 * j, 128), :] = block
        if i in (0, 2, 4):
            put_faces(base, own.at[i], faces.at[pl.ds(2 * i, 4)])


def window_of(scalars):
    core, extra = scalars[4], scalars[2] - scalars[0] - 4
    held = jnp.where(core == 0, scalars[1] - scalars[0], scalars[2] - scalars[1])
    lane = lanes()
    low = core == 0
    index = (lane + jnp.where(low, 0, 32 * held)) % 128
    index_other = (lane + jnp.where(low, 128 - 32 * held, 32 * extra)) % 128
    inside = (lane >= jnp.where(low, 0, 128 - 32 * held)) & (lane < jnp.where(low, 32 * held, 128))
    return lambda own, oth: jnp.where(inside, pick(own, index), pick(oth, index_other))


def face_window_kernel(scalars, own, oth, faces, sent):
    windowed = window_of(scalars)
    for i in range(12):
        for t in range(TILES):
            faces[i, part(t), :] = windowed(own[i, part(t), :], oth[i, part(t), :])
    for i in range(3):
        put_sent(scalars, faces.at[pl.ds(4 * i, 4)], sent.at[pl.ds(3 * i, 3)])


def put_sent(scalars, faces, sent):
    for t in range(TILES):
        sent[0, part(t), :] = faces[scalars[4], part(t), :]
        sent[1, part(t), :] = faces[2, part(t), :]
        sent[2, part(t), :] = faces[3, part(t), :]


def window_kernel(scalars, own, oth, window):
    windowed = window_of(scalars)
    for i in range(5):

        def rows(y, carry):
            for t in range(TILES):
                at = tile_row(y, t)
                window[i, at, :] = windowed(own[i, at, :], oth[i, at, :])
            return carry

        lax.fori_loop(0, SPAN, rows, 0, unroll=8)


def first_kernel(layers, scalars, fields, own, oth, far, post, vo, fo, do, go, faces, sent, ghost, pv, pk, pa):
    v, f, k, c, a = (fields.at[i] for i in range(5))
    where = whereabouts(scalars)
    base = where[1]
    ix, iy, iz = positions(base)
    lane = lanes()
    for number in range(3):
        group, outer = pl.ds(4 * number, 4), pl.ds(3 * number, 3)
        ghosts(where, own.at[group], oth.at[group], far.at[outer], post.at[outer], ghost.at[number])
    for t in range(TILES):
        rows = part(t)
        for face, gone, row in ((0, iz == 0, 0), (1, iz == layers - 1, 31)):
            edge = k[pl.ds(256 * t + row, 8, stride=SPAN), :]
            ghost[1, face, rows, :] = jnp.where(gone, edge, ghost[1, face, rows, :])
            ghost[2, face, rows, :] = jnp.where(gone, 1.0, ghost[2, face, rows, :])
    pad(base, v, ghost.at[0], pv, zero)
    pad(base, k, ghost.at[1], pk, lambda mine: mine)
    pad(base, a, ghost.at[2], pa, lambda mine: 1.0)
    edges = ((lane % 32 == 0) & (ix == 0), (lane % 32 == 31) & (ix == 1))

    def layer(y, carry):
        shade = parity(y)
        for t in range(TILES):
            rows = tile_row(y, t)
            value, values = around(y, t, pv, ghost.at[0])
            heat, heats = around(y, t, pk, ghost.at[1])
            opening, openings = around(y, t, pa, ghost.at[2])
            coefficients = []
            summed = None
            doubled = 2.0 * opening * heat
            for way in range(6):
                heat2, opening2 = heats[way], openings[way]
                if way < 2:
                    heat2 = jnp.where(edges[way], heat, heat2)
                    opening2 = jnp.where(edges[way], 1.0, opening2)
                b = doubled * opening2 * heat2 * inverted(heat + heat2)
                summed = b if summed is None else summed + b
                coefficients.append(jnp.where(edges[way], 0.0, b) if way < 2 else b)
            wall = jnp.where(opening == 0.5, heat, 0.0)
            diagonal = jnp.where(opening == 0.0, 1.0, c[rows, :] + summed + wall)
            inverse = inverted(diagonal)
            total = f[rows, :] * inverse
            fo[rows, :] = total
            do[rows, :] = diagonal
            for way in range(6):
                g = coefficients[way] * inverse
                go[way, rows, :] = g
                total = total + g * values[way]
            vo[rows, :] = jnp.where(shade == 0, total, value)
        return carry

    lax.fori_loop(0, SPAN, layer, 0, unroll=4)
    put_faces(base, vo, faces)
    put_sent(scalars, faces, sent)


def relaxed(y, t, f, g, padded, ghost):
    rows = tile_row(y, t)
    value, values = around(y, t, padded, ghost)
    total = f[rows, :]
    for way in range(6):
        total = total + g[way, rows, :] * values[way]
    return value, total


def sweep_kernel(shade_now, scalars, v, f, g, own, oth, far, post, vo, faces, sent, ghost, padded):
    where = whereabouts(scalars)
    base = where[1]
    ghosts(where, own, oth, far, post, ghost)
    pad(base, v, ghost, padded, zero)

    def layer(y, carry):
        shade = parity(y)
        for t in range(TILES):
            value, total = relaxed(y, t, f, g, padded, ghost)
            vo[tile_row(y, t), :] = jnp.where(shade == shade_now, total, value)
        return carry

    lax.fori_loop(0, SPAN, layer, 0, unroll=8)
    put_faces(base, vo, faces)
    put_sent(scalars, faces, sent)


def residual_kernel(scalars, v, f, g, d, own, oth, far, post, blocks, ghost, padded, pair):
    where = whereabouts(scalars)
    ghosts(where, own, oth, far, post, ghost)
    pad(where[1], v, ghost, padded, zero)
    lane = lanes()
    index = 2 * (lane % 64)

    def layer(y4, carry):
        for half in range(2):
            for t in range(TILES):
                added = None
                for step in range(2):
                    y = 4 * y4 + 2 * half + step
                    value, total = relaxed(y, t, f, g, padded, ghost)
                    rest = d[tile_row(y, t), :] * (total - value)
                    added = rest if added is None else added + rest
                pair[half, part(t), :] = added + turned(added, 127)
        for t in range(2):
            both = []
            for half in range(2):
                even = pair[half, pl.ds(16 * t, 8, stride=2), :]
                odd = pair[half, pl.ds(16 * t + 1, 8, stride=2), :]
                both.append(pick(even + odd, index))
            blocks[pl.ds(pl.multiple_of(16 * y4 + 8 * t, 8), 8), :] = (
                jnp.where(lane < 64, both[0], both[1]) * 0.125
            )
        return carry

    lax.fori_loop(0, 8, layer, 0, unroll=2)


def level_kernel(scalars, v, level, stack):
    core = scalars[4]
    held = jnp.where(core == 0, scalars[1] - scalars[0], scalars[2] - scalars[1])
    for j in range(8):
        stack[:, pl.ds(128 * j, 128)] = v[pl.ds(128 * j, 128), :].T
    for s in range(SLOTS):
        filled = s < held
        source = jnp.where(core == 0, s, jnp.where(filled, 4 - held + s, 0))
        for t in range(TILES):
            rows = pl.ds(pl.multiple_of(32 * source + 8 * t, 8), 8)
            level[s, part(t), :] = jnp.where(filled, stack[rows, :], 0.0)


def coarse_kernel(scalars, own, far, post, grid, table, joined):
    core = scalars[4]
    first, middle, last, next_last = scalars[0], scalars[1], scalars[2], scalars[3]
    mine = jnp.where(core == 0, first, middle)
    mine_end = jnp.where(core == 0, middle, last)
    leader = lax.div(mine + 7, 8) * 8
    held = leader < mine_end
    low = core == 0
    lane = lanes()

    @pl.when(held)
    def _():
        for t in range(16):
            rows = part(t)
            table[0, rows, :] = jnp.where(low, own[0, rows, :], own[1, rows, :])
            table[1, rows, :] = jnp.where(low, own[1, rows, :], own[0, rows, :])
            table[2, rows, :] = jnp.where(low, post[0, rows, :], far[0, rows, :])
            table[3, rows, :] = jnp.where(low, post[1, rows, :], far[1, rows, :])
            table[4, rows, :] = jnp.where(low, far[1, rows, :], post[1, rows, :])

        def source(patch):
            here = patch - first
            there = patch - last
            extra, extra2 = last - first - 4, next_last - last - 4
            entry = jnp.where(here < 4, here, here - extra + 4)
            entry2 = 8 + jnp.where(there < 4, there, there - extra2 + 4)
            entry3 = 16 + patch - next_last
            found = jnp.where(patch < last, entry, jnp.where(patch < next_last, entry2, entry3))
            found = jnp.clip(found, 0, 19)
            return lax.div(found, 4), lax.rem(found, 4)

        for iy in range(2):
            for iz in range(2):
                left, left_slot = source(leader + 2 * iy + 4 * iz)
                right, right_slot = source(leader + 1 + 2 * iy + 4 * iz)
                for y in range(16):
                    for t in range(2):
                        rows = pl.ds(16 * (y // 2) + 8 * t, 8)
                        index = 64 * (y % 2) + lane % 16
                        a = pick(table[left, rows, :], index + 16 * left_slot)
                        b = pick(table[right, rows, :], index + 16 * right_slot)
                        joined[pl.ds(SPAN * (16 * iy + y) + 16 * iz + 8 * t, 8), :] = jnp.where(lane < 16, a, b)
        for j in range(8):
            turn = joined[pl.ds(128 * j, 128), :].T
            grid[0, :, pl.ds(128 * j, 128)] = turn[0:SPAN, :]

    @pl.when(jnp.logical_not(held))
    def _():
        grid[0] = jnp.zeros((SPAN, LAYER), F32)


def call(kernel, out_shape, operands, specs=None, out_specs=None, scratch=(), name=None, limit=32, leading=(SMEM,)):
    return pl.pallas_call(
        kernel,
        out_shape=out_shape,
        in_specs=list(leading) + (specs or [VMEM] * (len(operands) - 1)),
        out_specs=out_specs or jax.tree.map(lambda _: VMEM, out_shape),
        scratch_shapes=list(scratch),
        compiler_params=pltpu.CompilerParams(vmem_limit_bytes=limit * 1024 * 1024),
        name=name,
    )(*operands)


def shards(v, f, k, c, kind, holder):
    devices = lax.axis_size(AXES)
    swap = [(i, i ^ 1) for i in range(devices)]
    reach = [(i, i + 1) for i in range(1, devices - 1, 2)]
    reach = reach + [(b, a) for a, b in reach]
    patches = holder.shape[0]

    def exchange(faces, sent):
        far = lax.ppermute(sent, AXES, reach)
        oth = lax.ppermute(faces, AXES, swap)
        post = lax.ppermute(far, AXES, swap)
        return faces, oth, far, post

    fields = [x.reshape(SLOTS * SPAN, LAYER) for x in (v, f, k, c, kind)]
    five = jax.ShapeDtypeStruct((5, LAYER, 128), F32)
    twelve = jax.ShapeDtypeStruct((12, SPAN, 128), F32)
    nine = jax.ShapeDtypeStruct((9, SPAN, 128), F32)
    three = jax.ShapeDtypeStruct((3, SPAN, 128), F32)
    scalars, own, faces = call(
        collect_kernel,
        [pltpu.SMEM((5,), jnp.int32), pltpu.VMEM(five.shape, F32), pltpu.VMEM(twelve.shape, F32)],
        [holder.reshape(patches // 128, 128), *fields],
        specs=[HBM] * 6,
        leading=[],
        out_specs=[SMEM, VMEM, VMEM],
        scratch=[pltpu.VMEM((patches // 128, 128), jnp.int32)]
        + [pltpu.VMEM(x.shape, x.dtype) for x in fields]
        + [pltpu.SemaphoreType.DMA((6,))],
        name="collect",
        limit=COLLECT_LIMIT,
    )
    faces, sent = call(
        face_window_kernel,
        [twelve, nine],
        [scalars, faces, lax.ppermute(faces, AXES, swap)],
        name="face_window",
    )
    sent, own = lax.optimization_barrier((sent, own))
    far = lax.ppermute(sent, AXES, reach)
    oth = lax.ppermute(faces, AXES, swap)
    window = call(window_kernel, five, [scalars, own, lax.ppermute(own, AXES, swap)], name="window")
    far, window = lax.optimization_barrier((far, window))
    post = lax.ppermute(far, AXES, swap)
    coefficients = jax.ShapeDtypeStruct((6, LAYER, 128), F32)
    wv, wf, wd, wg, faces, sent = call(
        functools.partial(first_kernel, patches // 4),
        [FIELD, FIELD, FIELD, coefficients, FACES, three],
        [scalars, window, faces, oth, far, post],
        scratch=[pltpu.VMEM((3, 4, SPAN, 128), F32)] + [PADDED] * 3,
        name="first",
    )
    for shade in (1, 0, 1):
        wv, faces, sent = call(
            functools.partial(sweep_kernel, shade),
            [FIELD, FACES, three],
            [scalars, wv, wf, wg, *exchange(faces, sent)],
            scratch=[GHOSTS, PADDED],
            name="sweep",
        )
    far = lax.ppermute(sent, AXES, reach)
    oth = lax.ppermute(faces, AXES, swap)
    level = call(
        level_kernel,
        jax.ShapeDtypeStruct((SLOTS, SPAN, LAYER), F32),
        [scalars, wv],
        scratch=[pltpu.VMEM((128, LAYER), F32)],
        name="level",
    )
    far, level = lax.optimization_barrier((far, level))
    post = lax.ppermute(far, AXES, swap)
    blocks = call(
        residual_kernel,
        jax.ShapeDtypeStruct((128, 128), F32),
        [scalars, wv, wf, wg, wd, faces, oth, far, post],
        scratch=[GHOSTS, PADDED, pltpu.VMEM((2, SPAN, 128), F32)],
        name="residual",
    )
    both = jnp.stack([blocks, lax.ppermute(blocks, AXES, swap)], 0)
    downward = [(i, i - 1) for i in range(2, devices, 2)] + [(i, i - 5) for i in range(5, devices, 2)]
    far = lax.ppermute(both, AXES, downward)
    post = lax.ppermute(far, AXES, swap)
    grid = call(
        coarse_kernel,
        jax.ShapeDtypeStruct((1, SPAN, LAYER), F32),
        [scalars, both, far, post],
        scratch=[pltpu.VMEM((5, 128, 128), F32), pltpu.VMEM((LAYER, 128), F32)],
        name="coarse",
    )
    return level, grid


def solution(mesh):
    spec = P(AXES, None, None)
    return jax.shard_map(
        shards,
        mesh=mesh,
        in_specs=(spec, spec, spec, spec, spec, P()),
        out_specs=(spec, spec),
        check_vma=False,
    )
```

profile of v0, /device:TPU:127, one launch (start us, length us, event | category | flops | bytes accessed | tf_op | source)
XLA Modules:
  0.0 93.4 jit_solution(2793201820379656457)
XLA Ops:
  0.6 2.7 %collect.1 = (s32[5]{0:T(128)S(4)}, f32[5,1024,128]{2,1,0:T(8,128)S(1)}, f32[12,32,128]{2,1,0:T(8,128)S(1)}) custom-call(s32[6,128]{1,0:T(8,128)} %bitcast.15, f32[128,1024]{1,0:T(8,128)} %bitcast.9, f32[128,1024]{1,0:T(8,128)} %bitcast.10, f32[128,1024]{1,0:T(8,128)} %bitcast.11, f32[128,1024]{1,0:T(8,128)} %bitcast.12, s32[128,1024]{1,0:T(8,128)} %bitcast.13), custom_call_target="tpu_custom_call" | custom-call | tf_op jit(solution)/shard_map/collect/pallas_call | solution.py:405
  3.4 0.8 collective-permute-start
  4.1 1.1 %collective-permute-done.oth = f32[12,32,128]{2,1,0:T(8,128)S(1)} collective-permute-done((f32[12,32,128]{2,1,0:T(8,128)S(1)}, f32[12,32,128]{2,1,0:T(8,128)S(1)}, u32[]{:S(2)}, u32[]{:S(2)}) %collective-permute-start) | collective-permute-done | bytes 196640 | tf_op jit(solution)/shard_map/ppermute | solution.py:450
  5.2 0.2 face_window.1
  5.4 0.5 collective-permute-start.2
  5.8 4.3 %collective-permute-start.1 = (f32[9,32,128]{2,1,0:T(8,128)S(1)}, f32[9,32,128]{2,1,0:T(8,128)S(1)}, u32[]{:S(2)}, u32[]{:S(2)}) collective-permute-start(f32[9,32,128]{2,1,0:T(8,128)S(1)} %get-tuple-element.32), channel_id=1, source_target_pairs={{1,2},{3,4},{5,6},{7,8},{9,10},{11,12},{13,14},{15,16},{17,18},{19... | collective-permute-start | bytes 442376 | tf_op jit(solution)/shard_map/ppermute | solution.py:454
  10.2 0.1 collective-permute-start.3
  10.3 0.1 collective-permute-done.2.oth
  10.4 2.8 %window.1.fields = f32[5,1024,128]{2,1,0:T(8,128)S(1)} custom-call(s32[5]{0:T(128)S(4)} %get-tuple-element.28.scalars, f32[5,1024,128]{2,1,0:T(8,128)S(1)} %get-tuple-element.33.own, f32[5,1024,128]{2,1,0:T(8,128)S(1)} %collective-permute-done.2.oth), custom_call_target="tpu_custom_call" | custom-call | tf_op jit(solution)/shard_map/window/pallas_call | solution.py:405
  13.2 4.5 %collective-permute-done.1.far = f32[9,32,128]{2,1,0:T(8,128)S(1)} collective-permute-done((f32[9,32,128]{2,1,0:T(8,128)S(1)}, f32[9,32,128]{2,1,0:T(8,128)S(1)}, u32[]{:S(2)}, u32[]{:S(2)}) %collective-permute-start.1) | collective-permute-done | bytes 147488 | tf_op jit(solution)/shard_map/ppermute | solution.py:454
  17.7 0.0 collective-permute-start.4
  17.7 1.4 %collective-permute-done.4.post = f32[9,32,128]{2,1,0:T(8,128)S(1)} collective-permute-done((f32[9,32,128]{2,1,0:T(8,128)S(1)}, f32[9,32,128]{2,1,0:T(8,128)S(1)}, u32[]{:S(2)}, u32[]{:S(2)}) %collective-permute-start.4) | collective-permute-done | bytes 147488 | tf_op jit(solution)/shard_map/ppermute | solution.py:458
  19.1 3.1 %first.1 = (f32[1024,128]{1,0:T(8,128)S(1)}, f32[1024,128]{1,0:T(8,128)S(1)}, f32[1024,128]{1,0:T(8,128)S(1)}, f32[6,1024,128]{2,1,0:T(8,128)S(1)}, f32[4,32,128...) custom-call(s32[5]{0:T(128)S(4)} %get-tuple-element.28.scalars, f32[5,1024,128]{2,1,0:T(8,128)S(1)} %window.1.fields, ...), custom_call_target="tpu_custom_call" | custom-call | tf_op jit(solution)/shard_map/first/pallas_call | solution.py:405
  22.2 4.4 %collective-permute-start.6 = (f32[3,32,128]{2,1,0:T(8,128)S(1)}, f32[3,32,128]{2,1,0:T(8,128)S(1)}, u32[]{:S(2)}, u32[]{:S(2)}) collective-permute-start(f32[3,32,128]{2,1,0:T(8,128)S(1)} %get-tuple-element.41), channel_id=1, source_target_pairs={{1,2},{3,4},{5,6},{7,8},{9,10},{11,12},{13,14},{15,16},{17,18},{19... | collective-permute-start | bytes 147464 | tf_op jit(solution)/shard_map/ppermute | solution.py:424
  26.6 0.1 collective-permute-start.5
  26.7 6.4 %collective-permute-done.6.far = f32[3,32,128]{2,1,0:T(8,128)S(1)} collective-permute-done((f32[3,32,128]{2,1,0:T(8,128)S(1)}, f32[3,32,128]{2,1,0:T(8,128)S(1)}, u32[]{:S(2)}, u32[]{:S(2)}) %collective-permute-start.6) | collective-permute-done | bytes 49184 | tf_op jit(solution)/shard_map/ppermute | solution.py:424
  33.0 0.0 collective-permute-done.5.oth
  33.0 1.2 %collective-permute-done.7.post = f32[3,32,128]{2,1,0:T(8,128)S(1)} collective-permute-done((f32[3,32,128]{2,1,0:T(8,128)S(1)}, f32[3,32,128]{2,1,0:T(8,128)S(1)}, u32[]{:S(2)}, u32[]{:S(2)}) %collective-permute-start.7) | collective-permute-done | bytes 49184 | tf_op jit(solution)/shard_map/ppermute | solution.py:426
  34.3 1.3 %sweep.3 = (f32[1024,128]{1,0:T(8,128)S(1)}, f32[4,32,128]{2,1,0:T(8,128)S(1)}, f32[3,32,128]{2,1,0:T(8,128)S(1)}) custom-call(s32[5]{0:T(128)S(4)} %get-tuple-element.28.scalars, f32[1024,128]{1,0:T(8,128)S(1)} %get-tuple-element.37.v, f32[1024,128]{1,0:T(8,128)S(1)} %get-tuple-element.38.f, f32[6,1024,128]{2,1,0:T(8,128)S(1)} %get-tuple-element.39.g, ...), custom_call_target="tpu_custom_call" | custom-call | tf_op jit(solution)/shard_map/sweep/pallas_call | solution.py:405
  35.6 4.4 %collective-permute-start.9 = (f32[3,32,128]{2,1,0:T(8,128)S(1)}, f32[3,32,128]{2,1,0:T(8,128)S(1)}, u32[]{:S(2)}, u32[]{:S(2)}) collective-permute-start(f32[3,32,128]{2,1,0:T(8,128)S(1)} %get-tuple-element.44), channel_id=1, source_target_pairs={{1,2},{3,4},{5,6},{7,8},{9,10},{11,12},{13,14},{15,16},{17,18},{19... | collective-permute-start | bytes 147464 | tf_op jit(solution)/shard_map/ppermute | solution.py:424
  39.9 0.1 collective-permute-start.8
  40.0 6.4 %collective-permute-done.9.far = f32[3,32,128]{2,1,0:T(8,128)S(1)} collective-permute-done((f32[3,32,128]{2,1,0:T(8,128)S(1)}, f32[3,32,128]{2,1,0:T(8,128)S(1)}, u32[]{:S(2)}, u32[]{:S(2)}) %collective-permute-start.9) | collective-permute-done | bytes 49184 | tf_op jit(solution)/shard_map/ppermute | solution.py:424
  46.4 0.0 collective-permute-start.10
  46.4 0.0 collective-permute-done.8.oth
  46.4 1.2 %collective-permute-done.10.post = f32[3,32,128]{2,1,0:T(8,128)S(1)} collective-permute-done((f32[3,32,128]{2,1,0:T(8,128)S(1)}, f32[3,32,128]{2,1,0:T(8,128)S(1)}, u32[]{:S(2)}, u32[]{:S(2)}) %collective-permute-start.10) | collective-permute-done | bytes 49184 | tf_op jit(solution)/shard_map/ppermute | solution.py:426
  47.6 1.3 %sweep.4 = (f32[1024,128]{1,0:T(8,128)S(1)}, f32[4,32,128]{2,1,0:T(8,128)S(1)}, f32[3,32,128]{2,1,0:T(8,128)S(1)}) custom-call(s32[5]{0:T(128)S(4)} %get-tuple-element.28.scalars, f32[1024,128]{1,0:T(8,128)S(1)} %get-tuple-element.42.v, f32[1024,128]{1,0:T(8,128)S(1)} %get-tuple-element.38.f, f32[6,1024,128]{2,1,0:T(8,128)S(1)} %get-tuple-element.39.g, ...), custom_call_target="tpu_custom_call" | custom-call | tf_op jit(solution)/shard_map/sweep/pallas_call | solution.py:405
  48.9 4.4 %collective-permute-start.12 = (f32[3,32,128]{2,1,0:T(8,128)S(1)}, f32[3,32,128]{2,1,0:T(8,128)S(1)}, u32[]{:S(2)}, u32[]{:S(2)}) collective-permute-start(f32[3,32,128]{2,1,0:T(8,128)S(1)} %get-tuple-element.47), channel_id=1, source_target_pairs={{1,2},{3,4},{5,6},{7,8},{9,10},{11,12},{13,14},{15,16},{17,18},{19... | collective-permute-start | bytes 147464 | tf_op jit(solution)/shard_map/ppermute | solution.py:424
  53.3 0.1 collective-permute-start.11
  53.4 6.4 %collective-permute-done.12.far = f32[3,32,128]{2,1,0:T(8,128)S(1)} collective-permute-done((f32[3,32,128]{2,1,0:T(8,128)S(1)}, f32[3,32,128]{2,1,0:T(8,128)S(1)}, u32[]{:S(2)}, u32[]{:S(2)}) %collective-permute-start.12) | collective-permute-done | bytes 49184 | tf_op jit(solution)/shard_map/ppermute | solution.py:424
  59.8 0.0 collective-permute-start.13
  59.8 0.0 collective-permute-done.11.oth
  59.8 1.2 %collective-permute-done.13.post = f32[3,32,128]{2,1,0:T(8,128)S(1)} collective-permute-done((f32[3,32,128]{2,1,0:T(8,128)S(1)}, f32[3,32,128]{2,1,0:T(8,128)S(1)}, u32[]{:S(2)}, u32[]{:S(2)}) %collective-permute-start.13) | collective-permute-done | bytes 49184 | tf_op jit(solution)/shard_map/ppermute | solution.py:426
  61.0 1.3 %sweep.5 = (f32[1024,128]{1,0:T(8,128)S(1)}, f32[4,32,128]{2,1,0:T(8,128)S(1)}, f32[3,32,128]{2,1,0:T(8,128)S(1)}) custom-call(s32[5]{0:T(128)S(4)} %get-tuple-element.28.scalars, f32[1024,128]{1,0:T(8,128)S(1)} %get-tuple-element.45.v, f32[1024,128]{1,0:T(8,128)S(1)} %get-tuple-element.38.f, f32[6,1024,128]{2,1,0:T(8,128)S(1)} %get-tuple-element.39.g, ...), custom_call_target="tpu_custom_call" | custom-call | tf_op jit(solution)/shard_map/sweep/pallas_call | solution.py:405
  62.3 4.4 %collective-permute-start.14 = (f32[3,32,128]{2,1,0:T(8,128)S(1)}, f32[3,32,128]{2,1,0:T(8,128)S(1)}, u32[]{:S(2)}, u32[]{:S(2)}) collective-permute-start(f32[3,32,128]{2,1,0:T(8,128)S(1)} %get-tuple-element.48), channel_id=1, source_target_pairs={{1,2},{3,4},{5,6},{7,8},{9,10},{11,12},{13,14},{15,16},{17,18},{19... | collective-permute-start | bytes 147464 | tf_op jit(solution)/shard_map/ppermute | solution.py:475
  66.7 0.1 collective-permute-start.15
  66.8 1.0 %level.1 = f32[4,32,1024]{2,1,0:T(8,128)} custom-call(s32[5]{0:T(128)S(4)} %get-tuple-element.28.scalars, f32[1024,128]{1,0:T(8,128)S(1)} %get-tuple-element.49.v), custom_call_target="tpu_custom_call" | custom-call | tf_op jit(solution)/shard_map/level/pallas_call | solution.py:405
  67.8 5.3 %collective-permute-done.14.far = f32[3,32,128]{2,1,0:T(8,128)S(1)} collective-permute-done((f32[3,32,128]{2,1,0:T(8,128)S(1)}, f32[3,32,128]{2,1,0:T(8,128)S(1)}, u32[]{:S(2)}, u32[]{:S(2)}) %collective-permute-start.14) | collective-permute-done | bytes 49184 | tf_op jit(solution)/shard_map/ppermute | solution.py:475
  73.1 0.0 collective-permute-start.16
  73.1 0.0 collective-permute-done.15.oth
  73.1 1.2 %collective-permute-done.16.post = f32[3,32,128]{2,1,0:T(8,128)S(1)} collective-permute-done((f32[3,32,128]{2,1,0:T(8,128)S(1)}, f32[3,32,128]{2,1,0:T(8,128)S(1)}, u32[]{:S(2)}, u32[]{:S(2)}) %collective-permute-start.16) | collective-permute-done | bytes 49184 | tf_op jit(solution)/shard_map/ppermute | solution.py:485
  74.4 1.8 %residual.1 = f32[128,128]{1,0:T(8,128)S(1)} custom-call(s32[5]{0:T(128)S(4)} %get-tuple-element.28.scalars, f32[1024,128]{1,0:T(8,128)S(1)} %get-tuple-element.49.v, f32[1024,128]{1,0:T(8,128)S(1)} %get-tuple-element.38.f, f32[6,1024,128]{2,1,0:T(8,128)S(1)} %get-tuple-element.39.g, f32[1024,128]{1,0:T(8,128)S(1)} %get-tuple-element.51.d, ...), custom_call_target="tpu_custom_call" | custom-call | tf_op jit(solution)/shard_map/residual/pallas_call | solution.py:405
  76.2 0.2 collective-permute-start.17
  76.4 1.1 %collective-permute-done.17 = f32[128,128]{1,0:T(8,128)S(1)} collective-permute-done((f32[128,128]{1,0:T(8,128)S(1)}, f32[128,128]{1,0:T(8,128)S(1)}, u32[]{:S(2)}, u32[]{:S(2)}) %collective-permute-start.17) | collective-permute-done | bytes 65568 | tf_op jit(solution)/shard_map/ppermute | solution.py:493
  77.5 1.9 %collective-permute-start.18 = (f32[2,128,128]{2,1,0:T(8,128)S(1)}, f32[2,128,128]{2,1,0:T(8,128)S(1)}, u32[]{:S(2)}, u32[]{:S(2)}) collective-permute-start(f32[2,128,128]{2,1,0:T(8,128)S(1)} %pad_maximum_fusion.own), channel_id=1, source_target_pairs={{2,1},{4,3},{6,5},{8,7},{10,9},{12,11},{14,13},{16,15},{18,17},{20... | collective-permute-start | bytes 393224 | tf_op jit(solution)/shard_map/ppermute | solution.py:495
  79.4 11.0 %collective-permute-done.18.far = f32[2,128,128]{2,1,0:T(8,128)S(1)} collective-permute-done((f32[2,128,128]{2,1,0:T(8,128)S(1)}, f32[2,128,128]{2,1,0:T(8,128)S(1)}, u32[]{:S(2)}, u32[]{:S(2)}) %collective-permute-start.18) | collective-permute-done | bytes 131104 | tf_op jit(solution)/shard_map/ppermute | solution.py:495
  90.4 0.5 collective-permute-start.19
  90.9 1.0 %collective-permute-done.19.post = f32[2,128,128]{2,1,0:T(8,128)S(1)} collective-permute-done((f32[2,128,128]{2,1,0:T(8,128)S(1)}, f32[2,128,128]{2,1,0:T(8,128)S(1)}, u32[]{:S(2)}, u32[]{:S(2)}) %collective-permute-start.19) | collective-permute-done | bytes 131104 | tf_op jit(solution)/shard_map/ppermute | solution.py:496
  91.9 1.5 %coarse.1 = f32[1,32,1024]{2,1,0:T(8,128)} custom-call(s32[5]{0:T(128)S(4)} %get-tuple-element.28.scalars, f32[2,128,128]{2,1,0:T(8,128)S(1)} %pad_maximum_fusion.own, f32[2,128,128]{2,1,0:T(8,128)S(1)} %collective-permute-done.18.far, f32[2,128,128]{2,1,0:T(8,128)S(1)} %collective-permute-done.19.post), custom_call_target="tpu_custom_call" | custom-call | tf_op jit(solution)/shard_map/coarse/pallas_call | solution.py:405
  (3 shorter events, 0.0 us)
Async XLA Ops:
  3.4 1.8 %collective-permute-start = (f32[12,32,128]{2,1,0:T(8,128)S(1)}, f32[12,32,128]{2,1,0:T(8,128)S(1)}, u32[]{:S(2)}, u32[]{:S(2)}) collective-permute-start(f32[12,32,128]{2,1,0:T(8,128)S(1)} %get-tuple-element.29.own), channel_id=1, source_target_pairs={{0,1},{1,0},{2,3},{3,2},{4,5},{5,4},{6,7},{7,6},{8,9},{9,8},{10,11... | collective-permute-start | bytes 589832 | tf_op jit(solution)/shard_map/ppermute | solution.py:450
  5.4 5.0 %collective-permute-start.2 = (f32[5,1024,128]{2,1,0:T(8,128)S(1)}, f32[5,1024,128]{2,1,0:T(8,128)S(1)}, u32[]{:S(2)}, u32[]{:S(2)}) collective-permute-start(f32[5,1024,128]{2,1,0:T(8,128)S(1)} %get-tuple-element.33.own), channel_id=1, source_target_pairs={{0,1},{1,0},{2,3},{3,2},{4,5},{5,4},{6,7},{7,6},{8,9},{9,8},{10,11... | collective-permute-start | bytes 7864328 | tf_op jit(solution)/shard_map/ppermute | solution.py:456
  5.8 11.9 %collective-permute-start.1 = (f32[9,32,128]{2,1,0:T(8,128)S(1)}, f32[9,32,128]{2,1,0:T(8,128)S(1)}, u32[]{:S(2)}, u32[]{:S(2)}) collective-permute-start(f32[9,32,128]{2,1,0:T(8,128)S(1)} %get-tuple-element.32), channel_id=1, source_target_pairs={{1,2},{3,4},{5,6},{7,8},{9,10},{11,12},{13,14},{15,16},{17,18},{19... | collective-permute-start | bytes 442376 | tf_op jit(solution)/shard_map/ppermute | solution.py:454
  10.2 7.5 %collective-permute-start.3 = (f32[12,32,128]{2,1,0:T(8,128)S(1)}, f32[12,32,128]{2,1,0:T(8,128)S(1)}, u32[]{:S(2)}, u32[]{:S(2)}) collective-permute-start(f32[12,32,128]{2,1,0:T(8,128)S(1)} %get-tuple-element.35.own), channel_id=1, source_target_pairs={{0,1},{1,0},{2,3},{3,2},{4,5},{5,4},{6,7},{7,6},{8,9},{9,8},{10,11... | collective-permute-start | bytes 589832 | tf_op jit(solution)/shard_map/ppermute | solution.py:455
  17.7 1.4 %collective-permute-start.4 = (f32[9,32,128]{2,1,0:T(8,128)S(1)}, f32[9,32,128]{2,1,0:T(8,128)S(1)}, u32[]{:S(2)}, u32[]{:S(2)}) collective-permute-start(f32[9,32,128]{2,1,0:T(8,128)S(1)} %collective-permute-done.1.far), channel_id=1, source_target_pairs={{0,1},{1,0},{2,3},{3,2},{4,5},{5,4},{6,7},{7,6},{8,9},{9,8},{10,11... | collective-permute-start | bytes 442376 | tf_op jit(solution)/shard_map/ppermute | solution.py:458
  22.2 10.8 %collective-permute-start.6 = (f32[3,32,128]{2,1,0:T(8,128)S(1)}, f32[3,32,128]{2,1,0:T(8,128)S(1)}, u32[]{:S(2)}, u32[]{:S(2)}) collective-permute-start(f32[3,32,128]{2,1,0:T(8,128)S(1)} %get-tuple-element.41), channel_id=1, source_target_pairs={{1,2},{3,4},{5,6},{7,8},{9,10},{11,12},{13,14},{15,16},{17,18},{19... | collective-permute-start | bytes 147464 | tf_op jit(solution)/shard_map/ppermute | solution.py:424
  26.6 6.5 %collective-permute-start.5 = (f32[4,32,128]{2,1,0:T(8,128)S(1)}, f32[4,32,128]{2,1,0:T(8,128)S(1)}, u32[]{:S(2)}, u32[]{:S(2)}) collective-permute-start(f32[4,32,128]{2,1,0:T(8,128)S(1)} %get-tuple-element.40.own), channel_id=1, source_target_pairs={{0,1},{1,0},{2,3},{3,2},{4,5},{5,4},{6,7},{7,6},{8,9},{9,8},{10,11... | collective-permute-start | bytes 196616 | tf_op jit(solution)/shard_map/ppermute | solution.py:425
  33.0 1.2 %collective-permute-start.7 = (f32[3,32,128]{2,1,0:T(8,128)S(1)}, f32[3,32,128]{2,1,0:T(8,128)S(1)}, u32[]{:S(2)}, u32[]{:S(2)}) collective-permute-start(f32[3,32,128]{2,1,0:T(8,128)S(1)} %collective-permute-done.6.far), channel_id=1, source_target_pairs={{0,1},{1,0},{2,3},{3,2},{4,5},{5,4},{6,7},{7,6},{8,9},{9,8},{10,11... | collective-permute-start | bytes 147464 | tf_op jit(solution)/shard_map/ppermute | solution.py:426
  35.6 10.8 %collective-permute-start.9 = (f32[3,32,128]{2,1,0:T(8,128)S(1)}, f32[3,32,128]{2,1,0:T(8,128)S(1)}, u32[]{:S(2)}, u32[]{:S(2)}) collective-permute-start(f32[3,32,128]{2,1,0:T(8,128)S(1)} %get-tuple-element.44), channel_id=1, source_target_pairs={{1,2},{3,4},{5,6},{7,8},{9,10},{11,12},{13,14},{15,16},{17,18},{19... | collective-permute-start | bytes 147464 | tf_op jit(solution)/shard_map/ppermute | solution.py:424
  39.9 6.5 %collective-permute-start.8 = (f32[4,32,128]{2,1,0:T(8,128)S(1)}, f32[4,32,128]{2,1,0:T(8,128)S(1)}, u32[]{:S(2)}, u32[]{:S(2)}) collective-permute-start(f32[4,32,128]{2,1,0:T(8,128)S(1)} %get-tuple-element.43.own), channel_id=1, source_target_pairs={{0,1},{1,0},{2,3},{3,2},{4,5},{5,4},{6,7},{7,6},{8,9},{9,8},{10,11... | collective-permute-start | bytes 196616 | tf_op jit(solution)/shard_map/ppermute | solution.py:425
  46.4 1.2 %collective-permute-start.10 = (f32[3,32,128]{2,1,0:T(8,128)S(1)}, f32[3,32,128]{2,1,0:T(8,128)S(1)}, u32[]{:S(2)}, u32[]{:S(2)}) collective-permute-start(f32[3,32,128]{2,1,0:T(8,128)S(1)} %collective-permute-done.9.far), channel_id=1, source_target_pairs={{0,1},{1,0},{2,3},{3,2},{4,5},{5,4},{6,7},{7,6},{8,9},{9,8},{10,11... | collective-permute-start | bytes 147464 | tf_op jit(solution)/shard_map/ppermute | solution.py:426
  48.9 10.8 %collective-permute-start.12 = (f32[3,32,128]{2,1,0:T(8,128)S(1)}, f32[3,32,128]{2,1,0:T(8,128)S(1)}, u32[]{:S(2)}, u32[]{:S(2)}) collective-permute-start(f32[3,32,128]{2,1,0:T(8,128)S(1)} %get-tuple-element.47), channel_id=1, source_target_pairs={{1,2},{3,4},{5,6},{7,8},{9,10},{11,12},{13,14},{15,16},{17,18},{19... | collective-permute-start | bytes 147464 | tf_op jit(solution)/shard_map/ppermute | solution.py:424
  53.3 6.5 %collective-permute-start.11 = (f32[4,32,128]{2,1,0:T(8,128)S(1)}, f32[4,32,128]{2,1,0:T(8,128)S(1)}, u32[]{:S(2)}, u32[]{:S(2)}) collective-permute-start(f32[4,32,128]{2,1,0:T(8,128)S(1)} %get-tuple-element.46.own), channel_id=1, source_target_pairs={{0,1},{1,0},{2,3},{3,2},{4,5},{5,4},{6,7},{7,6},{8,9},{9,8},{10,11... | collective-permute-start | bytes 196616 | tf_op jit(solution)/shard_map/ppermute | solution.py:425
  59.8 1.2 %collective-permute-start.13 = (f32[3,32,128]{2,1,0:T(8,128)S(1)}, f32[3,32,128]{2,1,0:T(8,128)S(1)}, u32[]{:S(2)}, u32[]{:S(2)}) collective-permute-start(f32[3,32,128]{2,1,0:T(8,128)S(1)} %collective-permute-done.12.far), channel_id=1, source_target_pairs={{0,1},{1,0},{2,3},{3,2},{4,5},{5,4},{6,7},{7,6},{8,9},{9,8},{10,11... | collective-permute-start | bytes 147464 | tf_op jit(solution)/shard_map/ppermute | solution.py:426
  62.3 10.8 %collective-permute-start.14 = (f32[3,32,128]{2,1,0:T(8,128)S(1)}, f32[3,32,128]{2,1,0:T(8,128)S(1)}, u32[]{:S(2)}, u32[]{:S(2)}) collective-permute-start(f32[3,32,128]{2,1,0:T(8,128)S(1)} %get-tuple-element.48), channel_id=1, source_target_pairs={{1,2},{3,4},{5,6},{7,8},{9,10},{11,12},{13,14},{15,16},{17,18},{19... | collective-permute-start | bytes 147464 | tf_op jit(solution)/shard_map/ppermute | solution.py:475
  66.7 6.5 %collective-permute-start.15 = (f32[4,32,128]{2,1,0:T(8,128)S(1)}, f32[4,32,128]{2,1,0:T(8,128)S(1)}, u32[]{:S(2)}, u32[]{:S(2)}) collective-permute-start(f32[4,32,128]{2,1,0:T(8,128)S(1)} %get-tuple-element.52.own), channel_id=1, source_target_pairs={{0,1},{1,0},{2,3},{3,2},{4,5},{5,4},{6,7},{7,6},{8,9},{9,8},{10,11... | collective-permute-start | bytes 196616 | tf_op jit(solution)/shard_map/ppermute | solution.py:476
  73.1 1.2 %collective-permute-start.16 = (f32[3,32,128]{2,1,0:T(8,128)S(1)}, f32[3,32,128]{2,1,0:T(8,128)S(1)}, u32[]{:S(2)}, u32[]{:S(2)}) collective-permute-start(f32[3,32,128]{2,1,0:T(8,128)S(1)} %collective-permute-done.14.far), channel_id=1, source_target_pairs={{0,1},{1,0},{2,3},{3,2},{4,5},{5,4},{6,7},{7,6},{8,9},{9,8},{10,11... | collective-permute-start | bytes 147464 | tf_op jit(solution)/shard_map/ppermute | solution.py:485
  76.2 1.3 %collective-permute-start.17 = (f32[128,128]{1,0:T(8,128)S(1)}, f32[128,128]{1,0:T(8,128)S(1)}, u32[]{:S(2)}, u32[]{:S(2)}) collective-permute-start(f32[128,128]{1,0:T(8,128)S(1)} %residual.1), channel_id=1, source_target_pairs={{0,1},{1,0},{2,3},{3,2},{4,5},{5,4},{6,7},{7,6},{8,9},{9,8},{10,11... | collective-permute-start | bytes 196616 | tf_op jit(solution)/shard_map/ppermute | solution.py:493
  77.5 12.9 %collective-permute-start.18 = (f32[2,128,128]{2,1,0:T(8,128)S(1)}, f32[2,128,128]{2,1,0:T(8,128)S(1)}, u32[]{:S(2)}, u32[]{:S(2)}) collective-permute-start(f32[2,128,128]{2,1,0:T(8,128)S(1)} %pad_maximum_fusion.own), channel_id=1, source_target_pairs={{2,1},{4,3},{6,5},{8,7},{10,9},{12,11},{14,13},{16,15},{18,17},{20... | collective-permute-start | bytes 393224 | tf_op jit(solution)/shard_map/ppermute | solution.py:495
  90.4 1.5 %collective-permute-start.19 = (f32[2,128,128]{2,1,0:T(8,128)S(1)}, f32[2,128,128]{2,1,0:T(8,128)S(1)}, u32[]{:S(2)}, u32[]{:S(2)}) collective-permute-start(f32[2,128,128]{2,1,0:T(8,128)S(1)} %collective-permute-done.18.far), channel_id=1, source_target_pairs={{0,1},{1,0},{2,3},{3,2},{4,5},{5,4},{6,7},{7,6},{8,9},{9,8},{10,11... | collective-permute-start | bytes 393224 | tf_op jit(solution)/shard_map/ppermute | solution.py:496
where the time goes:
time: 93.3 us; the launch traced here: 93.4 us
  waiting for transfers between devices  49.5 us (53%)
  starting transfers between devices  26.1 us (28%)
  Pallas kernels  17 us (18%)
    ppermute x3, waiting for transfers between devices, exchange(): far = lax.ppermute(sent, AXES, reach)  19.1 us
    pallas_call x10, Pallas kernels, call(): pl.pallas_call(kernel, out_shape=out_shape, in_specs=list(leading) + (spe...  17 us
    ppermute x3, starting transfers between devices, exchange(): far = lax.ppermute(sent, AXES, reach)  13.1 us
    ppermute x1, waiting for transfers between devices, shards(): far = lax.ppermute(both, AXES, downward)  11 us
    ppermute x2, waiting for transfers between devices, shards(): far = lax.ppermute(sent, AXES, reach)  9.87 us
    ppermute x2, starting transfers between devices, shards(): far = lax.ppermute(sent, AXES, reach)  8.7 us
    ppermute x3, waiting for transfers between devices, exchange(): post = lax.ppermute(far, AXES, swap)  3.67 us
    ppermute x3, waiting for transfers between devices, shards(): post = lax.ppermute(far, AXES, swap)  3.58 us
  transfers between devices with their start and end apart: 20, of which 15 were waited for; matrix products, arithmetic and copies ran while one was open for 0% of the time, Pallas kernels for 4%

commit v1 on v0

--- a/solution.py
+++ b/solution.py
@@ -44,8 +44,8 @@
 
 
 def whereabouts(scalars):
-    core = scalars[4]
-    first, last = scalars[0], scalars[2]
+    core = scalars[0]
+    first, last = scalars[1], scalars[3]
     return core, jnp.where(core == 0, first, last - 4), last - first - 4
 
 
@@ -79,14 +79,15 @@
     cut = 128 - 32 * start
 
     def window(face, slab, rows):
-        a, b = oth[face, rows, :], post[slab, rows, :]
+        a = oth[face, rows, :]
+        b = jnp.zeros((8, 128), F32) if post is None else post[slab, rows, :]
         lead = pick(jnp.where(low, a, b), moved)
         tail = pick(jnp.where(low, b, a), moved)
         return jnp.where(lane < cut, lead, tail)
 
     def sides(face, slab, rows):
         mid = window(face, slab, rows)
-        edge = far[slab, rows, :]
+        edge = jnp.zeros((8, 128), F32) if far is None else far[slab, rows, :]
         return jnp.where(low, edge, mid), jnp.where(low, mid, edge)
 
     for t in range(TILES):
@@ -167,10 +168,10 @@
         copies[i].start()
     counting.wait()
     count = []
-    for bound in (0, 1, 2, 4):
+    for bound in (0, 1, 2, 4, 6):
         count.append(jnp.sum((bounds[...] < device - core + bound).astype(jnp.int32)))
-        scalars[len(count) - 1] = count[-1]
-    scalars[4] = core
+        scalars[len(count)] = count[-1]
+    scalars[0] = core
     base = jnp.where(core == 0, count[0], count[1])
     for i in order:
         copies[i].wait()
@@ -184,8 +185,8 @@
 
 
 def window_of(scalars):
-    core, extra = scalars[4], scalars[2] - scalars[0] - 4
-    held = jnp.where(core == 0, scalars[1] - scalars[0], scalars[2] - scalars[1])
+    core, extra = scalars[0], scalars[3] - scalars[1] - 4
+    held = jnp.where(core == 0, scalars[2] - scalars[1], scalars[3] - scalars[2])
     lane = lanes()
     low = core == 0
     index = (lane + jnp.where(low, 0, 32 * held)) % 128
@@ -205,7 +206,7 @@
 
 def put_sent(scalars, faces, sent):
     for t in range(TILES):
-        sent[0, part(t), :] = faces[scalars[4], part(t), :]
+        sent[0, part(t), :] = faces[scalars[0], part(t), :]
         sent[1, part(t), :] = faces[2, part(t), :]
         sent[2, part(t), :] = faces[3, part(t), :]
 
@@ -223,7 +224,7 @@
         lax.fori_loop(0, SPAN, rows, 0, unroll=8)
 
 
-def first_kernel(layers, scalars, fields, own, oth, far, post, vo, fo, do, go, faces, sent, ghost, pv, pk, pa):
+def first_kernel(layers, scalars, fields, own, oth, far, post, vo, fo, do, go, edge, faces, sent, ghost, pv, pk, pa):
     v, f, k, c, a = (fields.at[i] for i in range(5))
     where = whereabouts(scalars)
     base = where[1]
@@ -232,6 +233,12 @@
     for number in range(3):
         group, outer = pl.ds(4 * number, 4), pl.ds(3 * number, 3)
         ghosts(where, own.at[group], oth.at[group], far.at[outer], post.at[outer], ghost.at[number])
+    for face in range(4):
+        for t in range(TILES):
+            rows = part(t)
+            heat, heat2 = own[4 + face, rows, :], ghost[1, face, rows, :]
+            opening, opening2 = own[8 + face, rows, :], ghost[2, face, rows, :]
+            edge[face, rows, :] = 2.0 * opening * heat * opening2 * heat2 * inverted(heat + heat2)
     for t in range(TILES):
         rows = part(t)
         for face, gone, row in ((0, iz == 0, 0), (1, iz == layers - 1, 31)):
@@ -288,7 +295,8 @@
     return value, total
 
 
-def sweep_kernel(shade_now, scalars, v, f, g, own, oth, far, post, vo, faces, sent, ghost, padded):
+def sweep_kernel(shade_now, scalars, v, f, g, own, oth, far, post, vo, faces, *rest):
+    *sent, ghost, padded = rest
     where = whereabouts(scalars)
     base = where[1]
     ghosts(where, own, oth, far, post, ghost)
@@ -303,12 +311,14 @@
 
     lax.fori_loop(0, SPAN, layer, 0, unroll=8)
     put_faces(base, vo, faces)
-    put_sent(scalars, faces, sent)
-
-
-def residual_kernel(scalars, v, f, g, d, own, oth, far, post, blocks, ghost, padded, pair):
+    if sent:
+        put_sent(scalars, faces, sent[0])
+
+
+def residual_kernel(scalars, v, f, g, d, edge, own, oth, blocks, cross, ghost, padded, pair):
     where = whereabouts(scalars)
-    ghosts(where, own, oth, far, post, ghost)
+    core = where[0]
+    ghosts(where, own, oth, None, None, ghost)
     pad(where[1], v, ghost, padded, zero)
     lane = lanes()
     index = 2 * (lane % 64)
@@ -336,10 +346,26 @@
 
     lax.fori_loop(0, 8, layer, 0, unroll=2)
 
+    def pooled(face):
+        for t in range(TILES):
+            product = edge[face, part(t), :] * own[face, part(t), :]
+            pair[0, part(t), :] = product + turned(product, 127)
+        result = []
+        for t in range(2):
+            both = pair[0, pl.ds(16 * t, 8, stride=2), :] + pair[0, pl.ds(16 * t + 1, 8, stride=2), :]
+            result.append(pick(both, index) * 0.125)
+        return result
+
+    for t, tile in enumerate(pooled(core)):
+        cross[part(t), :] = tile
+    for t, (along_y, along_x) in enumerate(zip(pooled(2), pooled(3))):
+        cross[part(2 + t), :] = jnp.where(lane < 64, along_y, along_x)
+    blocks[128:160, :] = cross[...]
+
 
 def level_kernel(scalars, v, level, stack):
-    core = scalars[4]
-    held = jnp.where(core == 0, scalars[1] - scalars[0], scalars[2] - scalars[1])
+    core = scalars[0]
+    held = jnp.where(core == 0, scalars[2] - scalars[1], scalars[3] - scalars[2])
     for j in range(8):
         stack[:, pl.ds(128 * j, 128)] = v[pl.ds(128 * j, 128), :].T
     for s in range(SLOTS):
@@ -350,15 +376,26 @@
             level[s, part(t), :] = jnp.where(filled, stack[rows, :], 0.0)
 
 
-def coarse_kernel(scalars, own, far, post, grid, table, joined):
-    core = scalars[4]
-    first, middle, last, next_last = scalars[0], scalars[1], scalars[2], scalars[3]
-    mine = jnp.where(core == 0, first, middle)
-    mine_end = jnp.where(core == 0, middle, last)
+def coarse_kernel(scalars, own, far, post, side, side_post, grid, table, crossing, joined):
+    core = scalars[0]
+    starts = [scalars[i] for i in (1, 3, 4, 5)]
+    mine = jnp.where(core == 0, scalars[1], scalars[2])
+    mine_end = jnp.where(core == 0, scalars[2], scalars[3])
     leader = lax.div(mine + 7, 8) * 8
     held = leader < mine_end
     low = core == 0
     lane = lanes()
+
+    def child(patch):
+        chip = (patch >= starts[1]).astype(jnp.int32) + (patch >= starts[2]).astype(jnp.int32)
+        begin = jnp.where(chip == 0, starts[0], jnp.where(chip == 1, starts[1], starts[2]))
+        end = jnp.where(chip == 0, starts[1], jnp.where(chip == 1, starts[2], starts[3]))
+        return chip, patch - begin, end - begin
+
+    def block(chip, j, count):
+        entry = jnp.where(j < 4, j, j - count + 8)
+        entry = jnp.clip(8 * chip + entry, 0, 19)
+        return lax.div(entry, 4), lax.rem(entry, 4)
 
     @pl.when(held)
     def _():
@@ -369,29 +406,62 @@
             table[2, rows, :] = jnp.where(low, post[0, rows, :], far[0, rows, :])
             table[3, rows, :] = jnp.where(low, post[1, rows, :], far[1, rows, :])
             table[4, rows, :] = jnp.where(low, far[1, rows, :], post[1, rows, :])
-
-        def source(patch):
-            here = patch - first
-            there = patch - last
-            extra, extra2 = last - first - 4, next_last - last - 4
-            entry = jnp.where(here < 4, here, here - extra + 4)
-            entry2 = 8 + jnp.where(there < 4, there, there - extra2 + 4)
-            entry3 = 16 + patch - next_last
-            found = jnp.where(patch < last, entry, jnp.where(patch < next_last, entry2, entry3))
-            found = jnp.clip(found, 0, 19)
-            return lax.div(found, 4), lax.rem(found, 4)
+        for t in range(4):
+            rows, last = part(t), part(16 + t)
+            crossing[0, rows, :] = jnp.where(low, side[rows, :], side_post[rows, :])
+            crossing[1, rows, :] = jnp.where(low, own[1, last, :], own[0, last, :])
+            crossing[2, rows, :] = jnp.where(low, post[1, last, :], far[1, last, :])
+            crossing[3, rows, :] = jnp.where(low, post[0, last, :], far[0, last, :])
+            crossing[4, rows, :] = jnp.where(low, far[1, last, :], post[1, last, :])
+            crossing[5, rows, :] = jnp.where(low, side_post[rows, :], side[rows, :])
+
+        def added(entry, rows, index, valid):
+            tile = pick(crossing[jnp.clip(entry, 0, 5), rows, :], jnp.clip(index, 0, 127))
+            return jnp.where(valid, tile, 0.0)
 
         for iy in range(2):
             for iz in range(2):
-                left, left_slot = source(leader + 2 * iy + 4 * iz)
-                right, right_slot = source(leader + 1 + 2 * iy + 4 * iz)
+                left = child(leader + 2 * iy + 4 * iz)
+                right = child(leader + 1 + 2 * iy + 4 * iz)
+                left_block, left_slot = block(*left)
+                right_block, right_slot = block(*right)
                 for y in range(16):
                     for t in range(2):
                         rows = pl.ds(16 * (y // 2) + 8 * t, 8)
                         index = 64 * (y % 2) + lane % 16
-                        a = pick(table[left, rows, :], index + 16 * left_slot)
-                        b = pick(table[right, rows, :], index + 16 * right_slot)
+                        a = pick(table[left_block, rows, :], index + 16 * left_slot)
+                        b = pick(table[right_block, rows, :], index + 16 * right_slot)
                         joined[pl.ds(SPAN * (16 * iy + y) + 16 * iz + 8 * t, 8), :] = jnp.where(lane < 16, a, b)
+
+                def pair_of(below, shift, rows):
+                    tiles = []
+                    for chip, j, count in (left, right):
+                        place = j if below else j - count + 4 - shift
+                        valid = (place < 4 - shift) if below else (place >= 0)
+                        entry = chip if below else 3 + chip
+                        slot = place + shift if below else place
+                        tiles.append(added(entry, rows, 16 * slot + lane % 16, valid))
+                    return jnp.where(lane < 16, tiles[0], tiles[1])
+
+                first_row = SPAN * 16 * iy + 16 * iz
+                for t in range(2):
+                    at = pl.ds(first_row + 8 * SPAN * t, 8, stride=SPAN)
+                    joined[at, :] = joined[at, :] + pair_of(True, 0, part(t))
+                    at = pl.ds(first_row + 8 * SPAN * t + 15, 8, stride=SPAN)
+                    joined[at, :] = joined[at, :] + pair_of(False, 0, part(t))
+                    at = pl.ds(first_row + (0 if iy else 15 * SPAN) + 8 * t, 8)
+                    joined[at, :] = joined[at, :] + pair_of(iy == 1, 2, part(2 + t))
+
+                @pl.when(left[0] != right[0])
+                def _():
+                    for y in range(16):
+                        for t in range(2):
+                            at = pl.ds(first_row + SPAN * y + 8 * t, 8)
+                            from_right = added(3 + left[0], part(2 + t), 0 * lane + 64 + y, True)
+                            from_left = added(right[0], part(2 + t), 0 * lane + 112 + y, True)
+                            side_tile = jnp.where(lane == 15, from_right, jnp.where(lane == 16, from_left, 0.0))
+                            joined[at, :] = joined[at, :] + side_tile
+
         for j in range(8):
             turn = joined[pl.ds(128 * j, 128), :].T
             grid[0, :, pl.ds(128 * j, 128)] = turn[0:SPAN, :]
@@ -433,7 +503,7 @@
     three = jax.ShapeDtypeStruct((3, SPAN, 128), F32)
     scalars, own, faces = call(
         collect_kernel,
-        [pltpu.SMEM((5,), jnp.int32), pltpu.VMEM(five.shape, F32), pltpu.VMEM(twelve.shape, F32)],
+        [pltpu.SMEM((6,), jnp.int32), pltpu.VMEM(five.shape, F32), pltpu.VMEM(twelve.shape, F32)],
         [holder.reshape(patches // 128, 128), *fields],
         specs=[HBM] * 6,
         leading=[],
@@ -457,23 +527,33 @@
     far, window = lax.optimization_barrier((far, window))
     post = lax.ppermute(far, AXES, swap)
     coefficients = jax.ShapeDtypeStruct((6, LAYER, 128), F32)
-    wv, wf, wd, wg, faces, sent = call(
+    wv, wf, wd, wg, edge, faces, *sent = call(
         functools.partial(first_kernel, patches // 4),
-        [FIELD, FIELD, FIELD, coefficients, FACES, three],
+        [FIELD, FIELD, FIELD, coefficients, FACES, FACES, three],
         [scalars, window, faces, oth, far, post],
         scratch=[pltpu.VMEM((3, 4, SPAN, 128), F32)] + [PADDED] * 3,
         name="first",
     )
-    for shade in (1, 0, 1):
-        wv, faces, sent = call(
+    for shade, more in ((1, [three]), (0, [three]), (1, [])):
+        wv, faces, *sent = call(
             functools.partial(sweep_kernel, shade),
-            [FIELD, FACES, three],
-            [scalars, wv, wf, wg, *exchange(faces, sent)],
+            [FIELD, FACES] + more,
+            [scalars, wv, wf, wg, *exchange(faces, *sent)],
             scratch=[GHOSTS, PADDED],
             name="sweep",
         )
-    far = lax.ppermute(sent, AXES, reach)
-    oth = lax.ppermute(faces, AXES, swap)
+    blocks, cross = call(
+        residual_kernel,
+        [jax.ShapeDtypeStruct((160, 128), F32), jax.ShapeDtypeStruct((SPAN, 128), F32)],
+        [scalars, wv, wf, wg, wd, edge, faces, lax.ppermute(faces, AXES, swap)],
+        scratch=[GHOSTS, PADDED, pltpu.VMEM((2, SPAN, 128), F32)],
+        name="residual",
+    )
+    beside = [(i, i - 5) for i in range(6, devices, 2)] + [(i, i + 1) for i in range(1, devices - 1, 2)]
+    side = lax.ppermute(cross, AXES, beside)
+    both = jnp.stack([blocks, lax.ppermute(blocks, AXES, swap)], 0)
+    downward = [(i, i - 1) for i in range(2, devices, 2)] + [(i, i - 5) for i in range(5, devices, 2)]
+    far = lax.ppermute(both, AXES, downward)
     level = call(
         level_kernel,
         jax.ShapeDtypeStruct((SLOTS, SPAN, LAYER), F32),
@@ -481,24 +561,14 @@
         scratch=[pltpu.VMEM((128, LAYER), F32)],
         name="level",
     )
-    far, level = lax.optimization_barrier((far, level))
+    far, side, level = lax.optimization_barrier((far, side, level))
     post = lax.ppermute(far, AXES, swap)
-    blocks = call(
-        residual_kernel,
-        jax.ShapeDtypeStruct((128, 128), F32),
-        [scalars, wv, wf, wg, wd, faces, oth, far, post],
-        scratch=[GHOSTS, PADDED, pltpu.VMEM((2, SPAN, 128), F32)],
-        name="residual",
-    )
-    both = jnp.stack([blocks, lax.ppermute(blocks, AXES, swap)], 0)
-    downward = [(i, i - 1) for i in range(2, devices, 2)] + [(i, i - 5) for i in range(5, devices, 2)]
-    far = lax.ppermute(both, AXES, downward)
-    post = lax.ppermute(far, AXES, swap)
+    side_post = lax.ppermute(side, AXES, swap)
     grid = call(
         coarse_kernel,
         jax.ShapeDtypeStruct((1, SPAN, LAYER), F32),
-        [scalars, both, far, post],
-        scratch=[pltpu.VMEM((5, 128, 128), F32), pltpu.VMEM((LAYER, 128), F32)],
+        [scalars, both, far, post, side, side_post],
+        scratch=[pltpu.VMEM((5, 128, 128), F32), pltpu.VMEM((6, SPAN, 128), F32), pltpu.VMEM((LAYER, 128), F32)],
         name="coarse",
     )
     return level, grid

time: 93.3 us -> 87.1 us (0.934)
  the two profiles are of different devices: /device:TPU:127 before, /device:TPU:129 now
where the time goes in v1:
time: 87.1 us; the launch traced here: 85.9 us
  starting transfers between devices  59.6 us (68%)
  Pallas kernels  16.2 us (19%)
  waiting for transfers between devices  9.34 us (11%)
    pallas_call x10, Pallas kernels, call(): pl.pallas_call(kernel, out_shape=out_shape, in_specs=list(leading) + (spe...  16.2 us
    ppermute x3, starting transfers between devices, exchange(): oth = lax.ppermute(faces, AXES, swap)  15.5 us
    ppermute x3, starting transfers between devices, exchange(): post = lax.ppermute(far, AXES, swap)  12.3 us
    ppermute x2, starting transfers between devices, shards(): post = lax.ppermute(far, AXES, swap)  11.6 us
    ppermute x3, starting transfers between devices, exchange(): far = lax.ppermute(sent, AXES, reach)  5.76 us
    ppermute x1, starting transfers between devices, shards(): oth = lax.ppermute(faces, AXES, swap)  3.72 us
    ppermute x1, starting transfers between devices, shards(): side = lax.ppermute(cross, AXES, beside)  3.64 us
    ppermute x1, starting transfers between devices, shards(): far = lax.ppermute(sent, AXES, reach)  3.13 us
  transfers between devices with their start and end apart: 20, of which 9 were waited for; matrix products, arithmetic and copies ran while one was open for 0% of the time, Pallas kernels for 4%

profile of v1, /device:TPU:129, one launch (start us, length us, event | category | flops | bytes accessed | tf_op | source)
XLA Modules:
  0.0 85.9 jit_solution(6093557054817267339)
XLA Ops:
  0.6 2.7 %collect.1 = (s32[6]{0:T(128)S(4)}, f32[5,1024,128]{2,1,0:T(8,128)S(1)}, f32[12,32,128]{2,1,0:T(8,128)S(1)}) custom-call(s32[6,128]{1,0:T(8,128)} %bitcast.15, f32[128,1024]{1,0:T(8,128)} %bitcast.9, f32[128,1024]{1,0:T(8,128)} %bitcast.10, f32[128,1024]{1,0:T(8,128)} %bitcast.11, f32[128,1024]{1,0:T(8,128)} %bitcast.12, s32[128,1024]{1,0:T(8,128)} %bitcast.13), custom_call_target="tpu_custom_call" | custom-call | tf_op jit(solution)/shard_map/collect/pallas_call | solution.py:475
  3.4 0.8 collective-permute-start
  4.1 1.1 %collective-permute-done.oth = f32[12,32,128]{2,1,0:T(8,128)S(1)} collective-permute-done((f32[12,32,128]{2,1,0:T(8,128)S(1)}, f32[12,32,128]{2,1,0:T(8,128)S(1)}, u32[]{:S(2)}, u32[]{:S(2)}) %collective-permute-start) | collective-permute-done | bytes 196640 | tf_op jit(solution)/shard_map/ppermute | solution.py:520
  5.2 0.2 face_window.1
  5.4 0.5 collective-permute-start.2
  5.8 3.1 %collective-permute-start.1 = (f32[9,32,128]{2,1,0:T(8,128)S(1)}, f32[9,32,128]{2,1,0:T(8,128)S(1)}, u32[]{:S(2)}, u32[]{:S(2)}) collective-permute-start(f32[9,32,128]{2,1,0:T(8,128)S(1)} %get-tuple-element.35), channel_id=1, source_target_pairs={{1,2},{3,4},{5,6},{7,8},{9,10},{11,12},{13,14},{15,16},{17,18},{19... | collective-permute-start | bytes 442376 | tf_op jit(solution)/shard_map/ppermute | solution.py:524
  9.0 3.7 %collective-permute-start.3 = (f32[12,32,128]{2,1,0:T(8,128)S(1)}, f32[12,32,128]{2,1,0:T(8,128)S(1)}, u32[]{:S(2)}, u32[]{:S(2)}) collective-permute-start(f32[12,32,128]{2,1,0:T(8,128)S(1)} %get-tuple-element.38.own), channel_id=1, source_target_pairs={{0,1},{1,0},{2,3},{3,2},{4,5},{5,4},{6,7},{7,6},{8,9},{9,8},{10,11... | collective-permute-start | bytes 589832 | tf_op jit(solution)/shard_map/ppermute | solution.py:525
  12.7 0.0 collective-permute-done.2.oth
  12.7 2.8 %window.1.fields = f32[5,1024,128]{2,1,0:T(8,128)S(1)} custom-call(s32[6]{0:T(128)S(4)} %get-tuple-element.31.scalars, f32[5,1024,128]{2,1,0:T(8,128)S(1)} %get-tuple-element.36.own, f32[5,1024,128]{2,1,0:T(8,128)S(1)} %collective-permute-done.2.oth), custom_call_target="tpu_custom_call" | custom-call | tf_op jit(solution)/shard_map/window/pallas_call | solution.py:475
  15.5 0.0 collective-permute-done.1.far
  15.5 2.3 %collective-permute-start.4 = (f32[9,32,128]{2,1,0:T(8,128)S(1)}, f32[9,32,128]{2,1,0:T(8,128)S(1)}, u32[]{:S(2)}, u32[]{:S(2)}) collective-permute-start(f32[9,32,128]{2,1,0:T(8,128)S(1)} %collective-permute-done.1.far), channel_id=1, source_target_pairs={{0,1},{1,0},{2,3},{3,2},{4,5},{5,4},{6,7},{7,6},{8,9},{9,8},{10,11... | collective-permute-start | bytes 442376 | tf_op jit(solution)/shard_map/ppermute | solution.py:528
  17.9 0.0 collective-permute-done.3.oth
  17.9 1.0 %collective-permute-done.4.post = f32[9,32,128]{2,1,0:T(8,128)S(1)} collective-permute-done((f32[9,32,128]{2,1,0:T(8,128)S(1)}, f32[9,32,128]{2,1,0:T(8,128)S(1)}, u32[]{:S(2)}, u32[]{:S(2)}) %collective-permute-start.4) | collective-permute-done | bytes 147488 | tf_op jit(solution)/shard_map/ppermute | solution.py:528
  18.9 3.0 %first.1 = (f32[1024,128]{1,0:T(8,128)S(1)}, f32[1024,128]{1,0:T(8,128)S(1)}, f32[1024,128]{1,0:T(8,128)S(1)}, f32[6,1024,128]{2,1,0:T(8,128)S(1)}, f32[4,32,128...) custom-call(s32[6]{0:T(128)S(4)} %get-tuple-element.31.scalars, ...), custom_call_target="tpu_custom_call" | custom-call | tf_op jit(solution)/shard_map/first/pallas_call | solution.py:475
  21.9 1.9 %collective-permute-start.6 = (f32[3,32,128]{2,1,0:T(8,128)S(1)}, f32[3,32,128]{2,1,0:T(8,128)S(1)}, u32[]{:S(2)}, u32[]{:S(2)}) collective-permute-start(f32[3,32,128]{2,1,0:T(8,128)S(1)} %get-tuple-element.44), channel_id=1, source_target_pairs={{1,2},{3,4},{5,6},{7,8},{9,10},{11,12},{13,14},{15,16},{17,18},{19... | collective-permute-start | bytes 147464 | tf_op jit(solution)/shard_map/ppermute | solution.py:494
  23.9 5.2 %collective-permute-start.5 = (f32[4,32,128]{2,1,0:T(8,128)S(1)}, f32[4,32,128]{2,1,0:T(8,128)S(1)}, u32[]{:S(2)}, u32[]{:S(2)}) collective-permute-start(f32[4,32,128]{2,1,0:T(8,128)S(1)} %get-tuple-element.43.own), channel_id=1, source_target_pairs={{0,1},{1,0},{2,3},{3,2},{4,5},{5,4},{6,7},{7,6},{8,9},{9,8},{10,11... | collective-permute-start | bytes 196616 | tf_op jit(solution)/shard_map/ppermute | solution.py:495
  29.0 0.0 collective-permute-done.6.far
  29.0 4.1 %collective-permute-start.7 = (f32[3,32,128]{2,1,0:T(8,128)S(1)}, f32[3,32,128]{2,1,0:T(8,128)S(1)}, u32[]{:S(2)}, u32[]{:S(2)}) collective-permute-start(f32[3,32,128]{2,1,0:T(8,128)S(1)} %collective-permute-done.6.far), channel_id=1, source_target_pairs={{0,1},{1,0},{2,3},{3,2},{4,5},{5,4},{6,7},{7,6},{8,9},{9,8},{10,11... | collective-permute-start | bytes 147464 | tf_op jit(solution)/shard_map/ppermute | solution.py:496
  33.1 0.0 collective-permute-done.5.oth
  33.1 0.9 %collective-permute-done.7.post = f32[3,32,128]{2,1,0:T(8,128)S(1)} collective-permute-done((f32[3,32,128]{2,1,0:T(8,128)S(1)}, f32[3,32,128]{2,1,0:T(8,128)S(1)}, u32[]{:S(2)}, u32[]{:S(2)}) %collective-permute-start.7) | collective-permute-done | bytes 49184 | tf_op jit(solution)/shard_map/ppermute | solution.py:496
  34.0 1.3 %sweep.3 = (f32[1024,128]{1,0:T(8,128)S(1)}, f32[4,32,128]{2,1,0:T(8,128)S(1)}, f32[3,32,128]{2,1,0:T(8,128)S(1)}) custom-call(s32[6]{0:T(128)S(4)} %get-tuple-element.31.scalars, f32[1024,128]{1,0:T(8,128)S(1)} %get-tuple-element.40.v, f32[1024,128]{1,0:T(8,128)S(1)} %get-tuple-element.41.f, f32[6,1024,128]{2,1,0:T(8,128)S(1)} %get-tuple-element.42.g, ...), custom_call_target="tpu_custom_call" | custom-call | tf_op jit(solution)/shard_map/sweep/pallas_call | solution.py:475
  35.3 1.9 %collective-permute-start.9 = (f32[3,32,128]{2,1,0:T(8,128)S(1)}, f32[3,32,128]{2,1,0:T(8,128)S(1)}, u32[]{:S(2)}, u32[]{:S(2)}) collective-permute-start(f32[3,32,128]{2,1,0:T(8,128)S(1)} %get-tuple-element.47), channel_id=1, source_target_pairs={{1,2},{3,4},{5,6},{7,8},{9,10},{11,12},{13,14},{15,16},{17,18},{19... | collective-permute-start | bytes 147464 | tf_op jit(solution)/shard_map/ppermute | solution.py:494
  37.2 5.2 %collective-permute-start.8 = (f32[4,32,128]{2,1,0:T(8,128)S(1)}, f32[4,32,128]{2,1,0:T(8,128)S(1)}, u32[]{:S(2)}, u32[]{:S(2)}) collective-permute-start(f32[4,32,128]{2,1,0:T(8,128)S(1)} %get-tuple-element.46.own), channel_id=1, source_target_pairs={{0,1},{1,0},{2,3},{3,2},{4,5},{5,4},{6,7},{7,6},{8,9},{9,8},{10,11... | collective-permute-start | bytes 196616 | tf_op jit(solution)/shard_map/ppermute | solution.py:495
  42.4 0.0 collective-permute-done.9.far
  42.4 4.1 %collective-permute-start.10 = (f32[3,32,128]{2,1,0:T(8,128)S(1)}, f32[3,32,128]{2,1,0:T(8,128)S(1)}, u32[]{:S(2)}, u32[]{:S(2)}) collective-permute-start(f32[3,32,128]{2,1,0:T(8,128)S(1)} %collective-permute-done.9.far), channel_id=1, source_target_pairs={{0,1},{1,0},{2,3},{3,2},{4,5},{5,4},{6,7},{7,6},{8,9},{9,8},{10,11... | collective-permute-start | bytes 147464 | tf_op jit(solution)/shard_map/ppermute | solution.py:496
  46.5 0.9 %collective-permute-done.10.post = f32[3,32,128]{2,1,0:T(8,128)S(1)} collective-permute-done((f32[3,32,128]{2,1,0:T(8,128)S(1)}, f32[3,32,128]{2,1,0:T(8,128)S(1)}, u32[]{:S(2)}, u32[]{:S(2)}) %collective-permute-start.10) | collective-permute-done | bytes 49184 | tf_op jit(solution)/shard_map/ppermute | solution.py:496
  47.4 1.3 %sweep.4 = (f32[1024,128]{1,0:T(8,128)S(1)}, f32[4,32,128]{2,1,0:T(8,128)S(1)}, f32[3,32,128]{2,1,0:T(8,128)S(1)}) custom-call(s32[6]{0:T(128)S(4)} %get-tuple-element.31.scalars, f32[1024,128]{1,0:T(8,128)S(1)} %get-tuple-element.45.v, f32[1024,128]{1,0:T(8,128)S(1)} %get-tuple-element.41.f, f32[6,1024,128]{2,1,0:T(8,128)S(1)} %get-tuple-element.42.g, ...), custom_call_target="tpu_custom_call" | custom-call | tf_op jit(solution)/shard_map/sweep/pallas_call | solution.py:475
  48.7 1.9 %collective-permute-start.12 = (f32[3,32,128]{2,1,0:T(8,128)S(1)}, f32[3,32,128]{2,1,0:T(8,128)S(1)}, u32[]{:S(2)}, u32[]{:S(2)}) collective-permute-start(f32[3,32,128]{2,1,0:T(8,128)S(1)} %get-tuple-element.50), channel_id=1, source_target_pairs={{1,2},{3,4},{5,6},{7,8},{9,10},{11,12},{13,14},{15,16},{17,18},{19... | collective-permute-start | bytes 147464 | tf_op jit(solution)/shard_map/ppermute | solution.py:494
  50.6 5.2 %collective-permute-start.11 = (f32[4,32,128]{2,1,0:T(8,128)S(1)}, f32[4,32,128]{2,1,0:T(8,128)S(1)}, u32[]{:S(2)}, u32[]{:S(2)}) collective-permute-start(f32[4,32,128]{2,1,0:T(8,128)S(1)} %get-tuple-element.49.own), channel_id=1, source_target_pairs={{0,1},{1,0},{2,3},{3,2},{4,5},{5,4},{6,7},{7,6},{8,9},{9,8},{10,11... | collective-permute-start | bytes 196616 | tf_op jit(solution)/shard_map/ppermute | solution.py:495
  55.8 0.0 collective-permute-done.12.far
  55.8 4.1 %collective-permute-start.13 = (f32[3,32,128]{2,1,0:T(8,128)S(1)}, f32[3,32,128]{2,1,0:T(8,128)S(1)}, u32[]{:S(2)}, u32[]{:S(2)}) collective-permute-start(f32[3,32,128]{2,1,0:T(8,128)S(1)} %collective-permute-done.12.far), channel_id=1, source_target_pairs={{0,1},{1,0},{2,3},{3,2},{4,5},{5,4},{6,7},{7,6},{8,9},{9,8},{10,11... | collective-permute-start | bytes 147464 | tf_op jit(solution)/shard_map/ppermute | solution.py:496
  59.9 0.9 %collective-permute-done.13.post = f32[3,32,128]{2,1,0:T(8,128)S(1)} collective-permute-done((f32[3,32,128]{2,1,0:T(8,128)S(1)}, f32[3,32,128]{2,1,0:T(8,128)S(1)}, u32[]{:S(2)}, u32[]{:S(2)}) %collective-permute-start.13) | collective-permute-done | bytes 49184 | tf_op jit(solution)/shard_map/ppermute | solution.py:496
  60.7 1.3 %sweep.5 = (f32[1024,128]{1,0:T(8,128)S(1)}, f32[4,32,128]{2,1,0:T(8,128)S(1)}) custom-call(s32[6]{0:T(128)S(4)} %get-tuple-element.31.scalars, f32[1024,128]{1,0:T(8,128)S(1)} %get-tuple-element.48.v, f32[1024,128]{1,0:T(8,128)S(1)} %get-tuple-element.41.f, f32[6,1024,128]{2,1,0:T(8,128)S(1)} %get-tuple-element.42.g, ...), custom_call_target="tpu_custom_call" | custom-call | tf_op jit(solution)/shard_map/sweep/pallas_call | solution.py:475
  62.0 0.4 collective-permute-start.14
  62.5 0.9 %collective-permute-done.14.oth = f32[4,32,128]{2,1,0:T(8,128)S(1)} collective-permute-done((f32[4,32,128]{2,1,0:T(8,128)S(1)}, f32[4,32,128]{2,1,0:T(8,128)S(1)}, u32[]{:S(2)}, u32[]{:S(2)}) %collective-permute-start.14) | collective-permute-done | bytes 65568 | tf_op jit(solution)/shard_map/ppermute | solution.py:548
  63.4 1.9 %residual.1 = (f32[160,128]{1,0:T(8,128)S(1)}, f32[32,128]{1,0:T(8,128)S(1)}) custom-call(s32[6]{0:T(128)S(4)} %get-tuple-element.31.scalars, f32[1024,128]{1,0:T(8,128)S(1)} %get-tuple-element.51.v, f32[1024,128]{1,0:T(8,128)S(1)} %get-tuple-element.41.f, f32[6,1024,128]{2,1,0:T(8,128)S(1)} %get-tuple-element.42.g, f32[1024,128]{1,0:T(8,128)S(1)} %get-tuple-element.52.d, ...), custom_call_target="tpu_custom_call" | custom-call | tf_op jit(solution)/shard_map/residual/pallas_call | solution.py:475
  65.3 0.4 collective-permute-start.15
  65.7 0.9 %collective-permute-done.15 = f32[160,128]{1,0:T(8,128)S(1)} collective-permute-done((f32[160,128]{1,0:T(8,128)S(1)}, f32[160,128]{1,0:T(8,128)S(1)}, u32[]{:S(2)}, u32[]{:S(2)}) %collective-permute-start.15) | collective-permute-done | bytes 81952 | tf_op jit(solution)/shard_map/ppermute | solution.py:554
  66.6 1.9 %collective-permute-start.16 = (f32[2,160,128]{2,1,0:T(8,128)S(1)}, f32[2,160,128]{2,1,0:T(8,128)S(1)}, u32[]{:S(2)}, u32[]{:S(2)}) collective-permute-start(f32[2,160,128]{2,1,0:T(8,128)S(1)} %pad_maximum_fusion.own), channel_id=1, source_target_pairs={{2,1},{4,3},{6,5},{8,7},{10,9},{12,11},{14,13},{16,15},{18,17},{20... | collective-permute-start | bytes 491528 | tf_op jit(solution)/shard_map/ppermute | solution.py:556
  68.5 3.6 %collective-permute-start.17 = (f32[32,128]{1,0:T(8,128)S(1)}, f32[32,128]{1,0:T(8,128)S(1)}, u32[]{:S(2)}, u32[]{:S(2)}) collective-permute-start(f32[32,128]{1,0:T(8,128)S(1)} %get-tuple-element.56), channel_id=1, source_target_pairs={{6,1},{8,3},{10,5},{12,7},{14,9},{16,11},{18,13},{20,15},{22,17},{... | collective-permute-start | bytes 49160 | tf_op jit(solution)/shard_map/ppermute | solution.py:553
  72.2 1.0 %level.1 = f32[4,32,1024]{2,1,0:T(8,128)} custom-call(s32[6]{0:T(128)S(4)} %get-tuple-element.31.scalars, f32[1024,128]{1,0:T(8,128)S(1)} %get-tuple-element.51.v), custom_call_target="tpu_custom_call" | custom-call | tf_op jit(solution)/shard_map/level/pallas_call | solution.py:475
  73.2 1.6 %collective-permute-done.17.side = f32[32,128]{1,0:T(8,128)S(1)} collective-permute-done((f32[32,128]{1,0:T(8,128)S(1)}, f32[32,128]{1,0:T(8,128)S(1)}, u32[]{:S(2)}, u32[]{:S(2)}) %collective-permute-start.17) | collective-permute-done | bytes 16416 | tf_op jit(solution)/shard_map/ppermute | solution.py:553
  74.8 0.0 collective-permute-done.16.far
  74.8 9.3 %collective-permute-start.18 = (f32[2,160,128]{2,1,0:T(8,128)S(1)}, f32[2,160,128]{2,1,0:T(8,128)S(1)}, u32[]{:S(2)}, u32[]{:S(2)}) collective-permute-start(f32[2,160,128]{2,1,0:T(8,128)S(1)} %collective-permute-done.16.far), channel_id=1, source_target_pairs={{0,1},{1,0},{2,3},{3,2},{4,5},{5,4},{6,7},{7,6},{8,9},{9,8},{10,11... | collective-permute-start | bytes 491528 | tf_op jit(solution)/shard_map/ppermute | solution.py:565
  84.1 0.0 collective-permute-start.19
  84.1 1.2 %collective-permute-done.19.side_post = f32[32,128]{1,0:T(8,128)S(1)} collective-permute-done((f32[32,128]{1,0:T(8,128)S(1)}, f32[32,128]{1,0:T(8,128)S(1)}, u32[]{:S(2)}, u32[]{:S(2)}) %collective-permute-start.19) | collective-permute-done | bytes 16416 | tf_op jit(solution)/shard_map/ppermute | solution.py:566
  85.3 0.0 collective-permute-done.18.post
  85.3 0.7 coarse.1
  (3 shorter events, 0.0 us)
Async XLA Ops:
  3.4 1.8 %collective-permute-start = (f32[12,32,128]{2,1,0:T(8,128)S(1)}, f32[12,32,128]{2,1,0:T(8,128)S(1)}, u32[]{:S(2)}, u32[]{:S(2)}) collective-permute-start(f32[12,32,128]{2,1,0:T(8,128)S(1)} %get-tuple-element.32.own), channel_id=1, source_target_pairs={{0,1},{1,0},{2,3},{3,2},{4,5},{5,4},{6,7},{7,6},{8,9},{9,8},{10,11... | collective-permute-start | bytes 589832 | tf_op jit(solution)/shard_map/ppermute | solution.py:520
  5.4 7.3 %collective-permute-start.2 = (f32[5,1024,128]{2,1,0:T(8,128)S(1)}, f32[5,1024,128]{2,1,0:T(8,128)S(1)}, u32[]{:S(2)}, u32[]{:S(2)}) collective-permute-start(f32[5,1024,128]{2,1,0:T(8,128)S(1)} %get-tuple-element.36.own), channel_id=1, source_target_pairs={{0,1},{1,0},{2,3},{3,2},{4,5},{5,4},{6,7},{7,6},{8,9},{9,8},{10,11... | collective-permute-start | bytes 7864328 | tf_op jit(solution)/shard_map/ppermute | solution.py:526
  5.8 9.7 %collective-permute-start.1 = (f32[9,32,128]{2,1,0:T(8,128)S(1)}, f32[9,32,128]{2,1,0:T(8,128)S(1)}, u32[]{:S(2)}, u32[]{:S(2)}) collective-permute-start(f32[9,32,128]{2,1,0:T(8,128)S(1)} %get-tuple-element.35), channel_id=1, source_target_pairs={{1,2},{3,4},{5,6},{7,8},{9,10},{11,12},{13,14},{15,16},{17,18},{19... | collective-permute-start | bytes 442376 | tf_op jit(solution)/shard_map/ppermute | solution.py:524
  9.0 8.9 %collective-permute-start.3 = (f32[12,32,128]{2,1,0:T(8,128)S(1)}, f32[12,32,128]{2,1,0:T(8,128)S(1)}, u32[]{:S(2)}, u32[]{:S(2)}) collective-permute-start(f32[12,32,128]{2,1,0:T(8,128)S(1)} %get-tuple-element.38.own), channel_id=1, source_target_pairs={{0,1},{1,0},{2,3},{3,2},{4,5},{5,4},{6,7},{7,6},{8,9},{9,8},{10,11... | collective-permute-start | bytes 589832 | tf_op jit(solution)/shard_map/ppermute | solution.py:525
  15.5 3.3 %collective-permute-start.4 = (f32[9,32,128]{2,1,0:T(8,128)S(1)}, f32[9,32,128]{2,1,0:T(8,128)S(1)}, u32[]{:S(2)}, u32[]{:S(2)}) collective-permute-start(f32[9,32,128]{2,1,0:T(8,128)S(1)} %collective-permute-done.1.far), channel_id=1, source_target_pairs={{0,1},{1,0},{2,3},{3,2},{4,5},{5,4},{6,7},{7,6},{8,9},{9,8},{10,11... | collective-permute-start | bytes 442376 | tf_op jit(solution)/shard_map/ppermute | solution.py:528
  21.9 7.1 %collective-permute-start.6 = (f32[3,32,128]{2,1,0:T(8,128)S(1)}, f32[3,32,128]{2,1,0:T(8,128)S(1)}, u32[]{:S(2)}, u32[]{:S(2)}) collective-permute-start(f32[3,32,128]{2,1,0:T(8,128)S(1)} %get-tuple-element.44), channel_id=1, source_target_pairs={{1,2},{3,4},{5,6},{7,8},{9,10},{11,12},{13,14},{15,16},{17,18},{19... | collective-permute-start | bytes 147464 | tf_op jit(solution)/shard_map/ppermute | solution.py:494
  23.9 9.3 %collective-permute-start.5 = (f32[4,32,128]{2,1,0:T(8,128)S(1)}, f32[4,32,128]{2,1,0:T(8,128)S(1)}, u32[]{:S(2)}, u32[]{:S(2)}) collective-permute-start(f32[4,32,128]{2,1,0:T(8,128)S(1)} %get-tuple-element.43.own), channel_id=1, source_target_pairs={{0,1},{1,0},{2,3},{3,2},{4,5},{5,4},{6,7},{7,6},{8,9},{9,8},{10,11... | collective-permute-start | bytes 196616 | tf_op jit(solution)/shard_map/ppermute | solution.py:495
  29.0 5.0 %collective-permute-start.7 = (f32[3,32,128]{2,1,0:T(8,128)S(1)}, f32[3,32,128]{2,1,0:T(8,128)S(1)}, u32[]{:S(2)}, u32[]{:S(2)}) collective-permute-start(f32[3,32,128]{2,1,0:T(8,128)S(1)} %collective-permute-done.6.far), channel_id=1, source_target_pairs={{0,1},{1,0},{2,3},{3,2},{4,5},{5,4},{6,7},{7,6},{8,9},{9,8},{10,11... | collective-permute-start | bytes 147464 | tf_op jit(solution)/shard_map/ppermute | solution.py:496
  35.3 7.1 %collective-permute-start.9 = (f32[3,32,128]{2,1,0:T(8,128)S(1)}, f32[3,32,128]{2,1,0:T(8,128)S(1)}, u32[]{:S(2)}, u32[]{:S(2)}) collective-permute-start(f32[3,32,128]{2,1,0:T(8,128)S(1)} %get-tuple-element.47), channel_id=1, source_target_pairs={{1,2},{3,4},{5,6},{7,8},{9,10},{11,12},{13,14},{15,16},{17,18},{19... | collective-permute-start | bytes 147464 | tf_op jit(solution)/shard_map/ppermute | solution.py:494
  37.2 9.3 %collective-permute-start.8 = (f32[4,32,128]{2,1,0:T(8,128)S(1)}, f32[4,32,128]{2,1,0:T(8,128)S(1)}, u32[]{:S(2)}, u32[]{:S(2)}) collective-permute-start(f32[4,32,128]{2,1,0:T(8,128)S(1)} %get-tuple-element.46.own), channel_id=1, source_target_pairs={{0,1},{1,0},{2,3},{3,2},{4,5},{5,4},{6,7},{7,6},{8,9},{9,8},{10,11... | collective-permute-start | bytes 196616 | tf_op jit(solution)/shard_map/ppermute | solution.py:495
  42.4 5.0 %collective-permute-start.10 = (f32[3,32,128]{2,1,0:T(8,128)S(1)}, f32[3,32,128]{2,1,0:T(8,128)S(1)}, u32[]{:S(2)}, u32[]{:S(2)}) collective-permute-start(f32[3,32,128]{2,1,0:T(8,128)S(1)} %collective-permute-done.9.far), channel_id=1, source_target_pairs={{0,1},{1,0},{2,3},{3,2},{4,5},{5,4},{6,7},{7,6},{8,9},{9,8},{10,11... | collective-permute-start | bytes 147464 | tf_op jit(solution)/shard_map/ppermute | solution.py:496
  48.7 7.1 %collective-permute-start.12 = (f32[3,32,128]{2,1,0:T(8,128)S(1)}, f32[3,32,128]{2,1,0:T(8,128)S(1)}, u32[]{:S(2)}, u32[]{:S(2)}) collective-permute-start(f32[3,32,128]{2,1,0:T(8,128)S(1)} %get-tuple-element.50), channel_id=1, source_target_pairs={{1,2},{3,4},{5,6},{7,8},{9,10},{11,12},{13,14},{15,16},{17,18},{19... | collective-permute-start | bytes 147464 | tf_op jit(solution)/shard_map/ppermute | solution.py:494
  50.6 9.3 %collective-permute-start.11 = (f32[4,32,128]{2,1,0:T(8,128)S(1)}, f32[4,32,128]{2,1,0:T(8,128)S(1)}, u32[]{:S(2)}, u32[]{:S(2)}) collective-permute-start(f32[4,32,128]{2,1,0:T(8,128)S(1)} %get-tuple-element.49.own), channel_id=1, source_target_pairs={{0,1},{1,0},{2,3},{3,2},{4,5},{5,4},{6,7},{7,6},{8,9},{9,8},{10,11... | collective-permute-start | bytes 196616 | tf_op jit(solution)/shard_map/ppermute | solution.py:495
  55.8 5.0 %collective-permute-start.13 = (f32[3,32,128]{2,1,0:T(8,128)S(1)}, f32[3,32,128]{2,1,0:T(8,128)S(1)}, u32[]{:S(2)}, u32[]{:S(2)}) collective-permute-start(f32[3,32,128]{2,1,0:T(8,128)S(1)} %collective-permute-done.12.far), channel_id=1, source_target_pairs={{0,1},{1,0},{2,3},{3,2},{4,5},{5,4},{6,7},{7,6},{8,9},{9,8},{10,11... | collective-permute-start | bytes 147464 | tf_op jit(solution)/shard_map/ppermute | solution.py:496
  62.0 1.3 %collective-permute-start.14 = (f32[4,32,128]{2,1,0:T(8,128)S(1)}, f32[4,32,128]{2,1,0:T(8,128)S(1)}, u32[]{:S(2)}, u32[]{:S(2)}) collective-permute-start(f32[4,32,128]{2,1,0:T(8,128)S(1)} %get-tuple-element.54.own), channel_id=1, source_target_pairs={{0,1},{1,0},{2,3},{3,2},{4,5},{5,4},{6,7},{7,6},{8,9},{9,8},{10,11... | collective-permute-start | bytes 196616 | tf_op jit(solution)/shard_map/ppermute | solution.py:548
  65.3 1.3 %collective-permute-start.15 = (f32[160,128]{1,0:T(8,128)S(1)}, f32[160,128]{1,0:T(8,128)S(1)}, u32[]{:S(2)}, u32[]{:S(2)}) collective-permute-start(f32[160,128]{1,0:T(8,128)S(1)} %get-tuple-element.55), channel_id=1, source_target_pairs={{0,1},{1,0},{2,3},{3,2},{4,5},{5,4},{6,7},{7,6},{8,9},{9,8},{10,11... | collective-permute-start | bytes 245768 | tf_op jit(solution)/shard_map/ppermute | solution.py:554
  66.6 8.2 %collective-permute-start.16 = (f32[2,160,128]{2,1,0:T(8,128)S(1)}, f32[2,160,128]{2,1,0:T(8,128)S(1)}, u32[]{:S(2)}, u32[]{:S(2)}) collective-permute-start(f32[2,160,128]{2,1,0:T(8,128)S(1)} %pad_maximum_fusion.own), channel_id=1, source_target_pairs={{2,1},{4,3},{6,5},{8,7},{10,9},{12,11},{14,13},{16,15},{18,17},{20... | collective-permute-start | bytes 491528 | tf_op jit(solution)/shard_map/ppermute | solution.py:556
  68.5 6.3 %collective-permute-start.17 = (f32[32,128]{1,0:T(8,128)S(1)}, f32[32,128]{1,0:T(8,128)S(1)}, u32[]{:S(2)}, u32[]{:S(2)}) collective-permute-start(f32[32,128]{1,0:T(8,128)S(1)} %get-tuple-element.56), channel_id=1, source_target_pairs={{6,1},{8,3},{10,5},{12,7},{14,9},{16,11},{18,13},{20,15},{22,17},{... | collective-permute-start | bytes 49160 | tf_op jit(solution)/shard_map/ppermute | solution.py:553
  74.8 10.5 %collective-permute-start.18 = (f32[2,160,128]{2,1,0:T(8,128)S(1)}, f32[2,160,128]{2,1,0:T(8,128)S(1)}, u32[]{:S(2)}, u32[]{:S(2)}) collective-permute-start(f32[2,160,128]{2,1,0:T(8,128)S(1)} %collective-permute-done.16.far), channel_id=1, source_target_pairs={{0,1},{1,0},{2,3},{3,2},{4,5},{5,4},{6,7},{7,6},{8,9},{9,8},{10,11... | collective-permute-start | bytes 491528 | tf_op jit(solution)/shard_map/ppermute | solution.py:565
  84.1 1.2 %collective-permute-start.19 = (f32[32,128]{1,0:T(8,128)S(1)}, f32[32,128]{1,0:T(8,128)S(1)}, u32[]{:S(2)}, u32[]{:S(2)}) collective-permute-start(f32[32,128]{1,0:T(8,128)S(1)} %collective-permute-done.17.side), channel_id=1, source_target_pairs={{0,1},{1,0},{2,3},{3,2},{4,5},{5,4},{6,7},{7,6},{8,9},{9,8},{10,11... | collective-permute-start | bytes 49160 | tf_op jit(solution)/shard_map/ppermute | solution.py:566

commit v2 on v1

--- a/solution.py
+++ b/solution.py
@@ -75,47 +75,56 @@
     ix, iy, _ = positions(base)
     low = core == 0
     start = jnp.where(low, 4 - extra, extra)
-    moved = (lane + 32 * start) % 128
-    cut = 128 - 32 * start
-
-    def window(face, slab, rows):
-        a = oth[face, rows, :]
-        b = jnp.zeros((8, 128), F32) if post is None else post[slab, rows, :]
-        lead = pick(jnp.where(low, a, b), moved)
-        tail = pick(jnp.where(low, b, a), moved)
-        return jnp.where(lane < cut, lead, tail)
-
-    def sides(face, slab, rows):
-        mid = window(face, slab, rows)
-        edge = jnp.zeros((8, 128), F32) if far is None else far[slab, rows, :]
-        return jnp.where(low, edge, mid), jnp.where(low, mid, edge)
-
+    single = 1 if far is not None and len(far.shape) == 2 else 0
+    x_far = jnp.where(low, 32, 64) + single
+    x_post = jnp.where(low, 64, 32) + single
+    x_turn = jnp.where(low, 96, 32)
+
+    def mixer(turn, lift):
+        target = (lane + turn) % 128
+        index, index_post = (target + 32 * start) % 128, (target + 32 * start + lift) % 128
+        here = jnp.where(target < 128 - 32 * start, 1, 0) == 1 - core
+        if post is None:
+            return lambda a, b: jnp.where(here, pick(a, index), 0.0)
+        return lambda a, b: jnp.where(here, pick(a, index), pick(b, index_post))
+
+    mix_z, mix_y, mix_x = mixer(0, 0), mixer(64, single), mixer(128 - x_turn, x_post)
+    y_index = (lane + 64 + single) % 128
+    x_index = (lane + x_far + jnp.where(low, 96, 32)) % 128
+    own_index = jnp.where(ix == 1, lane + 96, lane + 32) % 128
     for t in range(TILES):
         rows = part(t)
-        out[0, rows, :], out[1, rows, :] = sides(core, 0, rows)
-        below, above = sides(2, 1, rows)
+        if far is None:
+            z_edge = y_edge = x_edge = 0.0
+            z_post = nearest_post = None
+        else:
+            z_edge = far[rows, :] if single else far[0, rows, :]
+            nearest = z_edge if single else far[1, rows, :]
+            z_post = post[rows, :] if single else post[0, rows, :]
+            nearest_post = z_post if single else post[1, rows, :]
+            y_edge, x_edge = pick(nearest, y_index), pick(nearest, x_index)
+        mid = mix_z(oth[core, rows, :], z_post)
+        out[0, rows, :], out[1, rows, :] = jnp.where(low, z_edge, mid), jnp.where(low, mid, z_edge)
+        mid = mix_y(oth[2, rows, :], nearest_post)
         inner = turned(own[2, rows, :], 64)
+        below, above = jnp.where(low, y_edge, mid), jnp.where(low, mid, y_edge)
         out[2, rows, :] = jnp.where(
-            iy == 1,
-            jnp.where(lane < 64, turned(below, 64), inner),
-            jnp.where(lane < 64, inner, turned(above, 64)),
+            iy == 1, jnp.where(lane < 64, below, inner), jnp.where(lane < 64, inner, above)
         )
-        below, above = sides(3, 2, rows)
-        inner = own[3, rows, :]
+        mid = mix_x(oth[3, rows, :], nearest_post)
+        inner = pick(own[3, rows, :], own_index)
+        below, above = jnp.where(low, x_edge, mid), jnp.where(low, mid, x_edge)
         out[3, rows, :] = jnp.where(
-            ix == 1,
-            turned(jnp.where(lane < 96, inner, below), 32),
-            turned(jnp.where(lane < 32, above, inner), 96),
+            ix == 1, jnp.where(lane < 32, below, inner), jnp.where(lane >= 96, above, inner)
         )
 
 
-def pad(base, ref, ghost, padded, outside):
-    _, iy, iz = positions(base)
+def pad(base, ref, ghost, padded):
+    _, iy, _ = positions(base)
     for t in range(TILES):
         rows = part(t)
-        low_own, high_own = ref[rows, :], ref[pl.ds(31 * SPAN + 8 * t, 8), :]
-        padded[0, 8 + 8 * t : 16 + 8 * t, :] = jnp.where(iy == 1, ghost[2, rows, :], outside(low_own))
-        padded[SPAN + 1, 8 + 8 * t : 16 + 8 * t, :] = jnp.where(iy == 0, ghost[2, rows, :], outside(high_own))
+        padded[0, 8 + 8 * t : 16 + 8 * t, :] = jnp.where(iy == 1, ghost[2, rows, :], 0.0)
+        padded[SPAN + 1, 8 + 8 * t : 16 + 8 * t, :] = jnp.where(iy == 0, ghost[2, rows, :], 0.0)
 
     def layer(y, carry):
         for t in range(TILES):
@@ -149,10 +158,6 @@
 def inverted(x):
     guess = pl.reciprocal(x, approx=True)
     return guess * (2.0 - x * guess)
-
-
-def zero(own):
-    return 0.0
 
 
 def collect_kernel(holder, v, f, k, c, kind, scalars, own, faces, bounds, hv, hf, hk, hc, hkind, sems):
@@ -200,18 +205,32 @@
     for i in range(12):
         for t in range(TILES):
             faces[i, part(t), :] = windowed(own[i, part(t), :], oth[i, part(t), :])
-    for i in range(3):
-        put_sent(scalars, faces.at[pl.ds(4 * i, 4)], sent.at[pl.ds(3 * i, 3)])
-
-
-def put_sent(scalars, faces, sent):
+    put_sent(scalars, 1, faces, sent.at[0])
+    for i in (1, 2):
+        for t in range(TILES):
+            z, nearest = outgoing(scalars, faces.at[pl.ds(4 * i, 4)], t, 0)
+            sent[2 * i - 1, part(t), :] = z
+            sent[2 * i, part(t), :] = nearest
+
+
+def outgoing(scalars, faces, t, by):
+    core = scalars[0]
+    lane = (lanes() + 128 - by) % 128
+    along_y = jnp.where(lane >= 64, 1, 0) == core
+    y = faces[2, part(t), :]
+    y = turned(y, by) if by else y
+    x = pick(faces[3, part(t), :], (lane + 64 + 32 * core) % 128)
+    return faces[core, part(t), :], jnp.where(along_y, y, x)
+
+
+def put_sent(scalars, shade, faces, sent):
+    mine = (lax.broadcasted_iota(jnp.int32, (8, 128), 0) + lanes() + scalars[0]) % 2 == shade
     for t in range(TILES):
-        sent[0, part(t), :] = faces[scalars[0], part(t), :]
-        sent[1, part(t), :] = faces[2, part(t), :]
-        sent[2, part(t), :] = faces[3, part(t), :]
-
-
-def window_kernel(scalars, own, oth, window):
+        z, nearest = outgoing(scalars, faces, t, 1)
+        sent[part(t), :] = jnp.where(mine, z, nearest)
+
+
+def window_kernel(scalars, own, oth, window, inner):
     windowed = window_of(scalars)
     for i in range(5):
 
@@ -223,59 +242,96 @@
 
         lax.fori_loop(0, SPAN, rows, 0, unroll=8)
 
-
-def first_kernel(layers, scalars, fields, own, oth, far, post, vo, fo, do, go, edge, faces, sent, ghost, pv, pk, pa):
+    row = lax.broadcasted_iota(jnp.int32, (8, 128), 0)
+
+    def layer(y, carry):
+        above = jnp.minimum(y + 1, SPAN - 1)
+        heat = [window[2, tile_row(y, t), :] for t in range(TILES)]
+        open_heat = [heat[t] * window[4, tile_row(y, t), :] for t in range(TILES)]
+        heat_up = [pltpu.roll(x, 7, axis=0) for x in heat]
+        open_up = [pltpu.roll(x, 7, axis=0) for x in open_heat]
+        below = None
+        for t in range(TILES):
+            at = tile_row(y, t)
+            doubled = 2.0 * open_heat[t]
+            beside = doubled * turned(open_heat[t], 127) * inverted(heat[t] + turned(heat[t], 127))
+            inner[0, at, :] = turned(beside, 1)
+            inner[1, at, :] = beside
+            heat2 = window[2, tile_row(above, t), :]
+            inner[2, at, :] = doubled * window[4, tile_row(above, t), :] * heat2 * inverted(heat[t] + heat2)
+            heat2, open2 = heat_up[t], open_up[t]
+            if t < TILES - 1:
+                heat2 = jnp.where(row == 7, heat_up[t + 1], heat2)
+                open2 = jnp.where(row == 7, open_up[t + 1], open2)
+            over = doubled * open2 * inverted(heat[t] + heat2)
+            inner[4, at, :] = over
+            lifted = pltpu.roll(over, 1, axis=0)
+            inner[3, at, :] = lifted if below is None else jnp.where(row == 0, below, lifted)
+            below = lifted
+        return carry
+
+    lax.fori_loop(0, SPAN, layer, 0, unroll=2)
+
+
+def first_kernel(
+    layers, scalars, fields, inner, own, oth, far, post, vo, fo, do, go, edge, faces, sent, ghost, pv, ends
+):
     v, f, k, c, a = (fields.at[i] for i in range(5))
     where = whereabouts(scalars)
     base = where[1]
     ix, iy, iz = positions(base)
     lane = lanes()
+    row = lax.broadcasted_iota(jnp.int32, (8, 128), 0)
     for number in range(3):
-        group, outer = pl.ds(4 * number, 4), pl.ds(3 * number, 3)
+        group, outer = pl.ds(4 * number, 4), pl.ds(2 * number - 1, 2) if number else 0
         ghosts(where, own.at[group], oth.at[group], far.at[outer], post.at[outer], ghost.at[number])
-    for face in range(4):
-        for t in range(TILES):
-            rows = part(t)
-            heat, heat2 = own[4 + face, rows, :], ghost[1, face, rows, :]
-            opening, opening2 = own[8 + face, rows, :], ghost[2, face, rows, :]
-            edge[face, rows, :] = 2.0 * opening * heat * opening2 * heat2 * inverted(heat + heat2)
     for t in range(TILES):
         rows = part(t)
-        for face, gone, row in ((0, iz == 0, 0), (1, iz == layers - 1, 31)):
-            edge = k[pl.ds(256 * t + row, 8, stride=SPAN), :]
-            ghost[1, face, rows, :] = jnp.where(gone, edge, ghost[1, face, rows, :])
-            ghost[2, face, rows, :] = jnp.where(gone, 1.0, ghost[2, face, rows, :])
-    pad(base, v, ghost.at[0], pv, zero)
-    pad(base, k, ghost.at[1], pk, lambda mine: mine)
-    pad(base, a, ghost.at[2], pa, lambda mine: 1.0)
-    edges = ((lane % 32 == 0) & (ix == 0), (lane % 32 == 31) & (ix == 1))
+        for face in range(4):
+            heat, heat2 = own[4 + face, rows, :], ghost[1, face, rows, :]
+            open_heat = heat * own[8 + face, rows, :]
+            b = 2.0 * open_heat * ghost[2, face, rows, :] * heat2 * inverted(heat + heat2)
+            edge[face, rows, :] = b
+            if face < 2:
+                ends[face, rows, :] = jnp.where(iz == (layers - 1 if face else 0), open_heat, b)
+    pad(base, v, ghost.at[0], pv)
+    low_in, low_out = (lane % 32 == 0) & (ix == 1), (lane % 32 == 0) & (ix == 0)
+    high_in, high_out = (lane % 32 == 31) & (ix == 0), (lane % 32 == 31) & (ix == 1)
 
     def layer(y, carry):
         shade = parity(y)
         for t in range(TILES):
             rows = tile_row(y, t)
             value, values = around(y, t, pv, ghost.at[0])
-            heat, heats = around(y, t, pk, ghost.at[1])
-            opening, openings = around(y, t, pa, ghost.at[2])
-            coefficients = []
-            summed = None
-            doubled = 2.0 * opening * heat
-            for way in range(6):
-                heat2, opening2 = heats[way], openings[way]
-                if way < 2:
-                    heat2 = jnp.where(edges[way], heat, heat2)
-                    opening2 = jnp.where(edges[way], 1.0, opening2)
-                b = doubled * opening2 * heat2 * inverted(heat + heat2)
-                summed = b if summed is None else summed + b
-                coefficients.append(jnp.where(edges[way], 0.0, b) if way < 2 else b)
+            heat, opening = k[rows, :], a[rows, :]
+            open_heat = heat * opening
+            b_x = pick(edge[3, part(t), :], 32 * (lane // 32) + y)
+            b_y = edge[2, part(t), :]
+            b = [
+                jnp.where(low_in, b_x, jnp.where(low_out, open_heat, inner[0, rows, :])),
+                jnp.where(high_in, b_x, jnp.where(high_out, open_heat, inner[1, rows, :])),
+                jnp.where(
+                    y == 0, jnp.where(iy == 1, b_y, open_heat), inner[2, tile_row(jnp.maximum(y - 1, 0), t), :]
+                ),
+                jnp.where(y == SPAN - 1, jnp.where(iy == 0, b_y, open_heat), inner[2, rows, :]),
+                inner[3, rows, :],
+                inner[4, rows, :],
+            ]
+            if t == 0:
+                b[4] = jnp.where(row == 0, ends[0, pl.ds(y, 1), :], b[4])
+            if t == TILES - 1:
+                b[5] = jnp.where(row == 7, ends[1, pl.ds(y, 1), :], b[5])
+            summed = (b[0] + b[1]) + (b[2] + b[3]) + (b[4] + b[5])
             wall = jnp.where(opening == 0.5, heat, 0.0)
             diagonal = jnp.where(opening == 0.0, 1.0, c[rows, :] + summed + wall)
             inverse = inverted(diagonal)
             total = f[rows, :] * inverse
             fo[rows, :] = total
             do[rows, :] = diagonal
+            b[0] = jnp.where(low_out, 0.0, b[0])
+            b[1] = jnp.where(high_out, 0.0, b[1])
             for way in range(6):
-                g = coefficients[way] * inverse
+                g = b[way] * inverse
                 go[way, rows, :] = g
                 total = total + g * values[way]
             vo[rows, :] = jnp.where(shade == 0, total, value)
@@ -283,7 +339,7 @@
 
     lax.fori_loop(0, SPAN, layer, 0, unroll=4)
     put_faces(base, vo, faces)
-    put_sent(scalars, faces, sent)
+    put_sent(scalars, 0, faces, sent)
 
 
 def relaxed(y, t, f, g, padded, ghost):
@@ -300,7 +356,7 @@
     where = whereabouts(scalars)
     base = where[1]
     ghosts(where, own, oth, far, post, ghost)
-    pad(base, v, ghost, padded, zero)
+    pad(base, v, ghost, padded)
 
     def layer(y, carry):
         shade = parity(y)
@@ -312,14 +368,14 @@
     lax.fori_loop(0, SPAN, layer, 0, unroll=8)
     put_faces(base, vo, faces)
     if sent:
-        put_sent(scalars, faces, sent[0])
+        put_sent(scalars, shade_now, faces, sent[0])
 
 
 def residual_kernel(scalars, v, f, g, d, edge, own, oth, blocks, cross, ghost, padded, pair):
     where = whereabouts(scalars)
     core = where[0]
     ghosts(where, own, oth, None, None, ghost)
-    pad(where[1], v, ghost, padded, zero)
+    pad(where[1], v, ghost, padded)
     lane = lanes()
     index = 2 * (lane % 64)
 
@@ -499,8 +555,8 @@
     fields = [x.reshape(SLOTS * SPAN, LAYER) for x in (v, f, k, c, kind)]
     five = jax.ShapeDtypeStruct((5, LAYER, 128), F32)
     twelve = jax.ShapeDtypeStruct((12, SPAN, 128), F32)
-    nine = jax.ShapeDtypeStruct((9, SPAN, 128), F32)
-    three = jax.ShapeDtypeStruct((3, SPAN, 128), F32)
+    sent_first = jax.ShapeDtypeStruct((5, SPAN, 128), F32)
+    sent_later = jax.ShapeDtypeStruct((SPAN, 128), F32)
     scalars, own, faces = call(
         collect_kernel,
         [pltpu.SMEM((6,), jnp.int32), pltpu.VMEM(five.shape, F32), pltpu.VMEM(twelve.shape, F32)],
@@ -516,25 +572,25 @@
     )
     faces, sent = call(
         face_window_kernel,
-        [twelve, nine],
+        [twelve, sent_first],
         [scalars, faces, lax.ppermute(faces, AXES, swap)],
         name="face_window",
     )
     sent, own = lax.optimization_barrier((sent, own))
     far = lax.ppermute(sent, AXES, reach)
     oth = lax.ppermute(faces, AXES, swap)
-    window = call(window_kernel, five, [scalars, own, lax.ppermute(own, AXES, swap)], name="window")
-    far, window = lax.optimization_barrier((far, window))
+    window, inner = call(window_kernel, [five, five], [scalars, own, lax.ppermute(own, AXES, swap)], name="window")
+    far, window, inner = lax.optimization_barrier((far, window, inner))
     post = lax.ppermute(far, AXES, swap)
     coefficients = jax.ShapeDtypeStruct((6, LAYER, 128), F32)
     wv, wf, wd, wg, edge, faces, *sent = call(
         functools.partial(first_kernel, patches // 4),
-        [FIELD, FIELD, FIELD, coefficients, FACES, FACES, three],
-        [scalars, window, faces, oth, far, post],
-        scratch=[pltpu.VMEM((3, 4, SPAN, 128), F32)] + [PADDED] * 3,
+        [FIELD, FIELD, FIELD, coefficients, FACES, FACES, sent_later],
+        [scalars, window, inner, faces, oth, far, post],
+        scratch=[pltpu.VMEM((3, 4, SPAN, 128), F32), PADDED, pltpu.VMEM((2, SPAN, 128), F32)],
         name="first",
     )
-    for shade, more in ((1, [three]), (0, [three]), (1, [])):
+    for shade, more in ((1, [sent_later]), (0, [sent_later]), (1, [])):
         wv, faces, *sent = call(
             functools.partial(sweep_kernel, shade),
             [FIELD, FACES] + more,
@@ -550,10 +606,10 @@
         name="residual",
     )
     beside = [(i, i - 5) for i in range(6, devices, 2)] + [(i, i + 1) for i in range(1, devices - 1, 2)]
-    side = lax.ppermute(cross, AXES, beside)
     both = jnp.stack([blocks, lax.ppermute(blocks, AXES, swap)], 0)
     downward = [(i, i - 1) for i in range(2, devices, 2)] + [(i, i - 5) for i in range(5, devices, 2)]
     far = lax.ppermute(both, AXES, downward)
+    side = lax.ppermute(cross, AXES, beside)
     level = call(
         level_kernel,
         jax.ShapeDtypeStruct((SLOTS, SPAN, LAYER), F32),
@@ -561,7 +617,7 @@
         scratch=[pltpu.VMEM((128, LAYER), F32)],
         name="level",
     )
-    far, side, level = lax.optimization_barrier((far, side, level))
+    side, far, level = lax.optimization_barrier((side, far, level))
     post = lax.ppermute(far, AXES, swap)
     side_post = lax.ppermute(side, AXES, swap)
     grid = call(

time: 87.1 us -> 85.5 us (0.982)
  starting transfers between devices: 59.6 us -> 45.5 us
  waiting for transfers between devices: 9.34 us -> 19.6 us
  Pallas kernels: 16.2 us -> 18.1 us
    ppermute x3, starting transfers between devices: 15.5 us -> 1.15 us  [exchange(): oth = lax.ppermute(faces, AXES, swap)]
    ppermute x3, waiting for transfers between devices: 0.01 us -> 9.39 us  [exchange(): far = lax.ppermute(sent, AXES, reach)]
    ppermute x3, starting transfers between devices: 12.3 us -> 16.8 us  [exchange(): post = lax.ppermute(far, AXES, swap)]
    ppermute x1, starting transfers between devices: 3.72 us -> 0.14 us  [shards(): oth = lax.ppermute(faces, AXES, swap)]
    pallas_call x10, Pallas kernels: 16.2 us -> 18.1 us  [call(): pl.pallas_call(kernel, out_shape=out_shape, in_specs=list(leading) + (spe...]
    ppermute x1, waiting for transfers between devices: 0.01 us -> 1.03 us  [shards(): lax.ppermute(own, AXES, swap)]
  transfers between devices with their start and end apart: 20 -> 20, of which waited for: 9 -> 13; matrix products, arithmetic and copies ran while one was open for 0% -> 0% of each run, Pallas kernels for 4% -> 8%
where the time goes in v2:
time: 85.5 us; the launch traced here: 84 us
  starting transfers between devices  45.5 us (53%)
  waiting for transfers between devices  19.6 us (23%)
  Pallas kernels  18.1 us (21%)
    pallas_call x10, Pallas kernels, call(): pl.pallas_call(kernel, out_shape=out_shape, in_specs=list(leading) + (spe...  18.1 us
    ppermute x3, starting transfers between devices, exchange(): post = lax.ppermute(far, AXES, swap)  16.8 us
    ppermute x2, starting transfers between devices, shards(): post = lax.ppermute(far, AXES, swap)  10.8 us
    ppermute x3, waiting for transfers between devices, exchange(): far = lax.ppermute(sent, AXES, reach)  9.39 us
    ppermute x3, starting transfers between devices, exchange(): far = lax.ppermute(sent, AXES, reach)  5.73 us
    ppermute x1, starting transfers between devices, shards(): side = lax.ppermute(cross, AXES, beside)  3.64 us
    ppermute x1, starting transfers between devices, shards(): far = lax.ppermute(sent, AXES, reach)  3.36 us
    ppermute x3, waiting for transfers between devices, exchange(): post = lax.ppermute(far, AXES, swap)  2.52 us
  transfers between devices with their start and end apart: 20, of which 13 were waited for; matrix products, arithmetic and copies ran while one was open for 0% of the time, Pallas kernels for 8%

profile of v2, /device:TPU:129, one launch (start us, length us, event | category | flops | bytes accessed | tf_op | source)
XLA Modules:
  0.0 84.0 jit_solution(12650295578650034966)
XLA Ops:
  0.6 2.7 %collect.1 = (s32[6]{0:T(128)S(4)}, f32[5,1024,128]{2,1,0:T(8,128)S(1)}, f32[12,32,128]{2,1,0:T(8,128)S(1)}) custom-call(s32[6,128]{1,0:T(8,128)} %bitcast.15, f32[128,1024]{1,0:T(8,128)} %bitcast.9, f32[128,1024]{1,0:T(8,128)} %bitcast.10, f32[128,1024]{1,0:T(8,128)} %bitcast.11, f32[128,1024]{1,0:T(8,128)} %bitcast.12, s32[128,1024]{1,0:T(8,128)} %bitcast.13), custom_call_target="tpu_custom_call" | custom-call | tf_op jit(solution)/shard_map/collect/pallas_call | solution.py:531
  3.4 0.8 collective-permute-start
  4.1 1.1 %collective-permute-done.oth = f32[12,32,128]{2,1,0:T(8,128)S(1)} collective-permute-done((f32[12,32,128]{2,1,0:T(8,128)S(1)}, f32[12,32,128]{2,1,0:T(8,128)S(1)}, u32[]{:S(2)}, u32[]{:S(2)}) %collective-permute-start) | collective-permute-done | bytes 196640 | tf_op jit(solution)/shard_map/ppermute | solution.py:576
  5.2 0.3 face_window.1
  5.4 0.4 collective-permute-start.2
  5.9 0.1 collective-permute-start.3
  6.0 3.4 %collective-permute-start.1 = (f32[5,32,128]{2,1,0:T(8,128)S(1)}, f32[5,32,128]{2,1,0:T(8,128)S(1)}, u32[]{:S(2)}, u32[]{:S(2)}) collective-permute-start(f32[5,32,128]{2,1,0:T(8,128)S(1)} %get-tuple-element.38), channel_id=1, source_target_pairs={{1,2},{3,4},{5,6},{7,8},{9,10},{11,12},{13,14},{15,16},{17,18},{19... | collective-permute-start | bytes 245768 | tf_op jit(solution)/shard_map/ppermute | solution.py:580
  9.4 1.0 %collective-permute-done.2.oth = f32[5,1024,128]{2,1,0:T(8,128)S(1)} collective-permute-done((f32[5,1024,128]{2,1,0:T(8,128)S(1)}, f32[5,1024,128]{2,1,0:T(8,128)S(1)}, u32[]{:S(2)}, u32[]{:S(2)}) %collective-permute-start.2) | collective-permute-done | bytes 2621472 | tf_op jit(solution)/shard_map/ppermute | solution.py:582
  10.4 5.3 %window.1 = (f32[5,1024,128]{2,1,0:T(8,128)S(1)}, f32[5,1024,128]{2,1,0:T(8,128)S(1)}) custom-call(s32[6]{0:T(128)S(4)} %get-tuple-element.34.scalars, f32[5,1024,128]{2,1,0:T(8,128)S(1)} %get-tuple-element.39.own, f32[5,1024,128]{2,1,0:T(8,128)S(1)} %collective-permute-done.2.oth), custom_call_target="tpu_custom_call" | custom-call | tf_op jit(solution)/shard_map/window/pallas_call | solution.py:531
  15.7 0.0 collective-permute-done.1.far
  15.7 2.5 %collective-permute-start.4 = (f32[5,32,128]{2,1,0:T(8,128)S(1)}, f32[5,32,128]{2,1,0:T(8,128)S(1)}, u32[]{:S(2)}, u32[]{:S(2)}) collective-permute-start(f32[5,32,128]{2,1,0:T(8,128)S(1)} %collective-permute-done.1.far), channel_id=1, source_target_pairs={{0,1},{1,0},{2,3},{3,2},{4,5},{5,4},{6,7},{7,6},{8,9},{9,8},{10,11... | collective-permute-start | bytes 245768 | tf_op jit(solution)/shard_map/ppermute | solution.py:584
  18.2 0.0 collective-permute-done.3.oth
  18.2 0.9 %collective-permute-done.4.post = f32[5,32,128]{2,1,0:T(8,128)S(1)} collective-permute-done((f32[5,32,128]{2,1,0:T(8,128)S(1)}, f32[5,32,128]{2,1,0:T(8,128)S(1)}, u32[]{:S(2)}, u32[]{:S(2)}) %collective-permute-start.4) | collective-permute-done | bytes 81952 | tf_op jit(solution)/shard_map/ppermute | solution.py:584
  19.1 2.3 %first.1 = (f32[1024,128]{1,0:T(8,128)S(1)}, f32[1024,128]{1,0:T(8,128)S(1)}, f32[1024,128]{1,0:T(8,128)S(1)}, f32[6,1024,128]{2,1,0:T(8,128)S(1)}, f32[4,32,128...) custom-call(s32[6]{0:T(128)S(4)} %get-tuple-element.34.scalars, ...), custom_call_target="tpu_custom_call" | custom-call | tf_op jit(solution)/shard_map/first/pallas_call | solution.py:531
  21.4 0.4 collective-permute-start.5
  21.8 1.9 %collective-permute-start.6 = (f32[32,128]{1,0:T(8,128)S(1)}, f32[32,128]{1,0:T(8,128)S(1)}, u32[]{:S(2)}, u32[]{:S(2)}) collective-permute-start(f32[32,128]{1,0:T(8,128)S(1)} %get-tuple-element.50), channel_id=1, source_target_pairs={{1,2},{3,4},{5,6},{7,8},{9,10},{11,12},{13,14},{15,16},{17,18},{19... | collective-permute-start | bytes 49160 | tf_op jit(solution)/shard_map/ppermute | solution.py:550
  23.7 3.1 %collective-permute-done.6.far = f32[32,128]{1,0:T(8,128)S(1)} collective-permute-done((f32[32,128]{1,0:T(8,128)S(1)}, f32[32,128]{1,0:T(8,128)S(1)}, u32[]{:S(2)}, u32[]{:S(2)}) %collective-permute-start.6) | collective-permute-done | bytes 16416 | tf_op jit(solution)/shard_map/ppermute | solution.py:550
  26.8 5.6 %collective-permute-start.7 = (f32[32,128]{1,0:T(8,128)S(1)}, f32[32,128]{1,0:T(8,128)S(1)}, u32[]{:S(2)}, u32[]{:S(2)}) collective-permute-start(f32[32,128]{1,0:T(8,128)S(1)} %collective-permute-done.6.far), channel_id=1, source_target_pairs={{0,1},{1,0},{2,3},{3,2},{4,5},{5,4},{6,7},{7,6},{8,9},{9,8},{10,11... | collective-permute-start | bytes 49160 | tf_op jit(solution)/shard_map/ppermute | solution.py:552
  32.4 0.8 collective-permute-done.7.post
  33.2 1.4 %sweep.3 = (f32[1024,128]{1,0:T(8,128)S(1)}, f32[4,32,128]{2,1,0:T(8,128)S(1)}, f32[32,128]{1,0:T(8,128)S(1)}) custom-call(s32[6]{0:T(128)S(4)} %get-tuple-element.34.scalars, f32[1024,128]{1,0:T(8,128)S(1)} %get-tuple-element.46.v, f32[1024,128]{1,0:T(8,128)S(1)} %get-tuple-element.47.f, f32[6,1024,128]{2,1,0:T(8,128)S(1)} %get-tuple-element.48.g, ...), custom_call_target="tpu_custom_call" | custom-call | tf_op jit(solution)/shard_map/sweep/pallas_call | solution.py:531
  34.6 0.4 collective-permute-start.8
  35.0 1.9 %collective-permute-start.9 = (f32[32,128]{1,0:T(8,128)S(1)}, f32[32,128]{1,0:T(8,128)S(1)}, u32[]{:S(2)}, u32[]{:S(2)}) collective-permute-start(f32[32,128]{1,0:T(8,128)S(1)} %get-tuple-element.53), channel_id=1, source_target_pairs={{1,2},{3,4},{5,6},{7,8},{9,10},{11,12},{13,14},{15,16},{17,18},{19... | collective-permute-start | bytes 49160 | tf_op jit(solution)/shard_map/ppermute | solution.py:550
  36.9 3.1 %collective-permute-done.9.far = f32[32,128]{1,0:T(8,128)S(1)} collective-permute-done((f32[32,128]{1,0:T(8,128)S(1)}, f32[32,128]{1,0:T(8,128)S(1)}, u32[]{:S(2)}, u32[]{:S(2)}) %collective-permute-start.9) | collective-permute-done | bytes 16416 | tf_op jit(solution)/shard_map/ppermute | solution.py:550
  40.0 5.6 %collective-permute-start.10 = (f32[32,128]{1,0:T(8,128)S(1)}, f32[32,128]{1,0:T(8,128)S(1)}, u32[]{:S(2)}, u32[]{:S(2)}) collective-permute-start(f32[32,128]{1,0:T(8,128)S(1)} %collective-permute-done.9.far), channel_id=1, source_target_pairs={{0,1},{1,0},{2,3},{3,2},{4,5},{5,4},{6,7},{7,6},{8,9},{9,8},{10,11... | collective-permute-start | bytes 49160 | tf_op jit(solution)/shard_map/ppermute | solution.py:552
  45.6 0.8 collective-permute-done.10.post
  46.5 0.0 collective-permute-done.8.oth
  46.5 1.4 %sweep.4 = (f32[1024,128]{1,0:T(8,128)S(1)}, f32[4,32,128]{2,1,0:T(8,128)S(1)}, f32[32,128]{1,0:T(8,128)S(1)}) custom-call(s32[6]{0:T(128)S(4)} %get-tuple-element.34.scalars, f32[1024,128]{1,0:T(8,128)S(1)} %get-tuple-element.51.v, f32[1024,128]{1,0:T(8,128)S(1)} %get-tuple-element.47.f, f32[6,1024,128]{2,1,0:T(8,128)S(1)} %get-tuple-element.48.g, ...), custom_call_target="tpu_custom_call" | custom-call | tf_op jit(solution)/shard_map/sweep/pallas_call | solution.py:531
  47.8 0.4 collective-permute-start.11
  48.2 1.9 %collective-permute-start.12 = (f32[32,128]{1,0:T(8,128)S(1)}, f32[32,128]{1,0:T(8,128)S(1)}, u32[]{:S(2)}, u32[]{:S(2)}) collective-permute-start(f32[32,128]{1,0:T(8,128)S(1)} %get-tuple-element.56), channel_id=1, source_target_pairs={{1,2},{3,4},{5,6},{7,8},{9,10},{11,12},{13,14},{15,16},{17,18},{19... | collective-permute-start | bytes 49160 | tf_op jit(solution)/shard_map/ppermute | solution.py:550
  50.1 3.1 %collective-permute-done.12.far = f32[32,128]{1,0:T(8,128)S(1)} collective-permute-done((f32[32,128]{1,0:T(8,128)S(1)}, f32[32,128]{1,0:T(8,128)S(1)}, u32[]{:S(2)}, u32[]{:S(2)}) %collective-permute-start.12) | collective-permute-done | bytes 16416 | tf_op jit(solution)/shard_map/ppermute | solution.py:550
  53.2 5.6 %collective-permute-start.13 = (f32[32,128]{1,0:T(8,128)S(1)}, f32[32,128]{1,0:T(8,128)S(1)}, u32[]{:S(2)}, u32[]{:S(2)}) collective-permute-start(f32[32,128]{1,0:T(8,128)S(1)} %collective-permute-done.12.far), channel_id=1, source_target_pairs={{0,1},{1,0},{2,3},{3,2},{4,5},{5,4},{6,7},{7,6},{8,9},{9,8},{10,11... | collective-permute-start | bytes 49160 | tf_op jit(solution)/shard_map/ppermute | solution.py:552
  58.8 0.8 collective-permute-done.13.post
  59.7 0.0 collective-permute-done.11.oth
  59.7 1.3 %sweep.5 = (f32[1024,128]{1,0:T(8,128)S(1)}, f32[4,32,128]{2,1,0:T(8,128)S(1)}) custom-call(s32[6]{0:T(128)S(4)} %get-tuple-element.34.scalars, f32[1024,128]{1,0:T(8,128)S(1)} %get-tuple-element.54.v, f32[1024,128]{1,0:T(8,128)S(1)} %get-tuple-element.47.f, f32[6,1024,128]{2,1,0:T(8,128)S(1)} %get-tuple-element.48.g, ...), custom_call_target="tpu_custom_call" | custom-call | tf_op jit(solution)/shard_map/sweep/pallas_call | solution.py:531
  61.0 0.4 collective-permute-start.14
  61.4 0.9 %collective-permute-done.14.oth = f32[4,32,128]{2,1,0:T(8,128)S(1)} collective-permute-done((f32[4,32,128]{2,1,0:T(8,128)S(1)}, f32[4,32,128]{2,1,0:T(8,128)S(1)}, u32[]{:S(2)}, u32[]{:S(2)}) %collective-permute-start.14) | collective-permute-done | bytes 65568 | tf_op jit(solution)/shard_map/ppermute | solution.py:604
  62.3 1.9 %residual.1 = (f32[160,128]{1,0:T(8,128)S(1)}, f32[32,128]{1,0:T(8,128)S(1)}) custom-call(s32[6]{0:T(128)S(4)} %get-tuple-element.34.scalars, f32[1024,128]{1,0:T(8,128)S(1)} %get-tuple-element.57.v, f32[1024,128]{1,0:T(8,128)S(1)} %get-tuple-element.47.f, f32[6,1024,128]{2,1,0:T(8,128)S(1)} %get-tuple-element.48.g, f32[1024,128]{1,0:T(8,128)S(1)} %get-tuple-element.58.d, ...), custom_call_target="tpu_custom_call" | custom-call | tf_op jit(solution)/shard_map/residual/pallas_call | solution.py:531
  64.2 0.4 collective-permute-start.16
  64.5 0.9 %collective-permute-done.16 = f32[160,128]{1,0:T(8,128)S(1)} collective-permute-done((f32[160,128]{1,0:T(8,128)S(1)}, f32[160,128]{1,0:T(8,128)S(1)}, u32[]{:S(2)}, u32[]{:S(2)}) %collective-permute-start.16) | collective-permute-done | bytes 81952 | tf_op jit(solution)/shard_map/ppermute | solution.py:609
  65.5 1.9 %collective-permute-start.17 = (f32[2,160,128]{2,1,0:T(8,128)S(1)}, f32[2,160,128]{2,1,0:T(8,128)S(1)}, u32[]{:S(2)}, u32[]{:S(2)}) collective-permute-start(f32[2,160,128]{2,1,0:T(8,128)S(1)} %pad_maximum_fusion.own), channel_id=1, source_target_pairs={{2,1},{4,3},{6,5},{8,7},{10,9},{12,11},{14,13},{16,15},{18,17},{20... | collective-permute-start | bytes 491528 | tf_op jit(solution)/shard_map/ppermute | solution.py:611
  67.4 3.6 %collective-permute-start.15 = (f32[32,128]{1,0:T(8,128)S(1)}, f32[32,128]{1,0:T(8,128)S(1)}, u32[]{:S(2)}, u32[]{:S(2)}) collective-permute-start(f32[32,128]{1,0:T(8,128)S(1)} %get-tuple-element.61), channel_id=1, source_target_pairs={{6,1},{8,3},{10,5},{12,7},{14,9},{16,11},{18,13},{20,15},{22,17},{... | collective-permute-start | bytes 49160 | tf_op jit(solution)/shard_map/ppermute | solution.py:612
  71.1 1.0 %level.1 = f32[4,32,1024]{2,1,0:T(8,128)} custom-call(s32[6]{0:T(128)S(4)} %get-tuple-element.34.scalars, f32[1024,128]{1,0:T(8,128)S(1)} %get-tuple-element.57.v), custom_call_target="tpu_custom_call" | custom-call | tf_op jit(solution)/shard_map/level/pallas_call | solution.py:531
  72.1 1.7 %collective-permute-done.15.side = f32[32,128]{1,0:T(8,128)S(1)} collective-permute-done((f32[32,128]{1,0:T(8,128)S(1)}, f32[32,128]{1,0:T(8,128)S(1)}, u32[]{:S(2)}, u32[]{:S(2)}) %collective-permute-start.15) | collective-permute-done | bytes 16416 | tf_op jit(solution)/shard_map/ppermute | solution.py:612
  73.8 0.0 collective-permute-done.17.far
  73.8 8.4 %collective-permute-start.18 = (f32[2,160,128]{2,1,0:T(8,128)S(1)}, f32[2,160,128]{2,1,0:T(8,128)S(1)}, u32[]{:S(2)}, u32[]{:S(2)}) collective-permute-start(f32[2,160,128]{2,1,0:T(8,128)S(1)} %collective-permute-done.17.far), channel_id=1, source_target_pairs={{0,1},{1,0},{2,3},{3,2},{4,5},{5,4},{6,7},{7,6},{8,9},{9,8},{10,11... | collective-permute-start | bytes 491528 | tf_op jit(solution)/shard_map/ppermute | solution.py:621
  82.1 0.0 collective-permute-start.19
  82.1 1.2 %collective-permute-done.19.side_post = f32[32,128]{1,0:T(8,128)S(1)} collective-permute-done((f32[32,128]{1,0:T(8,128)S(1)}, f32[32,128]{1,0:T(8,128)S(1)}, u32[]{:S(2)}, u32[]{:S(2)}) %collective-permute-start.19) | collective-permute-done | bytes 16416 | tf_op jit(solution)/shard_map/ppermute | solution.py:622
  83.3 0.7 coarse.1
  (3 shorter events, 0.0 us)
Async XLA Ops:
  3.4 1.8 %collective-permute-start = (f32[12,32,128]{2,1,0:T(8,128)S(1)}, f32[12,32,128]{2,1,0:T(8,128)S(1)}, u32[]{:S(2)}, u32[]{:S(2)}) collective-permute-start(f32[12,32,128]{2,1,0:T(8,128)S(1)} %get-tuple-element.35.own), channel_id=1, source_target_pairs={{0,1},{1,0},{2,3},{3,2},{4,5},{5,4},{6,7},{7,6},{8,9},{9,8},{10,11... | collective-permute-start | bytes 589832 | tf_op jit(solution)/shard_map/ppermute | solution.py:576
  5.4 5.0 %collective-permute-start.2 = (f32[5,1024,128]{2,1,0:T(8,128)S(1)}, f32[5,1024,128]{2,1,0:T(8,128)S(1)}, u32[]{:S(2)}, u32[]{:S(2)}) collective-permute-start(f32[5,1024,128]{2,1,0:T(8,128)S(1)} %get-tuple-element.39.own), channel_id=1, source_target_pairs={{0,1},{1,0},{2,3},{3,2},{4,5},{5,4},{6,7},{7,6},{8,9},{9,8},{10,11... | collective-permute-start | bytes 7864328 | tf_op jit(solution)/shard_map/ppermute | solution.py:582
  5.9 12.3 %collective-permute-start.3 = (f32[12,32,128]{2,1,0:T(8,128)S(1)}, f32[12,32,128]{2,1,0:T(8,128)S(1)}, u32[]{:S(2)}, u32[]{:S(2)}) collective-permute-start(f32[12,32,128]{2,1,0:T(8,128)S(1)} %get-tuple-element.44.own), channel_id=1, source_target_pairs={{0,1},{1,0},{2,3},{3,2},{4,5},{5,4},{6,7},{7,6},{8,9},{9,8},{10,11... | collective-permute-start | bytes 589832 | tf_op jit(solution)/shard_map/ppermute | solution.py:581
  6.0 9.7 %collective-permute-start.1 = (f32[5,32,128]{2,1,0:T(8,128)S(1)}, f32[5,32,128]{2,1,0:T(8,128)S(1)}, u32[]{:S(2)}, u32[]{:S(2)}) collective-permute-start(f32[5,32,128]{2,1,0:T(8,128)S(1)} %get-tuple-element.38), channel_id=1, source_target_pairs={{1,2},{3,4},{5,6},{7,8},{9,10},{11,12},{13,14},{15,16},{17,18},{19... | collective-permute-start | bytes 245768 | tf_op jit(solution)/shard_map/ppermute | solution.py:580
  15.7 3.4 %collective-permute-start.4 = (f32[5,32,128]{2,1,0:T(8,128)S(1)}, f32[5,32,128]{2,1,0:T(8,128)S(1)}, u32[]{:S(2)}, u32[]{:S(2)}) collective-permute-start(f32[5,32,128]{2,1,0:T(8,128)S(1)} %collective-permute-done.1.far), channel_id=1, source_target_pairs={{0,1},{1,0},{2,3},{3,2},{4,5},{5,4},{6,7},{7,6},{8,9},{9,8},{10,11... | collective-permute-start | bytes 245768 | tf_op jit(solution)/shard_map/ppermute | solution.py:584
  21.4 11.9 %collective-permute-start.5 = (f32[4,32,128]{2,1,0:T(8,128)S(1)}, f32[4,32,128]{2,1,0:T(8,128)S(1)}, u32[]{:S(2)}, u32[]{:S(2)}) collective-permute-start(f32[4,32,128]{2,1,0:T(8,128)S(1)} %get-tuple-element.49.own), channel_id=1, source_target_pairs={{0,1},{1,0},{2,3},{3,2},{4,5},{5,4},{6,7},{7,6},{8,9},{9,8},{10,11... | collective-permute-start | bytes 196616 | tf_op jit(solution)/shard_map/ppermute | solution.py:551
  21.8 5.0 %collective-permute-start.6 = (f32[32,128]{1,0:T(8,128)S(1)}, f32[32,128]{1,0:T(8,128)S(1)}, u32[]{:S(2)}, u32[]{:S(2)}) collective-permute-start(f32[32,128]{1,0:T(8,128)S(1)} %get-tuple-element.50), channel_id=1, source_target_pairs={{1,2},{3,4},{5,6},{7,8},{9,10},{11,12},{13,14},{15,16},{17,18},{19... | collective-permute-start | bytes 49160 | tf_op jit(solution)/shard_map/ppermute | solution.py:550
  26.8 6.4 %collective-permute-start.7 = (f32[32,128]{1,0:T(8,128)S(1)}, f32[32,128]{1,0:T(8,128)S(1)}, u32[]{:S(2)}, u32[]{:S(2)}) collective-permute-start(f32[32,128]{1,0:T(8,128)S(1)} %collective-permute-done.6.far), channel_id=1, source_target_pairs={{0,1},{1,0},{2,3},{3,2},{4,5},{5,4},{6,7},{7,6},{8,9},{9,8},{10,11... | collective-permute-start | bytes 49160 | tf_op jit(solution)/shard_map/ppermute | solution.py:552
  34.6 11.9 %collective-permute-start.8 = (f32[4,32,128]{2,1,0:T(8,128)S(1)}, f32[4,32,128]{2,1,0:T(8,128)S(1)}, u32[]{:S(2)}, u32[]{:S(2)}) collective-permute-start(f32[4,32,128]{2,1,0:T(8,128)S(1)} %get-tuple-element.52.own), channel_id=1, source_target_pairs={{0,1},{1,0},{2,3},{3,2},{4,5},{5,4},{6,7},{7,6},{8,9},{9,8},{10,11... | collective-permute-start | bytes 196616 | tf_op jit(solution)/shard_map/ppermute | solution.py:551
  35.0 5.0 %collective-permute-start.9 = (f32[32,128]{1,0:T(8,128)S(1)}, f32[32,128]{1,0:T(8,128)S(1)}, u32[]{:S(2)}, u32[]{:S(2)}) collective-permute-start(f32[32,128]{1,0:T(8,128)S(1)} %get-tuple-element.53), channel_id=1, source_target_pairs={{1,2},{3,4},{5,6},{7,8},{9,10},{11,12},{13,14},{15,16},{17,18},{19... | collective-permute-start | bytes 49160 | tf_op jit(solution)/shard_map/ppermute | solution.py:550
  40.0 6.4 %collective-permute-start.10 = (f32[32,128]{1,0:T(8,128)S(1)}, f32[32,128]{1,0:T(8,128)S(1)}, u32[]{:S(2)}, u32[]{:S(2)}) collective-permute-start(f32[32,128]{1,0:T(8,128)S(1)} %collective-permute-done.9.far), channel_id=1, source_target_pairs={{0,1},{1,0},{2,3},{3,2},{4,5},{5,4},{6,7},{7,6},{8,9},{9,8},{10,11... | collective-permute-start | bytes 49160 | tf_op jit(solution)/shard_map/ppermute | solution.py:552
  47.8 11.9 %collective-permute-start.11 = (f32[4,32,128]{2,1,0:T(8,128)S(1)}, f32[4,32,128]{2,1,0:T(8,128)S(1)}, u32[]{:S(2)}, u32[]{:S(2)}) collective-permute-start(f32[4,32,128]{2,1,0:T(8,128)S(1)} %get-tuple-element.55.own), channel_id=1, source_target_pairs={{0,1},{1,0},{2,3},{3,2},{4,5},{5,4},{6,7},{7,6},{8,9},{9,8},{10,11... | collective-permute-start | bytes 196616 | tf_op jit(solution)/shard_map/ppermute | solution.py:551
  48.2 5.0 %collective-permute-start.12 = (f32[32,128]{1,0:T(8,128)S(1)}, f32[32,128]{1,0:T(8,128)S(1)}, u32[]{:S(2)}, u32[]{:S(2)}) collective-permute-start(f32[32,128]{1,0:T(8,128)S(1)} %get-tuple-element.56), channel_id=1, source_target_pairs={{1,2},{3,4},{5,6},{7,8},{9,10},{11,12},{13,14},{15,16},{17,18},{19... | collective-permute-start | bytes 49160 | tf_op jit(solution)/shard_map/ppermute | solution.py:550
  53.2 6.4 %collective-permute-start.13 = (f32[32,128]{1,0:T(8,128)S(1)}, f32[32,128]{1,0:T(8,128)S(1)}, u32[]{:S(2)}, u32[]{:S(2)}) collective-permute-start(f32[32,128]{1,0:T(8,128)S(1)} %collective-permute-done.12.far), channel_id=1, source_target_pairs={{0,1},{1,0},{2,3},{3,2},{4,5},{5,4},{6,7},{7,6},{8,9},{9,8},{10,11... | collective-permute-start | bytes 49160 | tf_op jit(solution)/shard_map/ppermute | solution.py:552
  61.0 1.3 %collective-permute-start.14 = (f32[4,32,128]{2,1,0:T(8,128)S(1)}, f32[4,32,128]{2,1,0:T(8,128)S(1)}, u32[]{:S(2)}, u32[]{:S(2)}) collective-permute-start(f32[4,32,128]{2,1,0:T(8,128)S(1)} %get-tuple-element.60.own), channel_id=1, source_target_pairs={{0,1},{1,0},{2,3},{3,2},{4,5},{5,4},{6,7},{7,6},{8,9},{9,8},{10,11... | collective-permute-start | bytes 196616 | tf_op jit(solution)/shard_map/ppermute | solution.py:604
  64.2 1.3 %collective-permute-start.16 = (f32[160,128]{1,0:T(8,128)S(1)}, f32[160,128]{1,0:T(8,128)S(1)}, u32[]{:S(2)}, u32[]{:S(2)}) collective-permute-start(f32[160,128]{1,0:T(8,128)S(1)} %get-tuple-element.62), channel_id=1, source_target_pairs={{0,1},{1,0},{2,3},{3,2},{4,5},{5,4},{6,7},{7,6},{8,9},{9,8},{10,11... | collective-permute-start | bytes 245768 | tf_op jit(solution)/shard_map/ppermute | solution.py:609
  65.5 8.3 %collective-permute-start.17 = (f32[2,160,128]{2,1,0:T(8,128)S(1)}, f32[2,160,128]{2,1,0:T(8,128)S(1)}, u32[]{:S(2)}, u32[]{:S(2)}) collective-permute-start(f32[2,160,128]{2,1,0:T(8,128)S(1)} %pad_maximum_fusion.own), channel_id=1, source_target_pairs={{2,1},{4,3},{6,5},{8,7},{10,9},{12,11},{14,13},{16,15},{18,17},{20... | collective-permute-start | bytes 491528 | tf_op jit(solution)/shard_map/ppermute | solution.py:611
  67.4 6.3 %collective-permute-start.15 = (f32[32,128]{1,0:T(8,128)S(1)}, f32[32,128]{1,0:T(8,128)S(1)}, u32[]{:S(2)}, u32[]{:S(2)}) collective-permute-start(f32[32,128]{1,0:T(8,128)S(1)} %get-tuple-element.61), channel_id=1, source_target_pairs={{6,1},{8,3},{10,5},{12,7},{14,9},{16,11},{18,13},{20,15},{22,17},{... | collective-permute-start | bytes 49160 | tf_op jit(solution)/shard_map/ppermute | solution.py:612
  73.8 9.5 %collective-permute-start.18 = (f32[2,160,128]{2,1,0:T(8,128)S(1)}, f32[2,160,128]{2,1,0:T(8,128)S(1)}, u32[]{:S(2)}, u32[]{:S(2)}) collective-permute-start(f32[2,160,128]{2,1,0:T(8,128)S(1)} %collective-permute-done.17.far), channel_id=1, source_target_pairs={{0,1},{1,0},{2,3},{3,2},{4,5},{5,4},{6,7},{7,6},{8,9},{9,8},{10,11... | collective-permute-start | bytes 491528 | tf_op jit(solution)/shard_map/ppermute | solution.py:621
  82.1 1.2 %collective-permute-start.19 = (f32[32,128]{1,0:T(8,128)S(1)}, f32[32,128]{1,0:T(8,128)S(1)}, u32[]{:S(2)}, u32[]{:S(2)}) collective-permute-start(f32[32,128]{1,0:T(8,128)S(1)} %collective-permute-done.15.side), channel_id=1, source_target_pairs={{0,1},{1,0},{2,3},{3,2},{4,5},{5,4},{6,7},{7,6},{8,9},{9,8},{10,11... | collective-permute-start | bytes 49160 | tf_op jit(solution)/shard_map/ppermute | solution.py:622

commit v3 on v2

--- a/solution.py
+++ b/solution.py
@@ -84,8 +84,8 @@
         target = (lane + turn) % 128
         index, index_post = (target + 32 * start) % 128, (target + 32 * start + lift) % 128
         here = jnp.where(target < 128 - 32 * start, 1, 0) == 1 - core
-        if post is None:
-            return lambda a, b: jnp.where(here, pick(a, index), 0.0)
+        if oth is None:
+            return lambda a, b: jnp.zeros((8, 128), F32)
         return lambda a, b: jnp.where(here, pick(a, index), pick(b, index_post))
 
     mix_z, mix_y, mix_x = mixer(0, 0), mixer(64, single), mixer(128 - x_turn, x_post)
@@ -103,15 +103,16 @@
             z_post = post[rows, :] if single else post[0, rows, :]
             nearest_post = z_post if single else post[1, rows, :]
             y_edge, x_edge = pick(nearest, y_index), pick(nearest, x_index)
-        mid = mix_z(oth[core, rows, :], z_post)
+        others = (None,) * 3 if oth is None else (oth[core, rows, :], oth[2, rows, :], oth[3, rows, :])
+        mid = mix_z(others[0], z_post)
         out[0, rows, :], out[1, rows, :] = jnp.where(low, z_edge, mid), jnp.where(low, mid, z_edge)
-        mid = mix_y(oth[2, rows, :], nearest_post)
+        mid = mix_y(others[1], nearest_post)
         inner = turned(own[2, rows, :], 64)
         below, above = jnp.where(low, y_edge, mid), jnp.where(low, mid, y_edge)
         out[2, rows, :] = jnp.where(
             iy == 1, jnp.where(lane < 64, below, inner), jnp.where(lane < 64, inner, above)
         )
-        mid = mix_x(oth[3, rows, :], nearest_post)
+        mid = mix_x(others[2], nearest_post)
         inner = pick(own[3, rows, :], own_index)
         below, above = jnp.where(low, x_edge, mid), jnp.where(low, mid, x_edge)
         out[3, rows, :] = jnp.where(
@@ -160,17 +161,15 @@
     return guess * (2.0 - x * guess)
 
 
-def collect_kernel(holder, v, f, k, c, kind, scalars, own, faces, bounds, hv, hf, hk, hc, hkind, sems):
+def collect_kernel(holder, v, k, kind, scalars, own, faces, bounds, hv, hk, hkind, sems):
     device = lax.axis_index(AXES)
     core = lax.rem(device, 2)
-    source = (v, f, k, c, kind)
-    landed = (hv, hf, hk, hc, hkind)
-    copies = [pltpu.make_async_copy(source[i], landed[i], sems.at[i]) for i in range(5)]
-    counting = pltpu.make_async_copy(holder, bounds, sems.at[5])
-    order = (0, 2, 4, 1, 3)
+    landed = (hv, hk, hkind)
+    copies = [pltpu.make_async_copy(ref, landed[i], sems.at[i]) for i, ref in enumerate((v, k, kind))]
+    counting = pltpu.make_async_copy(holder, bounds, sems.at[3])
     counting.start()
-    for i in order:
-        copies[i].start()
+    for copy in copies:
+        copy.start()
     counting.wait()
     count = []
     for bound in (0, 1, 2, 4, 6):
@@ -178,15 +177,25 @@
         scalars[len(count)] = count[-1]
     scalars[0] = core
     base = jnp.where(core == 0, count[0], count[1])
-    for i in order:
+    for i in range(3):
         copies[i].wait()
         for j in range(8):
             block = landed[i][:, pl.ds(128 * j, 128)].T
-            if i == 4:
+            if i == 2:
                 block = 1.0 - 0.5 * block.astype(F32)
             own[i, pl.ds(128 * j, 128), :] = block
-        if i in (0, 2, 4):
-            put_faces(base, own.at[i], faces.at[pl.ds(2 * i, 4)])
+        put_faces(base, own.at[i], faces.at[pl.ds(4 * i, 4)])
+
+
+def collect_rest_kernel(f, c, own, hf, hc, sems):
+    landed = (hf, hc)
+    copies = [pltpu.make_async_copy(ref, landed[i], sems.at[i]) for i, ref in enumerate((f, c))]
+    for copy in copies:
+        copy.start()
+    for i in range(2):
+        copies[i].wait()
+        for j in range(8):
+            own[i, pl.ds(128 * j, 128), :] = landed[i][:, pl.ds(128 * j, 128)].T
 
 
 def window_of(scalars):
@@ -230,14 +239,15 @@
         sent[part(t), :] = jnp.where(mine, z, nearest)
 
 
-def window_kernel(scalars, own, oth, window, inner):
+def window_kernel(scalars, own, oth, own_rest, oth_rest, window, inner):
     windowed = window_of(scalars)
     for i in range(5):
+        mine, theirs = (own.at[i], oth.at[i]) if i < 3 else (own_rest.at[i - 3], oth_rest.at[i - 3])
 
         def rows(y, carry):
             for t in range(TILES):
                 at = tile_row(y, t)
-                window[i, at, :] = windowed(own[i, at, :], oth[i, at, :])
+                window[i, at, :] = windowed(mine[at, :], theirs[at, :])
             return carry
 
         lax.fori_loop(0, SPAN, rows, 0, unroll=8)
@@ -246,8 +256,8 @@
 
     def layer(y, carry):
         above = jnp.minimum(y + 1, SPAN - 1)
-        heat = [window[2, tile_row(y, t), :] for t in range(TILES)]
-        open_heat = [heat[t] * window[4, tile_row(y, t), :] for t in range(TILES)]
+        heat = [window[1, tile_row(y, t), :] for t in range(TILES)]
+        open_heat = [heat[t] * window[2, tile_row(y, t), :] for t in range(TILES)]
         heat_up = [pltpu.roll(x, 7, axis=0) for x in heat]
         open_up = [pltpu.roll(x, 7, axis=0) for x in open_heat]
         below = None
@@ -257,8 +267,8 @@
             beside = doubled * turned(open_heat[t], 127) * inverted(heat[t] + turned(heat[t], 127))
             inner[0, at, :] = turned(beside, 1)
             inner[1, at, :] = beside
-            heat2 = window[2, tile_row(above, t), :]
-            inner[2, at, :] = doubled * window[4, tile_row(above, t), :] * heat2 * inverted(heat[t] + heat2)
+            heat2 = window[1, tile_row(above, t), :]
+            inner[2, at, :] = doubled * window[2, tile_row(above, t), :] * heat2 * inverted(heat[t] + heat2)
             heat2, open2 = heat_up[t], open_up[t]
             if t < TILES - 1:
                 heat2 = jnp.where(row == 7, heat_up[t + 1], heat2)
@@ -270,13 +280,13 @@
             below = lifted
         return carry
 
-    lax.fori_loop(0, SPAN, layer, 0, unroll=2)
+    lax.fori_loop(0, SPAN, layer, 0, unroll=4)
 
 
 def first_kernel(
     layers, scalars, fields, inner, own, oth, far, post, vo, fo, do, go, edge, faces, sent, ghost, pv, ends
 ):
-    v, f, k, c, a = (fields.at[i] for i in range(5))
+    v, k, a, f, c = (fields.at[i] for i in range(5))
     where = whereabouts(scalars)
     base = where[1]
     ix, iy, iz = positions(base)
@@ -371,10 +381,10 @@
         put_sent(scalars, shade_now, faces, sent[0])
 
 
-def residual_kernel(scalars, v, f, g, d, edge, own, oth, blocks, cross, ghost, padded, pair):
+def residual_kernel(scalars, v, f, g, d, edge, own, blocks, cross, ghost, padded, pair):
     where = whereabouts(scalars)
     core = where[0]
-    ghosts(where, own, oth, None, None, ghost)
+    ghosts(where, own, None, None, None, ghost)
     pad(where[1], v, ghost, padded)
     lane = lanes()
     index = 2 * (lane % 64)
@@ -412,11 +422,11 @@
             result.append(pick(both, index) * 0.125)
         return result
 
-    for t, tile in enumerate(pooled(core)):
-        cross[part(t), :] = tile
-    for t, (along_y, along_x) in enumerate(zip(pooled(2), pooled(3))):
-        cross[part(2 + t), :] = jnp.where(lane < 64, along_y, along_x)
-    blocks[128:160, :] = cross[...]
+    for t, (z_low, z_high, along_y, along_x) in enumerate(zip(*(pooled(face) for face in range(4)))):
+        blocks[128 + 8 * t : 136 + 8 * t, :] = z_low
+        blocks[144 + 8 * t : 152 + 8 * t, :] = z_high
+        blocks[160 + 8 * t : 168 + 8 * t, :] = jnp.where(lane < 64, along_y, along_x)
+        cross[part(t), :] = jnp.where(core == 0, z_low, z_high)
 
 
 def level_kernel(scalars, v, level, stack):
@@ -462,18 +472,33 @@
             table[2, rows, :] = jnp.where(low, post[0, rows, :], far[0, rows, :])
             table[3, rows, :] = jnp.where(low, post[1, rows, :], far[1, rows, :])
             table[4, rows, :] = jnp.where(low, far[1, rows, :], post[1, rows, :])
-        for t in range(4):
+        for t in range(6):
             rows, last = part(t), part(16 + t)
-            crossing[0, rows, :] = jnp.where(low, side[rows, :], side_post[rows, :])
-            crossing[1, rows, :] = jnp.where(low, own[1, last, :], own[0, last, :])
-            crossing[2, rows, :] = jnp.where(low, post[1, last, :], far[1, last, :])
-            crossing[3, rows, :] = jnp.where(low, post[0, last, :], far[0, last, :])
-            crossing[4, rows, :] = jnp.where(low, far[1, last, :], post[1, last, :])
-            crossing[5, rows, :] = jnp.where(low, side_post[rows, :], side[rows, :])
-
-        def added(entry, rows, index, valid):
-            tile = pick(crossing[jnp.clip(entry, 0, 5), rows, :], jnp.clip(index, 0, 127))
-            return jnp.where(valid, tile, 0.0)
+            crossing[2, rows, :] = jnp.where(low, own[0, last, :], own[1, last, :])
+            crossing[3, rows, :] = jnp.where(low, own[1, last, :], own[0, last, :])
+            crossing[4, rows, :] = jnp.where(low, post[0, last, :], far[0, last, :])
+            crossing[5, rows, :] = jnp.where(low, post[1, last, :], far[1, last, :])
+            crossing[6, rows, :] = jnp.where(low, far[1, last, :], post[1, last, :])
+            crossing[7, rows, :] = jnp.where(low, far[0, last, :], post[0, last, :])
+        for t in range(2):
+            rows = part(t)
+            crossing[1, part(2 + t), :] = jnp.where(low, side[rows, :], side_post[rows, :])
+            crossing[8, rows, :] = jnp.where(low, side_post[rows, :], side[rows, :])
+
+        def giver(chip, j, count, step):
+            q = j + step
+            in_first = j < 4
+            begin = jnp.where(in_first, 0, count - 4)
+            valid = (q < begin) | (q >= begin + 4)
+            entry = 2 * chip + jnp.where(q < 0, 1, jnp.where(q >= count, 4, jnp.where(in_first, 3, 2)))
+            slot = jnp.where(
+                q < 0, q + 4, jnp.where(q >= count, q - count, jnp.where(in_first, q - count + 4, q))
+            )
+            return valid, jnp.clip(entry, 1, 8), slot
+
+        def added(source, rows, index):
+            valid, entry, slot = source
+            return jnp.where(valid, pick(crossing[entry, rows, :], (index + 16 * slot) % 128), 0.0)
 
         for iy in range(2):
             for iz in range(2):
@@ -489,33 +514,28 @@
                         b = pick(table[right_block, rows, :], index + 16 * right_slot)
                         joined[pl.ds(SPAN * (16 * iy + y) + 16 * iz + 8 * t, 8), :] = jnp.where(lane < 16, a, b)
 
-                def pair_of(below, shift, rows):
-                    tiles = []
-                    for chip, j, count in (left, right):
-                        place = j if below else j - count + 4 - shift
-                        valid = (place < 4 - shift) if below else (place >= 0)
-                        entry = chip if below else 3 + chip
-                        slot = place + shift if below else place
-                        tiles.append(added(entry, rows, 16 * slot + lane % 16, valid))
+                def pair_of(step, rows):
+                    tiles = [added(giver(*one, step), rows, lane % 16) for one in (left, right)]
                     return jnp.where(lane < 16, tiles[0], tiles[1])
 
                 first_row = SPAN * 16 * iy + 16 * iz
                 for t in range(2):
                     at = pl.ds(first_row + 8 * SPAN * t, 8, stride=SPAN)
-                    joined[at, :] = joined[at, :] + pair_of(True, 0, part(t))
+                    joined[at, :] = joined[at, :] + pair_of(-4, part(2 + t))
                     at = pl.ds(first_row + 8 * SPAN * t + 15, 8, stride=SPAN)
-                    joined[at, :] = joined[at, :] + pair_of(False, 0, part(t))
+                    joined[at, :] = joined[at, :] + pair_of(4, part(t))
                     at = pl.ds(first_row + (0 if iy else 15 * SPAN) + 8 * t, 8)
-                    joined[at, :] = joined[at, :] + pair_of(iy == 1, 2, part(2 + t))
-
-                @pl.when(left[0] != right[0])
+                    joined[at, :] = joined[at, :] + pair_of(-2 if iy else 2, part(4 + t))
+                from_right, from_left = giver(*left, 1), giver(*right, -1)
+
+                @pl.when(from_right[0] | from_left[0])
                 def _():
                     for y in range(16):
                         for t in range(2):
                             at = pl.ds(first_row + SPAN * y + 8 * t, 8)
-                            from_right = added(3 + left[0], part(2 + t), 0 * lane + 64 + y, True)
-                            from_left = added(right[0], part(2 + t), 0 * lane + 112 + y, True)
-                            side_tile = jnp.where(lane == 15, from_right, jnp.where(lane == 16, from_left, 0.0))
+                            high = added(from_right, part(4 + t), 0 * lane + 64 + y)
+                            low_side = added(from_left, part(4 + t), 0 * lane + 64 + y)
+                            side_tile = jnp.where(lane == 15, high, jnp.where(lane == 16, low_side, 0.0))
                             joined[at, :] = joined[at, :] + side_tile
 
         for j in range(8):
@@ -552,34 +572,51 @@
         post = lax.ppermute(far, AXES, swap)
         return faces, oth, far, post
 
-    fields = [x.reshape(SLOTS * SPAN, LAYER) for x in (v, f, k, c, kind)]
+    v, f, k, c, kind = (x.reshape(SLOTS * SPAN, LAYER) for x in (v, f, k, c, kind))
     five = jax.ShapeDtypeStruct((5, LAYER, 128), F32)
     twelve = jax.ShapeDtypeStruct((12, SPAN, 128), F32)
     sent_first = jax.ShapeDtypeStruct((5, SPAN, 128), F32)
     sent_later = jax.ShapeDtypeStruct((SPAN, 128), F32)
+    landing = pltpu.VMEM((SLOTS * SPAN, LAYER), F32)
     scalars, own, faces = call(
         collect_kernel,
-        [pltpu.SMEM((6,), jnp.int32), pltpu.VMEM(five.shape, F32), pltpu.VMEM(twelve.shape, F32)],
-        [holder.reshape(patches // 128, 128), *fields],
-        specs=[HBM] * 6,
+        [pltpu.SMEM((6,), jnp.int32), pltpu.VMEM((3, LAYER, 128), F32), pltpu.VMEM(twelve.shape, F32)],
+        [holder.reshape(patches // 128, 128), v, k, kind],
+        specs=[HBM] * 4,
         leading=[],
         out_specs=[SMEM, VMEM, VMEM],
-        scratch=[pltpu.VMEM((patches // 128, 128), jnp.int32)]
-        + [pltpu.VMEM(x.shape, x.dtype) for x in fields]
-        + [pltpu.SemaphoreType.DMA((6,))],
+        scratch=[pltpu.VMEM((patches // 128, 128), jnp.int32), landing, landing]
+        + [pltpu.VMEM((SLOTS * SPAN, LAYER), jnp.int32), pltpu.SemaphoreType.DMA((4,))],
         name="collect",
         limit=COLLECT_LIMIT,
     )
+    own_rest = call(
+        collect_rest_kernel,
+        pltpu.VMEM((2, LAYER, 128), F32),
+        [f, c],
+        specs=[HBM] * 2,
+        leading=[],
+        out_specs=VMEM,
+        scratch=[landing, landing, pltpu.SemaphoreType.DMA((2,))],
+        name="collect_rest",
+        limit=COLLECT_LIMIT,
+    )
+    oth, own_rest = lax.optimization_barrier((lax.ppermute(faces, AXES, swap), own_rest))
     faces, sent = call(
         face_window_kernel,
         [twelve, sent_first],
-        [scalars, faces, lax.ppermute(faces, AXES, swap)],
+        [scalars, faces, oth],
         name="face_window",
     )
-    sent, own = lax.optimization_barrier((sent, own))
+    sent, own, own_rest = lax.optimization_barrier((sent, own, own_rest))
     far = lax.ppermute(sent, AXES, reach)
     oth = lax.ppermute(faces, AXES, swap)
-    window, inner = call(window_kernel, [five, five], [scalars, own, lax.ppermute(own, AXES, swap)], name="window")
+    window, inner = call(
+        window_kernel,
+        [five, five],
+        [scalars, own, lax.ppermute(own, AXES, swap), own_rest, lax.ppermute(own_rest, AXES, swap)],
+        name="window",
+    )
     far, window, inner = lax.optimization_barrier((far, window, inner))
     post = lax.ppermute(far, AXES, swap)
     coefficients = jax.ShapeDtypeStruct((6, LAYER, 128), F32)
@@ -600,8 +637,8 @@
         )
     blocks, cross = call(
         residual_kernel,
-        [jax.ShapeDtypeStruct((160, 128), F32), jax.ShapeDtypeStruct((SPAN, 128), F32)],
-        [scalars, wv, wf, wg, wd, edge, faces, lax.ppermute(faces, AXES, swap)],
+        [jax.ShapeDtypeStruct((176, 128), F32), jax.ShapeDtypeStruct((16, 128), F32)],
+        [scalars, wv, wf, wg, wd, edge, faces],
         scratch=[GHOSTS, PADDED, pltpu.VMEM((2, SPAN, 128), F32)],
         name="residual",
     )
@@ -610,6 +647,7 @@
     downward = [(i, i - 1) for i in range(2, devices, 2)] + [(i, i - 5) for i in range(5, devices, 2)]
     far = lax.ppermute(both, AXES, downward)
     side = lax.ppermute(cross, AXES, beside)
+    far, wv = lax.optimization_barrier((far, wv))
     level = call(
         level_kernel,
         jax.ShapeDtypeStruct((SLOTS, SPAN, LAYER), F32),
@@ -617,14 +655,15 @@
         scratch=[pltpu.VMEM((128, LAYER), F32)],
         name="level",
     )
-    side, far, level = lax.optimization_barrier((side, far, level))
+    side, level = lax.optimization_barrier((side, level))
+    side, far = lax.optimization_barrier((side, far))
     post = lax.ppermute(far, AXES, swap)
     side_post = lax.ppermute(side, AXES, swap)
     grid = call(
         coarse_kernel,
         jax.ShapeDtypeStruct((1, SPAN, LAYER), F32),
         [scalars, both, far, post, side, side_post],
-        scratch=[pltpu.VMEM((5, 128, 128), F32), pltpu.VMEM((6, SPAN, 128), F32), pltpu.VMEM((LAYER, 128), F32)],
+        scratch=[pltpu.VMEM((5, 128, 128), F32), pltpu.VMEM((9, 48, 128), F32), pltpu.VMEM((LAYER, 128), F32)],
         name="coarse",
     )
     return level, grid

time: 85.5 us -> 83.8 us (0.980)
  waiting for transfers between devices: 19.6 us -> 18.6 us
    ppermute x1, waiting for transfers between devices: 0.01 us -> 2.78 us  [shards(): far = lax.ppermute(both, AXES, downward)]
    ppermute x2 -> x1, waiting for transfers between devices: 1.98 us -> 0.01 us  [shards(): lax.ppermute(faces, AXES, swap)]
    ppermute x1, waiting for transfers between devices: 1.66 us -> 0.01 us  [shards(): side = lax.ppermute(cross, AXES, beside)]
    ppermute x1, waiting for transfers between devices: 1.03 us -> 0.01 us  [shards(): lax.ppermute(own, AXES, swap)]
    ppermute x0 -> x1, waiting for transfers between devices: none -> 0.89 us  [shards(): lax.ppermute(own_rest, AXES, swap)]
    pallas_call x10 -> x11, Pallas kernels: 18.1 us -> 18 us  [call(): pl.pallas_call(kernel, out_shape=out_shape, in_specs=list(leading) + (spe...]
  transfers between devices with their start and end apart: 20 -> 20, of which waited for: 13 -> 11; matrix products, arithmetic and copies ran while one was open for 0% -> 0% of each run, Pallas kernels for 8% -> 8%
where the time goes in v3:
time: 83.8 us; the launch traced here: 82.7 us
  starting transfers between devices  45.3 us (54%)
  waiting for transfers between devices  18.6 us (22%)
  Pallas kernels  18 us (21%)
    pallas_call x11, Pallas kernels, call(): pl.pallas_call(kernel, out_shape=out_shape, in_specs=list(leading) + (spe...  18 us
    ppermute x3, starting transfers between devices, exchange(): post = lax.ppermute(far, AXES, swap)  16.8 us
    ppermute x2, starting transfers between devices, shards(): post = lax.ppermute(far, AXES, swap)  10.8 us
    ppermute x3, waiting for transfers between devices, exchange(): far = lax.ppermute(sent, AXES, reach)  9.39 us
    ppermute x3, starting transfers between devices, exchange(): far = lax.ppermute(sent, AXES, reach)  5.73 us
    ppermute x1, starting transfers between devices, shards(): side = lax.ppermute(cross, AXES, beside)  3.64 us
    ppermute x1, starting transfers between devices, shards(): far = lax.ppermute(sent, AXES, reach)  3.4 us
    ppermute x1, waiting for transfers between devices, shards(): far = lax.ppermute(both, AXES, downward)  2.78 us
  transfers between devices with their start and end apart: 20, of which 11 were waited for; matrix products, arithmetic and copies ran while one was open for 0% of the time, Pallas kernels for 8%

profile of v3, /device:TPU:129, one launch (start us, length us, event | category | flops | bytes accessed | tf_op | source)
XLA Modules:
  0.0 82.7 jit_solution(17169227022740334509)
XLA Ops:
  0.6 2.3 %collect.1 = (s32[6]{0:T(128)S(4)}, f32[3,1024,128]{2,1,0:T(8,128)S(1)}, f32[12,32,128]{2,1,0:T(8,128)S(1)}) custom-call(s32[6,128]{1,0:T(8,128)} %bitcast.15, f32[128,1024]{1,0:T(8,128)} %bitcast.9, f32[128,1024]{1,0:T(8,128)} %bitcast.10, s32[128,1024]{1,0:T(8,128)} %bitcast.11), custom_call_target="tpu_custom_call" | custom-call | tf_op jit(solution)/shard_map/collect/pallas_call | solution.py:551
  2.9 0.8 collective-permute-start
  3.7 1.5 %collect_rest.1.own_rest = f32[2,1024,128]{2,1,0:T(8,128)S(1)} custom-call(f32[128,1024]{1,0:T(8,128)} %bitcast.12, f32[128,1024]{1,0:T(8,128)} %bitcast.13), custom_call_target="tpu_custom_call" | custom-call | tf_op jit(solution)/shard_map/collect_rest/pallas_call | solution.py:551
  5.2 0.0 collective-permute-done.oth
  5.2 0.3 face_window.1
  5.4 0.1 collective-permute-start.2
  5.5 0.5 collective-permute-start.3
  6.0 0.1 collective-permute-start.4
  6.1 3.4 %collective-permute-start.1 = (f32[5,32,128]{2,1,0:T(8,128)S(1)}, f32[5,32,128]{2,1,0:T(8,128)S(1)}, u32[]{:S(2)}, u32[]{:S(2)}) collective-permute-start(f32[5,32,128]{2,1,0:T(8,128)S(1)} %get-tuple-element.46), channel_id=1, source_target_pairs={{1,2},{3,4},{5,6},{7,8},{9,10},{11,12},{13,14},{15,16},{17,18},{19... | collective-permute-start | bytes 245768 | tf_op jit(solution)/shard_map/ppermute | solution.py:612
  9.5 0.9 %collective-permute-done.3.oth_rest = f32[2,1024,128]{2,1,0:T(8,128)S(1)} collective-permute-done((f32[2,1024,128]{2,1,0:T(8,128)S(1)}, f32[2,1024,128]{2,1,0:T(8,128)S(1)}, u32[]{:S(2)}, u32[]{:S(2)}) %collective-permute-start.3) | collective-permute-done | bytes 1048608 | tf_op jit(solution)/shard_map/ppermute | solution.py:617
  10.4 4.2 %window.1 = (f32[5,1024,128]{2,1,0:T(8,128)S(1)}, f32[5,1024,128]{2,1,0:T(8,128)S(1)}) custom-call(s32[6]{0:T(128)S(4)} %get-tuple-element.40.scalars, f32[3,1024,128]{2,1,0:T(8,128)S(1)} %get-tuple-element.47.own, f32[3,1024,128]{2,1,0:T(8,128)S(1)} %collective-permute-done.2.oth, f32[2,1024,128]{2,1,0:T(8,128)S(1)} %collect_rest.1.own_rest, ...), custom_call_target="tpu_custom_call" | custom-call | tf_op jit(solution)/shard_map/window/pallas_call | solution.py:551
  14.6 0.0 collective-permute-done.1.far
  14.6 3.1 %collective-permute-start.5 = (f32[5,32,128]{2,1,0:T(8,128)S(1)}, f32[5,32,128]{2,1,0:T(8,128)S(1)}, u32[]{:S(2)}, u32[]{:S(2)}) collective-permute-start(f32[5,32,128]{2,1,0:T(8,128)S(1)} %collective-permute-done.1.far), channel_id=1, source_target_pairs={{0,1},{1,0},{2,3},{3,2},{4,5},{5,4},{6,7},{7,6},{8,9},{9,8},{10,11... | collective-permute-start | bytes 245768 | tf_op jit(solution)/shard_map/ppermute | solution.py:621
  17.7 0.0 collective-permute-done.4.oth
  17.7 0.9 %collective-permute-done.5.post = f32[5,32,128]{2,1,0:T(8,128)S(1)} collective-permute-done((f32[5,32,128]{2,1,0:T(8,128)S(1)}, f32[5,32,128]{2,1,0:T(8,128)S(1)}, u32[]{:S(2)}, u32[]{:S(2)}) %collective-permute-start.5) | collective-permute-done | bytes 81952 | tf_op jit(solution)/shard_map/ppermute | solution.py:621
  18.6 2.3 %first.1 = (f32[1024,128]{1,0:T(8,128)S(1)}, f32[1024,128]{1,0:T(8,128)S(1)}, f32[1024,128]{1,0:T(8,128)S(1)}, f32[6,1024,128]{2,1,0:T(8,128)S(1)}, f32[4,32,128...) custom-call(s32[6]{0:T(128)S(4)} %get-tuple-element.40.scalars, ...), custom_call_target="tpu_custom_call" | custom-call | tf_op jit(solution)/shard_map/first/pallas_call | solution.py:551
  20.9 0.4 collective-permute-start.6
  21.3 1.9 %collective-permute-start.7 = (f32[32,128]{1,0:T(8,128)S(1)}, f32[32,128]{1,0:T(8,128)S(1)}, u32[]{:S(2)}, u32[]{:S(2)}) collective-permute-start(f32[32,128]{1,0:T(8,128)S(1)} %get-tuple-element.59), channel_id=1, source_target_pairs={{1,2},{3,4},{5,6},{7,8},{9,10},{11,12},{13,14},{15,16},{17,18},{19... | collective-permute-start | bytes 49160 | tf_op jit(solution)/shard_map/ppermute | solution.py:570
  23.2 3.1 %collective-permute-done.7.far = f32[32,128]{1,0:T(8,128)S(1)} collective-permute-done((f32[32,128]{1,0:T(8,128)S(1)}, f32[32,128]{1,0:T(8,128)S(1)}, u32[]{:S(2)}, u32[]{:S(2)}) %collective-permute-start.7) | collective-permute-done | bytes 16416 | tf_op jit(solution)/shard_map/ppermute | solution.py:570
  26.3 5.6 %collective-permute-start.8 = (f32[32,128]{1,0:T(8,128)S(1)}, f32[32,128]{1,0:T(8,128)S(1)}, u32[]{:S(2)}, u32[]{:S(2)}) collective-permute-start(f32[32,128]{1,0:T(8,128)S(1)} %collective-permute-done.7.far), channel_id=1, source_target_pairs={{0,1},{1,0},{2,3},{3,2},{4,5},{5,4},{6,7},{7,6},{8,9},{9,8},{10,11... | collective-permute-start | bytes 49160 | tf_op jit(solution)/shard_map/ppermute | solution.py:572
  31.9 0.8 %collective-permute-done.8.post = f32[32,128]{1,0:T(8,128)S(1)} collective-permute-done((f32[32,128]{1,0:T(8,128)S(1)}, f32[32,128]{1,0:T(8,128)S(1)}, u32[]{:S(2)}, u32[]{:S(2)}) %collective-permute-start.8) | collective-permute-done | bytes 16416 | tf_op jit(solution)/shard_map/ppermute | solution.py:572
  32.8 0.0 collective-permute-done.6.oth
  32.8 1.4 %sweep.3 = (f32[1024,128]{1,0:T(8,128)S(1)}, f32[4,32,128]{2,1,0:T(8,128)S(1)}, f32[32,128]{1,0:T(8,128)S(1)}) custom-call(s32[6]{0:T(128)S(4)} %get-tuple-element.40.scalars, f32[1024,128]{1,0:T(8,128)S(1)} %get-tuple-element.55.v, f32[1024,128]{1,0:T(8,128)S(1)} %get-tuple-element.56.f, f32[6,1024,128]{2,1,0:T(8,128)S(1)} %get-tuple-element.57.g, ...), custom_call_target="tpu_custom_call" | custom-call | tf_op jit(solution)/shard_map/sweep/pallas_call | solution.py:551
  34.1 0.4 collective-permute-start.9
  34.5 1.9 %collective-permute-start.10 = (f32[32,128]{1,0:T(8,128)S(1)}, f32[32,128]{1,0:T(8,128)S(1)}, u32[]{:S(2)}, u32[]{:S(2)}) collective-permute-start(f32[32,128]{1,0:T(8,128)S(1)} %get-tuple-element.62), channel_id=1, source_target_pairs={{1,2},{3,4},{5,6},{7,8},{9,10},{11,12},{13,14},{15,16},{17,18},{19... | collective-permute-start | bytes 49160 | tf_op jit(solution)/shard_map/ppermute | solution.py:570
  36.4 3.1 %collective-permute-done.10.far = f32[32,128]{1,0:T(8,128)S(1)} collective-permute-done((f32[32,128]{1,0:T(8,128)S(1)}, f32[32,128]{1,0:T(8,128)S(1)}, u32[]{:S(2)}, u32[]{:S(2)}) %collective-permute-start.10) | collective-permute-done | bytes 16416 | tf_op jit(solution)/shard_map/ppermute | solution.py:570
  39.5 5.6 %collective-permute-start.11 = (f32[32,128]{1,0:T(8,128)S(1)}, f32[32,128]{1,0:T(8,128)S(1)}, u32[]{:S(2)}, u32[]{:S(2)}) collective-permute-start(f32[32,128]{1,0:T(8,128)S(1)} %collective-permute-done.10.far), channel_id=1, source_target_pairs={{0,1},{1,0},{2,3},{3,2},{4,5},{5,4},{6,7},{7,6},{8,9},{9,8},{10,11... | collective-permute-start | bytes 49160 | tf_op jit(solution)/shard_map/ppermute | solution.py:572
  45.1 0.8 %collective-permute-done.11.post = f32[32,128]{1,0:T(8,128)S(1)} collective-permute-done((f32[32,128]{1,0:T(8,128)S(1)}, f32[32,128]{1,0:T(8,128)S(1)}, u32[]{:S(2)}, u32[]{:S(2)}) %collective-permute-start.11) | collective-permute-done | bytes 16416 | tf_op jit(solution)/shard_map/ppermute | solution.py:572
  46.0 0.0 collective-permute-done.9.oth
  46.0 1.4 %sweep.4 = (f32[1024,128]{1,0:T(8,128)S(1)}, f32[4,32,128]{2,1,0:T(8,128)S(1)}, f32[32,128]{1,0:T(8,128)S(1)}) custom-call(s32[6]{0:T(128)S(4)} %get-tuple-element.40.scalars, f32[1024,128]{1,0:T(8,128)S(1)} %get-tuple-element.60.v, f32[1024,128]{1,0:T(8,128)S(1)} %get-tuple-element.56.f, f32[6,1024,128]{2,1,0:T(8,128)S(1)} %get-tuple-element.57.g, ...), custom_call_target="tpu_custom_call" | custom-call | tf_op jit(solution)/shard_map/sweep/pallas_call | solution.py:551
  47.3 0.4 collective-permute-start.12
  47.7 1.9 %collective-permute-start.13 = (f32[32,128]{1,0:T(8,128)S(1)}, f32[32,128]{1,0:T(8,128)S(1)}, u32[]{:S(2)}, u32[]{:S(2)}) collective-permute-start(f32[32,128]{1,0:T(8,128)S(1)} %get-tuple-element.65), channel_id=1, source_target_pairs={{1,2},{3,4},{5,6},{7,8},{9,10},{11,12},{13,14},{15,16},{17,18},{19... | collective-permute-start | bytes 49160 | tf_op jit(solution)/shard_map/ppermute | solution.py:570
  49.6 3.1 %collective-permute-done.13.far = f32[32,128]{1,0:T(8,128)S(1)} collective-permute-done((f32[32,128]{1,0:T(8,128)S(1)}, f32[32,128]{1,0:T(8,128)S(1)}, u32[]{:S(2)}, u32[]{:S(2)}) %collective-permute-start.13) | collective-permute-done | bytes 16416 | tf_op jit(solution)/shard_map/ppermute | solution.py:570
  52.7 5.6 %collective-permute-start.14 = (f32[32,128]{1,0:T(8,128)S(1)}, f32[32,128]{1,0:T(8,128)S(1)}, u32[]{:S(2)}, u32[]{:S(2)}) collective-permute-start(f32[32,128]{1,0:T(8,128)S(1)} %collective-permute-done.13.far), channel_id=1, source_target_pairs={{0,1},{1,0},{2,3},{3,2},{4,5},{5,4},{6,7},{7,6},{8,9},{9,8},{10,11... | collective-permute-start | bytes 49160 | tf_op jit(solution)/shard_map/ppermute | solution.py:572
  58.3 0.8 %collective-permute-done.14.post = f32[32,128]{1,0:T(8,128)S(1)} collective-permute-done((f32[32,128]{1,0:T(8,128)S(1)}, f32[32,128]{1,0:T(8,128)S(1)}, u32[]{:S(2)}, u32[]{:S(2)}) %collective-permute-start.14) | collective-permute-done | bytes 16416 | tf_op jit(solution)/shard_map/ppermute | solution.py:572
  59.2 1.3 %sweep.5 = (f32[1024,128]{1,0:T(8,128)S(1)}, f32[4,32,128]{2,1,0:T(8,128)S(1)}) custom-call(s32[6]{0:T(128)S(4)} %get-tuple-element.40.scalars, f32[1024,128]{1,0:T(8,128)S(1)} %get-tuple-element.63.v, f32[1024,128]{1,0:T(8,128)S(1)} %get-tuple-element.56.f, f32[6,1024,128]{2,1,0:T(8,128)S(1)} %get-tuple-element.57.g, ...), custom_call_target="tpu_custom_call" | custom-call | tf_op jit(solution)/shard_map/sweep/pallas_call | solution.py:551
  60.5 1.8 %residual.1 = (f32[176,128]{1,0:T(8,128)S(1)}, f32[16,128]{1,0:T(8,128)S(1)}) custom-call(s32[6]{0:T(128)S(4)} %get-tuple-element.40.scalars, f32[1024,128]{1,0:T(8,128)S(1)} %get-tuple-element.72.v, f32[1024,128]{1,0:T(8,128)S(1)} %get-tuple-element.56.f, f32[6,1024,128]{2,1,0:T(8,128)S(1)} %get-tuple-element.57.g, f32[1024,128]{1,0:T(8,128)S(1)} %get-tuple-element.67.d, ...), custom_call_target="tpu_custom_call" | custom-call | tf_op jit(solution)/shard_map/residual/pallas_call | solution.py:551
  62.3 0.4 collective-permute-start.16
  62.7 0.9 %collective-permute-done.16 = f32[176,128]{1,0:T(8,128)S(1)} collective-permute-done((f32[176,128]{1,0:T(8,128)S(1)}, f32[176,128]{1,0:T(8,128)S(1)}, u32[]{:S(2)}, u32[]{:S(2)}) %collective-permute-start.16) | collective-permute-done | bytes 90144 | tf_op jit(solution)/shard_map/ppermute | solution.py:646
  63.7 1.9 %collective-permute-start.17 = (f32[2,176,128]{2,1,0:T(8,128)S(1)}, f32[2,176,128]{2,1,0:T(8,128)S(1)}, u32[]{:S(2)}, u32[]{:S(2)}) collective-permute-start(f32[2,176,128]{2,1,0:T(8,128)S(1)} %pad_maximum_fusion.own), channel_id=1, source_target_pairs={{2,1},{4,3},{6,5},{8,7},{10,9},{12,11},{14,13},{16,15},{18,17},{20... | collective-permute-start | bytes 540680 | tf_op jit(solution)/shard_map/ppermute | solution.py:648
  65.6 3.6 %collective-permute-start.15 = (f32[16,128]{1,0:T(8,128)S(1)}, f32[16,128]{1,0:T(8,128)S(1)}, u32[]{:S(2)}, u32[]{:S(2)}) collective-permute-start(f32[16,128]{1,0:T(8,128)S(1)} %get-tuple-element.70), channel_id=1, source_target_pairs={{6,1},{8,3},{10,5},{12,7},{14,9},{16,11},{18,13},{20,15},{22,17},{... | collective-permute-start | bytes 24584 | tf_op jit(solution)/shard_map/ppermute | solution.py:649
  69.3 2.8 %collective-permute-done.17.far = f32[2,176,128]{2,1,0:T(8,128)S(1)} collective-permute-done((f32[2,176,128]{2,1,0:T(8,128)S(1)}, f32[2,176,128]{2,1,0:T(8,128)S(1)}, u32[]{:S(2)}, u32[]{:S(2)}) %collective-permute-start.17) | collective-permute-done | bytes 180256 | tf_op jit(solution)/shard_map/ppermute | solution.py:648
  72.1 1.0 %level.1 = f32[4,32,1024]{2,1,0:T(8,128)} custom-call(s32[6]{0:T(128)S(4)} %get-tuple-element.40.scalars, f32[1024,128]{1,0:T(8,128)S(1)} %get-tuple-element.72.v), custom_call_target="tpu_custom_call" | custom-call | tf_op jit(solution)/shard_map/level/pallas_call | solution.py:551
  73.1 0.0 collective-permute-done.15.side
  73.1 7.7 %collective-permute-start.18 = (f32[2,176,128]{2,1,0:T(8,128)S(1)}, f32[2,176,128]{2,1,0:T(8,128)S(1)}, u32[]{:S(2)}, u32[]{:S(2)}) collective-permute-start(f32[2,176,128]{2,1,0:T(8,128)S(1)} %collective-permute-done.17.far), channel_id=1, source_target_pairs={{0,1},{1,0},{2,3},{3,2},{4,5},{5,4},{6,7},{7,6},{8,9},{9,8},{10,11... | collective-permute-start | bytes 540680 | tf_op jit(solution)/shard_map/ppermute | solution.py:660
  80.8 0.0 collective-permute-start.19
  80.8 1.2 %collective-permute-done.19.side_post = f32[16,128]{1,0:T(8,128)S(1)} collective-permute-done((f32[16,128]{1,0:T(8,128)S(1)}, f32[16,128]{1,0:T(8,128)S(1)}, u32[]{:S(2)}, u32[]{:S(2)}) %collective-permute-start.19) | collective-permute-done | bytes 8224 | tf_op jit(solution)/shard_map/ppermute | solution.py:661
  82.0 0.7 coarse.1
  (4 shorter events, 0.0 us)
Async XLA Ops:
  2.9 2.2 %collective-permute-start = (f32[12,32,128]{2,1,0:T(8,128)S(1)}, f32[12,32,128]{2,1,0:T(8,128)S(1)}, u32[]{:S(2)}, u32[]{:S(2)}) collective-permute-start(f32[12,32,128]{2,1,0:T(8,128)S(1)} %get-tuple-element.41.own), channel_id=1, source_target_pairs={{0,1},{1,0},{2,3},{3,2},{4,5},{5,4},{6,7},{7,6},{8,9},{9,8},{10,11... | collective-permute-start | bytes 589832 | tf_op jit(solution)/shard_map/ppermute | solution.py:604
  5.4 5.0 %collective-permute-start.2 = (f32[3,1024,128]{2,1,0:T(8,128)S(1)}, f32[3,1024,128]{2,1,0:T(8,128)S(1)}, u32[]{:S(2)}, u32[]{:S(2)}) collective-permute-start(f32[3,1024,128]{2,1,0:T(8,128)S(1)} %get-tuple-element.47.own), channel_id=1, source_target_pairs={{0,1},{1,0},{2,3},{3,2},{4,5},{5,4},{6,7},{7,6},{8,9},{9,8},{10,11... | collective-permute-start | bytes 4718600 | tf_op jit(solution)/shard_map/ppermute | solution.py:617
  5.5 4.9 %collective-permute-start.3 = (f32[2,1024,128]{2,1,0:T(8,128)S(1)}, f32[2,1024,128]{2,1,0:T(8,128)S(1)}, u32[]{:S(2)}, u32[]{:S(2)}) collective-permute-start(f32[2,1024,128]{2,1,0:T(8,128)S(1)} %collect_rest.1.own_rest), channel_id=1, source_target_pairs={{0,1},{1,0},{2,3},{3,2},{4,5},{5,4},{6,7},{7,6},{8,9},{9,8},{10,11... | collective-permute-start | bytes 3145736 | tf_op jit(solution)/shard_map/ppermute | solution.py:617
  6.0 11.7 %collective-permute-start.4 = (f32[12,32,128]{2,1,0:T(8,128)S(1)}, f32[12,32,128]{2,1,0:T(8,128)S(1)}, u32[]{:S(2)}, u32[]{:S(2)}) collective-permute-start(f32[12,32,128]{2,1,0:T(8,128)S(1)} %get-tuple-element.53.own), channel_id=1, source_target_pairs={{0,1},{1,0},{2,3},{3,2},{4,5},{5,4},{6,7},{7,6},{8,9},{9,8},{10,11... | collective-permute-start | bytes 589832 | tf_op jit(solution)/shard_map/ppermute | solution.py:613
  6.1 8.5 %collective-permute-start.1 = (f32[5,32,128]{2,1,0:T(8,128)S(1)}, f32[5,32,128]{2,1,0:T(8,128)S(1)}, u32[]{:S(2)}, u32[]{:S(2)}) collective-permute-start(f32[5,32,128]{2,1,0:T(8,128)S(1)} %get-tuple-element.46), channel_id=1, source_target_pairs={{1,2},{3,4},{5,6},{7,8},{9,10},{11,12},{13,14},{15,16},{17,18},{19... | collective-permute-start | bytes 245768 | tf_op jit(solution)/shard_map/ppermute | solution.py:612
  14.6 4.0 %collective-permute-start.5 = (f32[5,32,128]{2,1,0:T(8,128)S(1)}, f32[5,32,128]{2,1,0:T(8,128)S(1)}, u32[]{:S(2)}, u32[]{:S(2)}) collective-permute-start(f32[5,32,128]{2,1,0:T(8,128)S(1)} %collective-permute-done.1.far), channel_id=1, source_target_pairs={{0,1},{1,0},{2,3},{3,2},{4,5},{5,4},{6,7},{7,6},{8,9},{9,8},{10,11... | collective-permute-start | bytes 245768 | tf_op jit(solution)/shard_map/ppermute | solution.py:621
  20.9 11.9 %collective-permute-start.6 = (f32[4,32,128]{2,1,0:T(8,128)S(1)}, f32[4,32,128]{2,1,0:T(8,128)S(1)}, u32[]{:S(2)}, u32[]{:S(2)}) collective-permute-start(f32[4,32,128]{2,1,0:T(8,128)S(1)} %get-tuple-element.58.own), channel_id=1, source_target_pairs={{0,1},{1,0},{2,3},{3,2},{4,5},{5,4},{6,7},{7,6},{8,9},{9,8},{10,11... | collective-permute-start | bytes 196616 | tf_op jit(solution)/shard_map/ppermute | solution.py:571
  21.3 5.0 %collective-permute-start.7 = (f32[32,128]{1,0:T(8,128)S(1)}, f32[32,128]{1,0:T(8,128)S(1)}, u32[]{:S(2)}, u32[]{:S(2)}) collective-permute-start(f32[32,128]{1,0:T(8,128)S(1)} %get-tuple-element.59), channel_id=1, source_target_pairs={{1,2},{3,4},{5,6},{7,8},{9,10},{11,12},{13,14},{15,16},{17,18},{19... | collective-permute-start | bytes 49160 | tf_op jit(solution)/shard_map/ppermute | solution.py:570
  26.3 6.4 %collective-permute-start.8 = (f32[32,128]{1,0:T(8,128)S(1)}, f32[32,128]{1,0:T(8,128)S(1)}, u32[]{:S(2)}, u32[]{:S(2)}) collective-permute-start(f32[32,128]{1,0:T(8,128)S(1)} %collective-permute-done.7.far), channel_id=1, source_target_pairs={{0,1},{1,0},{2,3},{3,2},{4,5},{5,4},{6,7},{7,6},{8,9},{9,8},{10,11... | collective-permute-start | bytes 49160 | tf_op jit(solution)/shard_map/ppermute | solution.py:572
  34.1 11.9 %collective-permute-start.9 = (f32[4,32,128]{2,1,0:T(8,128)S(1)}, f32[4,32,128]{2,1,0:T(8,128)S(1)}, u32[]{:S(2)}, u32[]{:S(2)}) collective-permute-start(f32[4,32,128]{2,1,0:T(8,128)S(1)} %get-tuple-element.61.own), channel_id=1, source_target_pairs={{0,1},{1,0},{2,3},{3,2},{4,5},{5,4},{6,7},{7,6},{8,9},{9,8},{10,11... | collective-permute-start | bytes 196616 | tf_op jit(solution)/shard_map/ppermute | solution.py:571
  34.5 5.0 %collective-permute-start.10 = (f32[32,128]{1,0:T(8,128)S(1)}, f32[32,128]{1,0:T(8,128)S(1)}, u32[]{:S(2)}, u32[]{:S(2)}) collective-permute-start(f32[32,128]{1,0:T(8,128)S(1)} %get-tuple-element.62), channel_id=1, source_target_pairs={{1,2},{3,4},{5,6},{7,8},{9,10},{11,12},{13,14},{15,16},{17,18},{19... | collective-permute-start | bytes 49160 | tf_op jit(solution)/shard_map/ppermute | solution.py:570
  39.5 6.4 %collective-permute-start.11 = (f32[32,128]{1,0:T(8,128)S(1)}, f32[32,128]{1,0:T(8,128)S(1)}, u32[]{:S(2)}, u32[]{:S(2)}) collective-permute-start(f32[32,128]{1,0:T(8,128)S(1)} %collective-permute-done.10.far), channel_id=1, source_target_pairs={{0,1},{1,0},{2,3},{3,2},{4,5},{5,4},{6,7},{7,6},{8,9},{9,8},{10,11... | collective-permute-start | bytes 49160 | tf_op jit(solution)/shard_map/ppermute | solution.py:572
  47.3 11.9 %collective-permute-start.12 = (f32[4,32,128]{2,1,0:T(8,128)S(1)}, f32[4,32,128]{2,1,0:T(8,128)S(1)}, u32[]{:S(2)}, u32[]{:S(2)}) collective-permute-start(f32[4,32,128]{2,1,0:T(8,128)S(1)} %get-tuple-element.64.own), channel_id=1, source_target_pairs={{0,1},{1,0},{2,3},{3,2},{4,5},{5,4},{6,7},{7,6},{8,9},{9,8},{10,11... | collective-permute-start | bytes 196616 | tf_op jit(solution)/shard_map/ppermute | solution.py:571
  47.7 5.0 %collective-permute-start.13 = (f32[32,128]{1,0:T(8,128)S(1)}, f32[32,128]{1,0:T(8,128)S(1)}, u32[]{:S(2)}, u32[]{:S(2)}) collective-permute-start(f32[32,128]{1,0:T(8,128)S(1)} %get-tuple-element.65), channel_id=1, source_target_pairs={{1,2},{3,4},{5,6},{7,8},{9,10},{11,12},{13,14},{15,16},{17,18},{19... | collective-permute-start | bytes 49160 | tf_op jit(solution)/shard_map/ppermute | solution.py:570
  52.7 6.4 %collective-permute-start.14 = (f32[32,128]{1,0:T(8,128)S(1)}, f32[32,128]{1,0:T(8,128)S(1)}, u32[]{:S(2)}, u32[]{:S(2)}) collective-permute-start(f32[32,128]{1,0:T(8,128)S(1)} %collective-permute-done.13.far), channel_id=1, source_target_pairs={{0,1},{1,0},{2,3},{3,2},{4,5},{5,4},{6,7},{7,6},{8,9},{9,8},{10,11... | collective-permute-start | bytes 49160 | tf_op jit(solution)/shard_map/ppermute | solution.py:572
  62.3 1.4 %collective-permute-start.16 = (f32[176,128]{1,0:T(8,128)S(1)}, f32[176,128]{1,0:T(8,128)S(1)}, u32[]{:S(2)}, u32[]{:S(2)}) collective-permute-start(f32[176,128]{1,0:T(8,128)S(1)} %get-tuple-element.71), channel_id=1, source_target_pairs={{0,1},{1,0},{2,3},{3,2},{4,5},{5,4},{6,7},{7,6},{8,9},{9,8},{10,11... | collective-permute-start | bytes 270344 | tf_op jit(solution)/shard_map/ppermute | solution.py:646
  63.7 8.4 %collective-permute-start.17 = (f32[2,176,128]{2,1,0:T(8,128)S(1)}, f32[2,176,128]{2,1,0:T(8,128)S(1)}, u32[]{:S(2)}, u32[]{:S(2)}) collective-permute-start(f32[2,176,128]{2,1,0:T(8,128)S(1)} %pad_maximum_fusion.own), channel_id=1, source_target_pairs={{2,1},{4,3},{6,5},{8,7},{10,9},{12,11},{14,13},{16,15},{18,17},{20... | collective-permute-start | bytes 540680 | tf_op jit(solution)/shard_map/ppermute | solution.py:648
  65.6 7.5 %collective-permute-start.15 = (f32[16,128]{1,0:T(8,128)S(1)}, f32[16,128]{1,0:T(8,128)S(1)}, u32[]{:S(2)}, u32[]{:S(2)}) collective-permute-start(f32[16,128]{1,0:T(8,128)S(1)} %get-tuple-element.70), channel_id=1, source_target_pairs={{6,1},{8,3},{10,5},{12,7},{14,9},{16,11},{18,13},{20,15},{22,17},{... | collective-permute-start | bytes 24584 | tf_op jit(solution)/shard_map/ppermute | solution.py:649
  73.1 8.9 %collective-permute-start.18 = (f32[2,176,128]{2,1,0:T(8,128)S(1)}, f32[2,176,128]{2,1,0:T(8,128)S(1)}, u32[]{:S(2)}, u32[]{:S(2)}) collective-permute-start(f32[2,176,128]{2,1,0:T(8,128)S(1)} %collective-permute-done.17.far), channel_id=1, source_target_pairs={{0,1},{1,0},{2,3},{3,2},{4,5},{5,4},{6,7},{7,6},{8,9},{9,8},{10,11... | collective-permute-start | bytes 540680 | tf_op jit(solution)/shard_map/ppermute | solution.py:660
  80.8 1.2 %collective-permute-start.19 = (f32[16,128]{1,0:T(8,128)S(1)}, f32[16,128]{1,0:T(8,128)S(1)}, u32[]{:S(2)}, u32[]{:S(2)}) collective-permute-start(f32[16,128]{1,0:T(8,128)S(1)} %collective-permute-done.15.side), channel_id=1, source_target_pairs={{0,1},{1,0},{2,3},{3,2},{4,5},{5,4},{6,7},{7,6},{8,9},{9,8},{10,11... | collective-permute-start | bytes 24584 | tf_op jit(solution)/shard_map/ppermute | solution.py:661

commit v4 on v3

--- a/solution.py
+++ b/solution.py
@@ -347,7 +347,7 @@
             vo[rows, :] = jnp.where(shade == 0, total, value)
         return carry
 
-    lax.fori_loop(0, SPAN, layer, 0, unroll=4)
+    lax.fori_loop(0, SPAN, layer, 0, unroll=16)
     put_faces(base, vo, faces)
     put_sent(scalars, 0, faces, sent)
 
@@ -375,7 +375,7 @@
             vo[tile_row(y, t), :] = jnp.where(shade == shade_now, total, value)
         return carry
 
-    lax.fori_loop(0, SPAN, layer, 0, unroll=8)
+    lax.fori_loop(0, SPAN, layer, 0, unroll=32)
     put_faces(base, vo, faces)
     if sent:
         put_sent(scalars, shade_now, faces, sent[0])

time: 83.8 us -> 82.8 us (0.988)
  Pallas kernels: 18 us -> 16.8 us
    pallas_call x11, Pallas kernels: 18 us -> 16.8 us  [call(): pl.pallas_call(kernel, out_shape=out_shape, in_specs=list(leading) + (spe...]
where the time goes in v4:
time: 82.8 us; the launch traced here: 81.7 us
  starting transfers between devices  45.5 us (55%)
  waiting for transfers between devices  18.6 us (22%)
  Pallas kernels  16.8 us (20%)
    pallas_call x11, Pallas kernels, call(): pl.pallas_call(kernel, out_shape=out_shape, in_specs=list(leading) + (spe...  16.8 us
    ppermute x3, starting transfers between devices, exchange(): post = lax.ppermute(far, AXES, swap)  16.8 us
    ppermute x2, starting transfers between devices, shards(): post = lax.ppermute(far, AXES, swap)  10.8 us
    ppermute x3, waiting for transfers between devices, exchange(): far = lax.ppermute(sent, AXES, reach)  9.39 us
    ppermute x3, starting transfers between devices, exchange(): far = lax.ppermute(sent, AXES, reach)  5.73 us
    ppermute x1, starting transfers between devices, shards(): side = lax.ppermute(cross, AXES, beside)  3.64 us
    ppermute x1, starting transfers between devices, shards(): far = lax.ppermute(sent, AXES, reach)  3.4 us
    ppermute x1, waiting for transfers between devices, shards(): far = lax.ppermute(both, AXES, downward)  2.78 us
  transfers between devices with their start and end apart: 20, of which 11 were waited for; matrix products, arithmetic and copies ran while one was open for 0% of the time, Pallas kernels for 8%

profile of v4, /device:TPU:129, one launch (start us, length us, event | category | flops | bytes accessed | tf_op | source)
XLA Modules:
  0.0 81.7 jit_solution(3321672403504336211)
XLA Ops:
  0.6 2.3 %collect.1 = (s32[6]{0:T(128)S(4)}, f32[3,1024,128]{2,1,0:T(8,128)S(1)}, f32[12,32,128]{2,1,0:T(8,128)S(1)}) custom-call(s32[6,128]{1,0:T(8,128)} %bitcast.15, f32[128,1024]{1,0:T(8,128)} %bitcast.9, f32[128,1024]{1,0:T(8,128)} %bitcast.10, s32[128,1024]{1,0:T(8,128)} %bitcast.11), custom_call_target="tpu_custom_call" | custom-call | tf_op jit(solution)/shard_map/collect/pallas_call | solution.py:551
  2.9 0.8 collective-permute-start
  3.7 1.5 %collect_rest.1.own_rest = f32[2,1024,128]{2,1,0:T(8,128)S(1)} custom-call(f32[128,1024]{1,0:T(8,128)} %bitcast.12, f32[128,1024]{1,0:T(8,128)} %bitcast.13), custom_call_target="tpu_custom_call" | custom-call | tf_op jit(solution)/shard_map/collect_rest/pallas_call | solution.py:551
  5.2 0.0 collective-permute-done.oth
  5.2 0.3 face_window.1
  5.4 0.1 collective-permute-start.2
  5.5 0.5 collective-permute-start.3
  6.0 0.1 collective-permute-start.4
  6.1 3.4 %collective-permute-start.1 = (f32[5,32,128]{2,1,0:T(8,128)S(1)}, f32[5,32,128]{2,1,0:T(8,128)S(1)}, u32[]{:S(2)}, u32[]{:S(2)}) collective-permute-start(f32[5,32,128]{2,1,0:T(8,128)S(1)} %get-tuple-element.46), channel_id=1, source_target_pairs={{1,2},{3,4},{5,6},{7,8},{9,10},{11,12},{13,14},{15,16},{17,18},{19... | collective-permute-start | bytes 245768 | tf_op jit(solution)/shard_map/ppermute | solution.py:612
  9.5 0.9 %collective-permute-done.3.oth_rest = f32[2,1024,128]{2,1,0:T(8,128)S(1)} collective-permute-done((f32[2,1024,128]{2,1,0:T(8,128)S(1)}, f32[2,1024,128]{2,1,0:T(8,128)S(1)}, u32[]{:S(2)}, u32[]{:S(2)}) %collective-permute-start.3) | collective-permute-done | bytes 1048608 | tf_op jit(solution)/shard_map/ppermute | solution.py:617
  10.4 4.2 %window.1 = (f32[5,1024,128]{2,1,0:T(8,128)S(1)}, f32[5,1024,128]{2,1,0:T(8,128)S(1)}) custom-call(s32[6]{0:T(128)S(4)} %get-tuple-element.40.scalars, f32[3,1024,128]{2,1,0:T(8,128)S(1)} %get-tuple-element.47.own, f32[3,1024,128]{2,1,0:T(8,128)S(1)} %collective-permute-done.2.oth, f32[2,1024,128]{2,1,0:T(8,128)S(1)} %collect_rest.1.own_rest, ...), custom_call_target="tpu_custom_call" | custom-call | tf_op jit(solution)/shard_map/window/pallas_call | solution.py:551
  14.6 0.0 collective-permute-done.1.far
  14.6 3.1 %collective-permute-start.5 = (f32[5,32,128]{2,1,0:T(8,128)S(1)}, f32[5,32,128]{2,1,0:T(8,128)S(1)}, u32[]{:S(2)}, u32[]{:S(2)}) collective-permute-start(f32[5,32,128]{2,1,0:T(8,128)S(1)} %collective-permute-done.1.far), channel_id=1, source_target_pairs={{0,1},{1,0},{2,3},{3,2},{4,5},{5,4},{6,7},{7,6},{8,9},{9,8},{10,11... | collective-permute-start | bytes 245768 | tf_op jit(solution)/shard_map/ppermute | solution.py:621
  17.7 0.0 collective-permute-done.4.oth
  17.7 0.9 %collective-permute-done.5.post = f32[5,32,128]{2,1,0:T(8,128)S(1)} collective-permute-done((f32[5,32,128]{2,1,0:T(8,128)S(1)}, f32[5,32,128]{2,1,0:T(8,128)S(1)}, u32[]{:S(2)}, u32[]{:S(2)}) %collective-permute-start.5) | collective-permute-done | bytes 81952 | tf_op jit(solution)/shard_map/ppermute | solution.py:621
  18.6 1.9 %first.1 = (f32[1024,128]{1,0:T(8,128)S(1)}, f32[1024,128]{1,0:T(8,128)S(1)}, f32[1024,128]{1,0:T(8,128)S(1)}, f32[6,1024,128]{2,1,0:T(8,128)S(1)}, f32[4,32,128...) custom-call(s32[6]{0:T(128)S(4)} %get-tuple-element.40.scalars, ...), custom_call_target="tpu_custom_call" | custom-call | tf_op jit(solution)/shard_map/first/pallas_call | solution.py:551
  20.5 0.4 collective-permute-start.6
  20.9 1.9 %collective-permute-start.7 = (f32[32,128]{1,0:T(8,128)S(1)}, f32[32,128]{1,0:T(8,128)S(1)}, u32[]{:S(2)}, u32[]{:S(2)}) collective-permute-start(f32[32,128]{1,0:T(8,128)S(1)} %get-tuple-element.59), channel_id=1, source_target_pairs={{1,2},{3,4},{5,6},{7,8},{9,10},{11,12},{13,14},{15,16},{17,18},{19... | collective-permute-start | bytes 49160 | tf_op jit(solution)/shard_map/ppermute | solution.py:570
  22.8 3.1 %collective-permute-done.7.far = f32[32,128]{1,0:T(8,128)S(1)} collective-permute-done((f32[32,128]{1,0:T(8,128)S(1)}, f32[32,128]{1,0:T(8,128)S(1)}, u32[]{:S(2)}, u32[]{:S(2)}) %collective-permute-start.7) | collective-permute-done | bytes 16416 | tf_op jit(solution)/shard_map/ppermute | solution.py:570
  25.9 5.6 %collective-permute-start.8 = (f32[32,128]{1,0:T(8,128)S(1)}, f32[32,128]{1,0:T(8,128)S(1)}, u32[]{:S(2)}, u32[]{:S(2)}) collective-permute-start(f32[32,128]{1,0:T(8,128)S(1)} %collective-permute-done.7.far), channel_id=1, source_target_pairs={{0,1},{1,0},{2,3},{3,2},{4,5},{5,4},{6,7},{7,6},{8,9},{9,8},{10,11... | collective-permute-start | bytes 49160 | tf_op jit(solution)/shard_map/ppermute | solution.py:572
  31.5 0.8 %collective-permute-done.8.post = f32[32,128]{1,0:T(8,128)S(1)} collective-permute-done((f32[32,128]{1,0:T(8,128)S(1)}, f32[32,128]{1,0:T(8,128)S(1)}, u32[]{:S(2)}, u32[]{:S(2)}) %collective-permute-start.8) | collective-permute-done | bytes 16416 | tf_op jit(solution)/shard_map/ppermute | solution.py:572
  32.3 0.0 collective-permute-done.6.oth
  32.3 1.1 %sweep.3 = (f32[1024,128]{1,0:T(8,128)S(1)}, f32[4,32,128]{2,1,0:T(8,128)S(1)}, f32[32,128]{1,0:T(8,128)S(1)}) custom-call(s32[6]{0:T(128)S(4)} %get-tuple-element.40.scalars, f32[1024,128]{1,0:T(8,128)S(1)} %get-tuple-element.55.v, f32[1024,128]{1,0:T(8,128)S(1)} %get-tuple-element.56.f, f32[6,1024,128]{2,1,0:T(8,128)S(1)} %get-tuple-element.57.g, ...), custom_call_target="tpu_custom_call" | custom-call | tf_op jit(solution)/shard_map/sweep/pallas_call | solution.py:551
  33.5 0.4 collective-permute-start.9
  33.8 1.9 %collective-permute-start.10 = (f32[32,128]{1,0:T(8,128)S(1)}, f32[32,128]{1,0:T(8,128)S(1)}, u32[]{:S(2)}, u32[]{:S(2)}) collective-permute-start(f32[32,128]{1,0:T(8,128)S(1)} %get-tuple-element.62), channel_id=1, source_target_pairs={{1,2},{3,4},{5,6},{7,8},{9,10},{11,12},{13,14},{15,16},{17,18},{19... | collective-permute-start | bytes 49160 | tf_op jit(solution)/shard_map/ppermute | solution.py:570
  35.8 3.1 %collective-permute-done.10.far = f32[32,128]{1,0:T(8,128)S(1)} collective-permute-done((f32[32,128]{1,0:T(8,128)S(1)}, f32[32,128]{1,0:T(8,128)S(1)}, u32[]{:S(2)}, u32[]{:S(2)}) %collective-permute-start.10) | collective-permute-done | bytes 16416 | tf_op jit(solution)/shard_map/ppermute | solution.py:570
  38.9 5.6 %collective-permute-start.11 = (f32[32,128]{1,0:T(8,128)S(1)}, f32[32,128]{1,0:T(8,128)S(1)}, u32[]{:S(2)}, u32[]{:S(2)}) collective-permute-start(f32[32,128]{1,0:T(8,128)S(1)} %collective-permute-done.10.far), channel_id=1, source_target_pairs={{0,1},{1,0},{2,3},{3,2},{4,5},{5,4},{6,7},{7,6},{8,9},{9,8},{10,11... | collective-permute-start | bytes 49160 | tf_op jit(solution)/shard_map/ppermute | solution.py:572
  44.5 0.8 %collective-permute-done.11.post = f32[32,128]{1,0:T(8,128)S(1)} collective-permute-done((f32[32,128]{1,0:T(8,128)S(1)}, f32[32,128]{1,0:T(8,128)S(1)}, u32[]{:S(2)}, u32[]{:S(2)}) %collective-permute-start.11) | collective-permute-done | bytes 16416 | tf_op jit(solution)/shard_map/ppermute | solution.py:572
  45.3 1.1 %sweep.4 = (f32[1024,128]{1,0:T(8,128)S(1)}, f32[4,32,128]{2,1,0:T(8,128)S(1)}, f32[32,128]{1,0:T(8,128)S(1)}) custom-call(s32[6]{0:T(128)S(4)} %get-tuple-element.40.scalars, f32[1024,128]{1,0:T(8,128)S(1)} %get-tuple-element.60.v, f32[1024,128]{1,0:T(8,128)S(1)} %get-tuple-element.56.f, f32[6,1024,128]{2,1,0:T(8,128)S(1)} %get-tuple-element.57.g, ...), custom_call_target="tpu_custom_call" | custom-call | tf_op jit(solution)/shard_map/sweep/pallas_call | solution.py:551
  46.4 0.4 collective-permute-start.12
  46.8 1.9 %collective-permute-start.13 = (f32[32,128]{1,0:T(8,128)S(1)}, f32[32,128]{1,0:T(8,128)S(1)}, u32[]{:S(2)}, u32[]{:S(2)}) collective-permute-start(f32[32,128]{1,0:T(8,128)S(1)} %get-tuple-element.65), channel_id=1, source_target_pairs={{1,2},{3,4},{5,6},{7,8},{9,10},{11,12},{13,14},{15,16},{17,18},{19... | collective-permute-start | bytes 49160 | tf_op jit(solution)/shard_map/ppermute | solution.py:570
  48.7 3.1 %collective-permute-done.13.far = f32[32,128]{1,0:T(8,128)S(1)} collective-permute-done((f32[32,128]{1,0:T(8,128)S(1)}, f32[32,128]{1,0:T(8,128)S(1)}, u32[]{:S(2)}, u32[]{:S(2)}) %collective-permute-start.13) | collective-permute-done | bytes 16416 | tf_op jit(solution)/shard_map/ppermute | solution.py:570
  51.9 5.6 %collective-permute-start.14 = (f32[32,128]{1,0:T(8,128)S(1)}, f32[32,128]{1,0:T(8,128)S(1)}, u32[]{:S(2)}, u32[]{:S(2)}) collective-permute-start(f32[32,128]{1,0:T(8,128)S(1)} %collective-permute-done.13.far), channel_id=1, source_target_pairs={{0,1},{1,0},{2,3},{3,2},{4,5},{5,4},{6,7},{7,6},{8,9},{9,8},{10,11... | collective-permute-start | bytes 49160 | tf_op jit(solution)/shard_map/ppermute | solution.py:572
  57.5 0.8 %collective-permute-done.14.post = f32[32,128]{1,0:T(8,128)S(1)} collective-permute-done((f32[32,128]{1,0:T(8,128)S(1)}, f32[32,128]{1,0:T(8,128)S(1)}, u32[]{:S(2)}, u32[]{:S(2)}) %collective-permute-start.14) | collective-permute-done | bytes 16416 | tf_op jit(solution)/shard_map/ppermute | solution.py:572
  58.3 0.0 collective-permute-done.12.oth
  58.3 1.0 %sweep.5 = (f32[1024,128]{1,0:T(8,128)S(1)}, f32[4,32,128]{2,1,0:T(8,128)S(1)}) custom-call(s32[6]{0:T(128)S(4)} %get-tuple-element.40.scalars, f32[1024,128]{1,0:T(8,128)S(1)} %get-tuple-element.63.v, f32[1024,128]{1,0:T(8,128)S(1)} %get-tuple-element.56.f, f32[6,1024,128]{2,1,0:T(8,128)S(1)} %get-tuple-element.57.g, ...), custom_call_target="tpu_custom_call" | custom-call | tf_op jit(solution)/shard_map/sweep/pallas_call | solution.py:551
  59.3 1.8 %residual.1 = (f32[176,128]{1,0:T(8,128)S(1)}, f32[16,128]{1,0:T(8,128)S(1)}) custom-call(s32[6]{0:T(128)S(4)} %get-tuple-element.40.scalars, f32[1024,128]{1,0:T(8,128)S(1)} %get-tuple-element.72.v, f32[1024,128]{1,0:T(8,128)S(1)} %get-tuple-element.56.f, f32[6,1024,128]{2,1,0:T(8,128)S(1)} %get-tuple-element.57.g, f32[1024,128]{1,0:T(8,128)S(1)} %get-tuple-element.67.d, ...), custom_call_target="tpu_custom_call" | custom-call | tf_op jit(solution)/shard_map/residual/pallas_call | solution.py:551
  61.2 0.6 collective-permute-start.16
  61.8 0.9 %collective-permute-done.16 = f32[176,128]{1,0:T(8,128)S(1)} collective-permute-done((f32[176,128]{1,0:T(8,128)S(1)}, f32[176,128]{1,0:T(8,128)S(1)}, u32[]{:S(2)}, u32[]{:S(2)}) %collective-permute-start.16) | collective-permute-done | bytes 90144 | tf_op jit(solution)/shard_map/ppermute | solution.py:646
  62.8 1.9 %collective-permute-start.17 = (f32[2,176,128]{2,1,0:T(8,128)S(1)}, f32[2,176,128]{2,1,0:T(8,128)S(1)}, u32[]{:S(2)}, u32[]{:S(2)}) collective-permute-start(f32[2,176,128]{2,1,0:T(8,128)S(1)} %pad_maximum_fusion.own), channel_id=1, source_target_pairs={{2,1},{4,3},{6,5},{8,7},{10,9},{12,11},{14,13},{16,15},{18,17},{20... | collective-permute-start | bytes 540680 | tf_op jit(solution)/shard_map/ppermute | solution.py:648
  64.7 3.6 %collective-permute-start.15 = (f32[16,128]{1,0:T(8,128)S(1)}, f32[16,128]{1,0:T(8,128)S(1)}, u32[]{:S(2)}, u32[]{:S(2)}) collective-permute-start(f32[16,128]{1,0:T(8,128)S(1)} %get-tuple-element.70), channel_id=1, source_target_pairs={{6,1},{8,3},{10,5},{12,7},{14,9},{16,11},{18,13},{20,15},{22,17},{... | collective-permute-start | bytes 24584 | tf_op jit(solution)/shard_map/ppermute | solution.py:649
  68.3 2.8 %collective-permute-done.17.far = f32[2,176,128]{2,1,0:T(8,128)S(1)} collective-permute-done((f32[2,176,128]{2,1,0:T(8,128)S(1)}, f32[2,176,128]{2,1,0:T(8,128)S(1)}, u32[]{:S(2)}, u32[]{:S(2)}) %collective-permute-start.17) | collective-permute-done | bytes 180256 | tf_op jit(solution)/shard_map/ppermute | solution.py:648
  71.1 1.0 %level.1 = f32[4,32,1024]{2,1,0:T(8,128)} custom-call(s32[6]{0:T(128)S(4)} %get-tuple-element.40.scalars, f32[1024,128]{1,0:T(8,128)S(1)} %get-tuple-element.72.v), custom_call_target="tpu_custom_call" | custom-call | tf_op jit(solution)/shard_map/level/pallas_call | solution.py:551
  72.2 7.7 %collective-permute-start.18 = (f32[2,176,128]{2,1,0:T(8,128)S(1)}, f32[2,176,128]{2,1,0:T(8,128)S(1)}, u32[]{:S(2)}, u32[]{:S(2)}) collective-permute-start(f32[2,176,128]{2,1,0:T(8,128)S(1)} %collective-permute-done.17.far), channel_id=1, source_target_pairs={{0,1},{1,0},{2,3},{3,2},{4,5},{5,4},{6,7},{7,6},{8,9},{9,8},{10,11... | collective-permute-start | bytes 540680 | tf_op jit(solution)/shard_map/ppermute | solution.py:660
  79.9 0.0 collective-permute-start.19
  79.9 1.2 %collective-permute-done.19.side_post = f32[16,128]{1,0:T(8,128)S(1)} collective-permute-done((f32[16,128]{1,0:T(8,128)S(1)}, f32[16,128]{1,0:T(8,128)S(1)}, u32[]{:S(2)}, u32[]{:S(2)}) %collective-permute-start.19) | collective-permute-done | bytes 8224 | tf_op jit(solution)/shard_map/ppermute | solution.py:661
  81.0 0.0 collective-permute-done.18.post
  81.1 0.7 coarse.1
  (4 shorter events, 0.0 us)
Async XLA Ops:
  2.9 2.2 %collective-permute-start = (f32[12,32,128]{2,1,0:T(8,128)S(1)}, f32[12,32,128]{2,1,0:T(8,128)S(1)}, u32[]{:S(2)}, u32[]{:S(2)}) collective-permute-start(f32[12,32,128]{2,1,0:T(8,128)S(1)} %get-tuple-element.41.own), channel_id=1, source_target_pairs={{0,1},{1,0},{2,3},{3,2},{4,5},{5,4},{6,7},{7,6},{8,9},{9,8},{10,11... | collective-permute-start | bytes 589832 | tf_op jit(solution)/shard_map/ppermute | solution.py:604
  5.4 5.0 %collective-permute-start.2 = (f32[3,1024,128]{2,1,0:T(8,128)S(1)}, f32[3,1024,128]{2,1,0:T(8,128)S(1)}, u32[]{:S(2)}, u32[]{:S(2)}) collective-permute-start(f32[3,1024,128]{2,1,0:T(8,128)S(1)} %get-tuple-element.47.own), channel_id=1, source_target_pairs={{0,1},{1,0},{2,3},{3,2},{4,5},{5,4},{6,7},{7,6},{8,9},{9,8},{10,11... | collective-permute-start | bytes 4718600 | tf_op jit(solution)/shard_map/ppermute | solution.py:617
  5.5 4.9 %collective-permute-start.3 = (f32[2,1024,128]{2,1,0:T(8,128)S(1)}, f32[2,1024,128]{2,1,0:T(8,128)S(1)}, u32[]{:S(2)}, u32[]{:S(2)}) collective-permute-start(f32[2,1024,128]{2,1,0:T(8,128)S(1)} %collect_rest.1.own_rest), channel_id=1, source_target_pairs={{0,1},{1,0},{2,3},{3,2},{4,5},{5,4},{6,7},{7,6},{8,9},{9,8},{10,11... | collective-permute-start | bytes 3145736 | tf_op jit(solution)/shard_map/ppermute | solution.py:617
  6.0 11.7 %collective-permute-start.4 = (f32[12,32,128]{2,1,0:T(8,128)S(1)}, f32[12,32,128]{2,1,0:T(8,128)S(1)}, u32[]{:S(2)}, u32[]{:S(2)}) collective-permute-start(f32[12,32,128]{2,1,0:T(8,128)S(1)} %get-tuple-element.53.own), channel_id=1, source_target_pairs={{0,1},{1,0},{2,3},{3,2},{4,5},{5,4},{6,7},{7,6},{8,9},{9,8},{10,11... | collective-permute-start | bytes 589832 | tf_op jit(solution)/shard_map/ppermute | solution.py:613
  6.1 8.5 %collective-permute-start.1 = (f32[5,32,128]{2,1,0:T(8,128)S(1)}, f32[5,32,128]{2,1,0:T(8,128)S(1)}, u32[]{:S(2)}, u32[]{:S(2)}) collective-permute-start(f32[5,32,128]{2,1,0:T(8,128)S(1)} %get-tuple-element.46), channel_id=1, source_target_pairs={{1,2},{3,4},{5,6},{7,8},{9,10},{11,12},{13,14},{15,16},{17,18},{19... | collective-permute-start | bytes 245768 | tf_op jit(solution)/shard_map/ppermute | solution.py:612
  14.6 4.0 %collective-permute-start.5 = (f32[5,32,128]{2,1,0:T(8,128)S(1)}, f32[5,32,128]{2,1,0:T(8,128)S(1)}, u32[]{:S(2)}, u32[]{:S(2)}) collective-permute-start(f32[5,32,128]{2,1,0:T(8,128)S(1)} %collective-permute-done.1.far), channel_id=1, source_target_pairs={{0,1},{1,0},{2,3},{3,2},{4,5},{5,4},{6,7},{7,6},{8,9},{9,8},{10,11... | collective-permute-start | bytes 245768 | tf_op jit(solution)/shard_map/ppermute | solution.py:621
  20.5 11.9 %collective-permute-start.6 = (f32[4,32,128]{2,1,0:T(8,128)S(1)}, f32[4,32,128]{2,1,0:T(8,128)S(1)}, u32[]{:S(2)}, u32[]{:S(2)}) collective-permute-start(f32[4,32,128]{2,1,0:T(8,128)S(1)} %get-tuple-element.58.own), channel_id=1, source_target_pairs={{0,1},{1,0},{2,3},{3,2},{4,5},{5,4},{6,7},{7,6},{8,9},{9,8},{10,11... | collective-permute-start | bytes 196616 | tf_op jit(solution)/shard_map/ppermute | solution.py:571
  20.9 5.0 %collective-permute-start.7 = (f32[32,128]{1,0:T(8,128)S(1)}, f32[32,128]{1,0:T(8,128)S(1)}, u32[]{:S(2)}, u32[]{:S(2)}) collective-permute-start(f32[32,128]{1,0:T(8,128)S(1)} %get-tuple-element.59), channel_id=1, source_target_pairs={{1,2},{3,4},{5,6},{7,8},{9,10},{11,12},{13,14},{15,16},{17,18},{19... | collective-permute-start | bytes 49160 | tf_op jit(solution)/shard_map/ppermute | solution.py:570
  25.9 6.4 %collective-permute-start.8 = (f32[32,128]{1,0:T(8,128)S(1)}, f32[32,128]{1,0:T(8,128)S(1)}, u32[]{:S(2)}, u32[]{:S(2)}) collective-permute-start(f32[32,128]{1,0:T(8,128)S(1)} %collective-permute-done.7.far), channel_id=1, source_target_pairs={{0,1},{1,0},{2,3},{3,2},{4,5},{5,4},{6,7},{7,6},{8,9},{9,8},{10,11... | collective-permute-start | bytes 49160 | tf_op jit(solution)/shard_map/ppermute | solution.py:572
  33.5 11.9 %collective-permute-start.9 = (f32[4,32,128]{2,1,0:T(8,128)S(1)}, f32[4,32,128]{2,1,0:T(8,128)S(1)}, u32[]{:S(2)}, u32[]{:S(2)}) collective-permute-start(f32[4,32,128]{2,1,0:T(8,128)S(1)} %get-tuple-element.61.own), channel_id=1, source_target_pairs={{0,1},{1,0},{2,3},{3,2},{4,5},{5,4},{6,7},{7,6},{8,9},{9,8},{10,11... | collective-permute-start | bytes 196616 | tf_op jit(solution)/shard_map/ppermute | solution.py:571
  33.8 5.0 %collective-permute-start.10 = (f32[32,128]{1,0:T(8,128)S(1)}, f32[32,128]{1,0:T(8,128)S(1)}, u32[]{:S(2)}, u32[]{:S(2)}) collective-permute-start(f32[32,128]{1,0:T(8,128)S(1)} %get-tuple-element.62), channel_id=1, source_target_pairs={{1,2},{3,4},{5,6},{7,8},{9,10},{11,12},{13,14},{15,16},{17,18},{19... | collective-permute-start | bytes 49160 | tf_op jit(solution)/shard_map/ppermute | solution.py:570
  38.9 6.4 %collective-permute-start.11 = (f32[32,128]{1,0:T(8,128)S(1)}, f32[32,128]{1,0:T(8,128)S(1)}, u32[]{:S(2)}, u32[]{:S(2)}) collective-permute-start(f32[32,128]{1,0:T(8,128)S(1)} %collective-permute-done.10.far), channel_id=1, source_target_pairs={{0,1},{1,0},{2,3},{3,2},{4,5},{5,4},{6,7},{7,6},{8,9},{9,8},{10,11... | collective-permute-start | bytes 49160 | tf_op jit(solution)/shard_map/ppermute | solution.py:572
  46.4 11.9 %collective-permute-start.12 = (f32[4,32,128]{2,1,0:T(8,128)S(1)}, f32[4,32,128]{2,1,0:T(8,128)S(1)}, u32[]{:S(2)}, u32[]{:S(2)}) collective-permute-start(f32[4,32,128]{2,1,0:T(8,128)S(1)} %get-tuple-element.64.own), channel_id=1, source_target_pairs={{0,1},{1,0},{2,3},{3,2},{4,5},{5,4},{6,7},{7,6},{8,9},{9,8},{10,11... | collective-permute-start | bytes 196616 | tf_op jit(solution)/shard_map/ppermute | solution.py:571
  46.8 5.0 %collective-permute-start.13 = (f32[32,128]{1,0:T(8,128)S(1)}, f32[32,128]{1,0:T(8,128)S(1)}, u32[]{:S(2)}, u32[]{:S(2)}) collective-permute-start(f32[32,128]{1,0:T(8,128)S(1)} %get-tuple-element.65), channel_id=1, source_target_pairs={{1,2},{3,4},{5,6},{7,8},{9,10},{11,12},{13,14},{15,16},{17,18},{19... | collective-permute-start | bytes 49160 | tf_op jit(solution)/shard_map/ppermute | solution.py:570
  51.9 6.4 %collective-permute-start.14 = (f32[32,128]{1,0:T(8,128)S(1)}, f32[32,128]{1,0:T(8,128)S(1)}, u32[]{:S(2)}, u32[]{:S(2)}) collective-permute-start(f32[32,128]{1,0:T(8,128)S(1)} %collective-permute-done.13.far), channel_id=1, source_target_pairs={{0,1},{1,0},{2,3},{3,2},{4,5},{5,4},{6,7},{7,6},{8,9},{9,8},{10,11... | collective-permute-start | bytes 49160 | tf_op jit(solution)/shard_map/ppermute | solution.py:572
  61.2 1.6 %collective-permute-start.16 = (f32[176,128]{1,0:T(8,128)S(1)}, f32[176,128]{1,0:T(8,128)S(1)}, u32[]{:S(2)}, u32[]{:S(2)}) collective-permute-start(f32[176,128]{1,0:T(8,128)S(1)} %get-tuple-element.71), channel_id=1, source_target_pairs={{0,1},{1,0},{2,3},{3,2},{4,5},{5,4},{6,7},{7,6},{8,9},{9,8},{10,11... | collective-permute-start | bytes 270344 | tf_op jit(solution)/shard_map/ppermute | solution.py:646
  62.8 8.4 %collective-permute-start.17 = (f32[2,176,128]{2,1,0:T(8,128)S(1)}, f32[2,176,128]{2,1,0:T(8,128)S(1)}, u32[]{:S(2)}, u32[]{:S(2)}) collective-permute-start(f32[2,176,128]{2,1,0:T(8,128)S(1)} %pad_maximum_fusion.own), channel_id=1, source_target_pairs={{2,1},{4,3},{6,5},{8,7},{10,9},{12,11},{14,13},{16,15},{18,17},{20... | collective-permute-start | bytes 540680 | tf_op jit(solution)/shard_map/ppermute | solution.py:648
  64.7 7.5 %collective-permute-start.15 = (f32[16,128]{1,0:T(8,128)S(1)}, f32[16,128]{1,0:T(8,128)S(1)}, u32[]{:S(2)}, u32[]{:S(2)}) collective-permute-start(f32[16,128]{1,0:T(8,128)S(1)} %get-tuple-element.70), channel_id=1, source_target_pairs={{6,1},{8,3},{10,5},{12,7},{14,9},{16,11},{18,13},{20,15},{22,17},{... | collective-permute-start | bytes 24584 | tf_op jit(solution)/shard_map/ppermute | solution.py:649
  72.2 8.9 %collective-permute-start.18 = (f32[2,176,128]{2,1,0:T(8,128)S(1)}, f32[2,176,128]{2,1,0:T(8,128)S(1)}, u32[]{:S(2)}, u32[]{:S(2)}) collective-permute-start(f32[2,176,128]{2,1,0:T(8,128)S(1)} %collective-permute-done.17.far), channel_id=1, source_target_pairs={{0,1},{1,0},{2,3},{3,2},{4,5},{5,4},{6,7},{7,6},{8,9},{9,8},{10,11... | collective-permute-start | bytes 540680 | tf_op jit(solution)/shard_map/ppermute | solution.py:660
  79.9 1.2 %collective-permute-start.19 = (f32[16,128]{1,0:T(8,128)S(1)}, f32[16,128]{1,0:T(8,128)S(1)}, u32[]{:S(2)}, u32[]{:S(2)}) collective-permute-start(f32[16,128]{1,0:T(8,128)S(1)} %collective-permute-done.15.side), channel_id=1, source_target_pairs={{0,1},{1,0},{2,3},{3,2},{4,5},{5,4},{6,7},{7,6},{8,9},{9,8},{10,11... | collective-permute-start | bytes 24584 | tf_op jit(solution)/shard_map/ppermute | solution.py:661

commit v5 on v4

--- a/solution.py
+++ b/solution.py
@@ -134,7 +134,7 @@
         padded[y + 1, 40:41, :] = ghost[1, pl.ds(y, 1), :]
         return carry
 
-    lax.fori_loop(0, SPAN, layer, 0, unroll=4)
+    lax.fori_loop(0, SPAN, layer, 0, unroll=16)
 
 
 def around(y, t, padded, ghost):

time: 82.8 us -> 83.1 us (level); the launches traced: 81.7 us -> 83 us
  Pallas kernels: 16.8 us -> 18.1 us
    pallas_call x11, Pallas kernels: 16.8 us -> 18.1 us  [call(): pl.pallas_call(kernel, out_shape=out_shape, in_specs=list(leading) + (spe...]
where the time goes in v5:
time: 83.1 us; the launch traced here: 83 us
  starting transfers between devices  45.5 us (55%)
  waiting for transfers between devices  18.6 us (22%)
  Pallas kernels  18.1 us (22%)
    pallas_call x11, Pallas kernels, call(): pl.pallas_call(kernel, out_shape=out_shape, in_specs=list(leading) + (spe...  18.1 us
    ppermute x3, starting transfers between devices, exchange(): post = lax.ppermute(far, AXES, swap)  16.8 us
    ppermute x2, starting transfers between devices, shards(): post = lax.ppermute(far, AXES, swap)  10.8 us
    ppermute x3, waiting for transfers between devices, exchange(): far = lax.ppermute(sent, AXES, reach)  9.39 us
    ppermute x3, starting transfers between devices, exchange(): far = lax.ppermute(sent, AXES, reach)  5.73 us
    ppermute x1, starting transfers between devices, shards(): side = lax.ppermute(cross, AXES, beside)  3.64 us
    ppermute x1, starting transfers between devices, shards(): far = lax.ppermute(sent, AXES, reach)  3.4 us
    ppermute x1, waiting for transfers between devices, shards(): far = lax.ppermute(both, AXES, downward)  2.78 us
  transfers between devices with their start and end apart: 20, of which 11 were waited for; matrix products, arithmetic and copies ran while one was open for 0% of the time, Pallas kernels for 8%

profile of v5, /device:TPU:129, one launch (start us, length us, event | category | flops | bytes accessed | tf_op | source)
XLA Modules:
  0.0 83.0 jit_solution(9938109273251258822)
XLA Ops:
  0.6 2.3 %collect.1 = (s32[6]{0:T(128)S(4)}, f32[3,1024,128]{2,1,0:T(8,128)S(1)}, f32[12,32,128]{2,1,0:T(8,128)S(1)}) custom-call(s32[6,128]{1,0:T(8,128)} %bitcast.15, f32[128,1024]{1,0:T(8,128)} %bitcast.9, f32[128,1024]{1,0:T(8,128)} %bitcast.10, s32[128,1024]{1,0:T(8,128)} %bitcast.11), custom_call_target="tpu_custom_call" | custom-call | tf_op jit(solution)/shard_map/collect/pallas_call | solution.py:551
  2.9 0.8 collective-permute-start
  3.7 1.5 %collect_rest.1.own_rest = f32[2,1024,128]{2,1,0:T(8,128)S(1)} custom-call(f32[128,1024]{1,0:T(8,128)} %bitcast.12, f32[128,1024]{1,0:T(8,128)} %bitcast.13), custom_call_target="tpu_custom_call" | custom-call | tf_op jit(solution)/shard_map/collect_rest/pallas_call | solution.py:551
  5.2 0.3 face_window.1
  5.4 0.1 collective-permute-start.2
  5.5 0.5 collective-permute-start.3
  6.0 0.1 collective-permute-start.4
  6.1 3.4 %collective-permute-start.1 = (f32[5,32,128]{2,1,0:T(8,128)S(1)}, f32[5,32,128]{2,1,0:T(8,128)S(1)}, u32[]{:S(2)}, u32[]{:S(2)}) collective-permute-start(f32[5,32,128]{2,1,0:T(8,128)S(1)} %get-tuple-element.46), channel_id=1, source_target_pairs={{1,2},{3,4},{5,6},{7,8},{9,10},{11,12},{13,14},{15,16},{17,18},{19... | collective-permute-start | bytes 245768 | tf_op jit(solution)/shard_map/ppermute | solution.py:612
  9.5 0.9 %collective-permute-done.3.oth_rest = f32[2,1024,128]{2,1,0:T(8,128)S(1)} collective-permute-done((f32[2,1024,128]{2,1,0:T(8,128)S(1)}, f32[2,1024,128]{2,1,0:T(8,128)S(1)}, u32[]{:S(2)}, u32[]{:S(2)}) %collective-permute-start.3) | collective-permute-done | bytes 1048608 | tf_op jit(solution)/shard_map/ppermute | solution.py:617
  10.4 0.0 collective-permute-done.2.oth
  10.4 4.2 %window.1 = (f32[5,1024,128]{2,1,0:T(8,128)S(1)}, f32[5,1024,128]{2,1,0:T(8,128)S(1)}) custom-call(s32[6]{0:T(128)S(4)} %get-tuple-element.40.scalars, f32[3,1024,128]{2,1,0:T(8,128)S(1)} %get-tuple-element.47.own, f32[3,1024,128]{2,1,0:T(8,128)S(1)} %collective-permute-done.2.oth, f32[2,1024,128]{2,1,0:T(8,128)S(1)} %collect_rest.1.own_rest, ...), custom_call_target="tpu_custom_call" | custom-call | tf_op jit(solution)/shard_map/window/pallas_call | solution.py:551
  14.6 0.0 collective-permute-done.1.far
  14.6 3.1 %collective-permute-start.5 = (f32[5,32,128]{2,1,0:T(8,128)S(1)}, f32[5,32,128]{2,1,0:T(8,128)S(1)}, u32[]{:S(2)}, u32[]{:S(2)}) collective-permute-start(f32[5,32,128]{2,1,0:T(8,128)S(1)} %collective-permute-done.1.far), channel_id=1, source_target_pairs={{0,1},{1,0},{2,3},{3,2},{4,5},{5,4},{6,7},{7,6},{8,9},{9,8},{10,11... | collective-permute-start | bytes 245768 | tf_op jit(solution)/shard_map/ppermute | solution.py:621
  17.7 0.0 collective-permute-done.4.oth
  17.7 0.9 %collective-permute-done.5.post = f32[5,32,128]{2,1,0:T(8,128)S(1)} collective-permute-done((f32[5,32,128]{2,1,0:T(8,128)S(1)}, f32[5,32,128]{2,1,0:T(8,128)S(1)}, u32[]{:S(2)}, u32[]{:S(2)}) %collective-permute-start.5) | collective-permute-done | bytes 81952 | tf_op jit(solution)/shard_map/ppermute | solution.py:621
  18.6 1.8 %first.1 = (f32[1024,128]{1,0:T(8,128)S(1)}, f32[1024,128]{1,0:T(8,128)S(1)}, f32[1024,128]{1,0:T(8,128)S(1)}, f32[6,1024,128]{2,1,0:T(8,128)S(1)}, f32[4,32,128...) custom-call(s32[6]{0:T(128)S(4)} %get-tuple-element.40.scalars, ...), custom_call_target="tpu_custom_call" | custom-call | tf_op jit(solution)/shard_map/first/pallas_call | solution.py:551
  20.5 0.4 collective-permute-start.6
  20.9 1.9 %collective-permute-start.7 = (f32[32,128]{1,0:T(8,128)S(1)}, f32[32,128]{1,0:T(8,128)S(1)}, u32[]{:S(2)}, u32[]{:S(2)}) collective-permute-start(f32[32,128]{1,0:T(8,128)S(1)} %get-tuple-element.59), channel_id=1, source_target_pairs={{1,2},{3,4},{5,6},{7,8},{9,10},{11,12},{13,14},{15,16},{17,18},{19... | collective-permute-start | bytes 49160 | tf_op jit(solution)/shard_map/ppermute | solution.py:570
  22.8 3.1 %collective-permute-done.7.far = f32[32,128]{1,0:T(8,128)S(1)} collective-permute-done((f32[32,128]{1,0:T(8,128)S(1)}, f32[32,128]{1,0:T(8,128)S(1)}, u32[]{:S(2)}, u32[]{:S(2)}) %collective-permute-start.7) | collective-permute-done | bytes 16416 | tf_op jit(solution)/shard_map/ppermute | solution.py:570
  25.9 5.6 %collective-permute-start.8 = (f32[32,128]{1,0:T(8,128)S(1)}, f32[32,128]{1,0:T(8,128)S(1)}, u32[]{:S(2)}, u32[]{:S(2)}) collective-permute-start(f32[32,128]{1,0:T(8,128)S(1)} %collective-permute-done.7.far), channel_id=1, source_target_pairs={{0,1},{1,0},{2,3},{3,2},{4,5},{5,4},{6,7},{7,6},{8,9},{9,8},{10,11... | collective-permute-start | bytes 49160 | tf_op jit(solution)/shard_map/ppermute | solution.py:572
  31.5 0.8 %collective-permute-done.8.post = f32[32,128]{1,0:T(8,128)S(1)} collective-permute-done((f32[32,128]{1,0:T(8,128)S(1)}, f32[32,128]{1,0:T(8,128)S(1)}, u32[]{:S(2)}, u32[]{:S(2)}) %collective-permute-start.8) | collective-permute-done | bytes 16416 | tf_op jit(solution)/shard_map/ppermute | solution.py:572
  32.3 0.0 collective-permute-done.6.oth
  32.3 1.1 %sweep.3 = (f32[1024,128]{1,0:T(8,128)S(1)}, f32[4,32,128]{2,1,0:T(8,128)S(1)}, f32[32,128]{1,0:T(8,128)S(1)}) custom-call(s32[6]{0:T(128)S(4)} %get-tuple-element.40.scalars, f32[1024,128]{1,0:T(8,128)S(1)} %get-tuple-element.55.v, f32[1024,128]{1,0:T(8,128)S(1)} %get-tuple-element.56.f, f32[6,1024,128]{2,1,0:T(8,128)S(1)} %get-tuple-element.57.g, ...), custom_call_target="tpu_custom_call" | custom-call | tf_op jit(solution)/shard_map/sweep/pallas_call | solution.py:551
  33.4 0.4 collective-permute-start.9
  33.8 1.9 %collective-permute-start.10 = (f32[32,128]{1,0:T(8,128)S(1)}, f32[32,128]{1,0:T(8,128)S(1)}, u32[]{:S(2)}, u32[]{:S(2)}) collective-permute-start(f32[32,128]{1,0:T(8,128)S(1)} %get-tuple-element.62), channel_id=1, source_target_pairs={{1,2},{3,4},{5,6},{7,8},{9,10},{11,12},{13,14},{15,16},{17,18},{19... | collective-permute-start | bytes 49160 | tf_op jit(solution)/shard_map/ppermute | solution.py:570
  35.7 3.1 %collective-permute-done.10.far = f32[32,128]{1,0:T(8,128)S(1)} collective-permute-done((f32[32,128]{1,0:T(8,128)S(1)}, f32[32,128]{1,0:T(8,128)S(1)}, u32[]{:S(2)}, u32[]{:S(2)}) %collective-permute-start.10) | collective-permute-done | bytes 16416 | tf_op jit(solution)/shard_map/ppermute | solution.py:570
  38.9 5.6 %collective-permute-start.11 = (f32[32,128]{1,0:T(8,128)S(1)}, f32[32,128]{1,0:T(8,128)S(1)}, u32[]{:S(2)}, u32[]{:S(2)}) collective-permute-start(f32[32,128]{1,0:T(8,128)S(1)} %collective-permute-done.10.far), channel_id=1, source_target_pairs={{0,1},{1,0},{2,3},{3,2},{4,5},{5,4},{6,7},{7,6},{8,9},{9,8},{10,11... | collective-permute-start | bytes 49160 | tf_op jit(solution)/shard_map/ppermute | solution.py:572
  44.5 0.8 %collective-permute-done.11.post = f32[32,128]{1,0:T(8,128)S(1)} collective-permute-done((f32[32,128]{1,0:T(8,128)S(1)}, f32[32,128]{1,0:T(8,128)S(1)}, u32[]{:S(2)}, u32[]{:S(2)}) %collective-permute-start.11) | collective-permute-done | bytes 16416 | tf_op jit(solution)/shard_map/ppermute | solution.py:572
  45.3 0.0 collective-permute-done.9.oth
  45.3 1.1 %sweep.4 = (f32[1024,128]{1,0:T(8,128)S(1)}, f32[4,32,128]{2,1,0:T(8,128)S(1)}, f32[32,128]{1,0:T(8,128)S(1)}) custom-call(s32[6]{0:T(128)S(4)} %get-tuple-element.40.scalars, f32[1024,128]{1,0:T(8,128)S(1)} %get-tuple-element.60.v, f32[1024,128]{1,0:T(8,128)S(1)} %get-tuple-element.56.f, f32[6,1024,128]{2,1,0:T(8,128)S(1)} %get-tuple-element.57.g, ...), custom_call_target="tpu_custom_call" | custom-call | tf_op jit(solution)/shard_map/sweep/pallas_call | solution.py:551
  46.4 0.4 collective-permute-start.12
  46.8 1.9 %collective-permute-start.13 = (f32[32,128]{1,0:T(8,128)S(1)}, f32[32,128]{1,0:T(8,128)S(1)}, u32[]{:S(2)}, u32[]{:S(2)}) collective-permute-start(f32[32,128]{1,0:T(8,128)S(1)} %get-tuple-element.65), channel_id=1, source_target_pairs={{1,2},{3,4},{5,6},{7,8},{9,10},{11,12},{13,14},{15,16},{17,18},{19... | collective-permute-start | bytes 49160 | tf_op jit(solution)/shard_map/ppermute | solution.py:570
  48.7 3.1 %collective-permute-done.13.far = f32[32,128]{1,0:T(8,128)S(1)} collective-permute-done((f32[32,128]{1,0:T(8,128)S(1)}, f32[32,128]{1,0:T(8,128)S(1)}, u32[]{:S(2)}, u32[]{:S(2)}) %collective-permute-start.13) | collective-permute-done | bytes 16416 | tf_op jit(solution)/shard_map/ppermute | solution.py:570
  51.8 5.6 %collective-permute-start.14 = (f32[32,128]{1,0:T(8,128)S(1)}, f32[32,128]{1,0:T(8,128)S(1)}, u32[]{:S(2)}, u32[]{:S(2)}) collective-permute-start(f32[32,128]{1,0:T(8,128)S(1)} %collective-permute-done.13.far), channel_id=1, source_target_pairs={{0,1},{1,0},{2,3},{3,2},{4,5},{5,4},{6,7},{7,6},{8,9},{9,8},{10,11... | collective-permute-start | bytes 49160 | tf_op jit(solution)/shard_map/ppermute | solution.py:572
  57.4 0.8 %collective-permute-done.14.post = f32[32,128]{1,0:T(8,128)S(1)} collective-permute-done((f32[32,128]{1,0:T(8,128)S(1)}, f32[32,128]{1,0:T(8,128)S(1)}, u32[]{:S(2)}, u32[]{:S(2)}) %collective-permute-start.14) | collective-permute-done | bytes 16416 | tf_op jit(solution)/shard_map/ppermute | solution.py:572
  58.3 0.0 collective-permute-done.12.oth
  58.3 1.0 %sweep.5 = (f32[1024,128]{1,0:T(8,128)S(1)}, f32[4,32,128]{2,1,0:T(8,128)S(1)}) custom-call(s32[6]{0:T(128)S(4)} %get-tuple-element.40.scalars, f32[1024,128]{1,0:T(8,128)S(1)} %get-tuple-element.63.v, f32[1024,128]{1,0:T(8,128)S(1)} %get-tuple-element.56.f, f32[6,1024,128]{2,1,0:T(8,128)S(1)} %get-tuple-element.57.g, ...), custom_call_target="tpu_custom_call" | custom-call | tf_op jit(solution)/shard_map/sweep/pallas_call | solution.py:551
  59.3 1.8 %residual.1 = (f32[176,128]{1,0:T(8,128)S(1)}, f32[16,128]{1,0:T(8,128)S(1)}) custom-call(s32[6]{0:T(128)S(4)} %get-tuple-element.40.scalars, f32[1024,128]{1,0:T(8,128)S(1)} %get-tuple-element.72.v, f32[1024,128]{1,0:T(8,128)S(1)} %get-tuple-element.56.f, f32[6,1024,128]{2,1,0:T(8,128)S(1)} %get-tuple-element.57.g, f32[1024,128]{1,0:T(8,128)S(1)} %get-tuple-element.67.d, ...), custom_call_target="tpu_custom_call" | custom-call | tf_op jit(solution)/shard_map/residual/pallas_call | solution.py:551
  61.1 0.6 collective-permute-start.16
  61.7 0.9 %collective-permute-done.16 = f32[176,128]{1,0:T(8,128)S(1)} collective-permute-done((f32[176,128]{1,0:T(8,128)S(1)}, f32[176,128]{1,0:T(8,128)S(1)}, u32[]{:S(2)}, u32[]{:S(2)}) %collective-permute-start.16) | collective-permute-done | bytes 90144 | tf_op jit(solution)/shard_map/ppermute | solution.py:646
  62.7 1.9 %collective-permute-start.17 = (f32[2,176,128]{2,1,0:T(8,128)S(1)}, f32[2,176,128]{2,1,0:T(8,128)S(1)}, u32[]{:S(2)}, u32[]{:S(2)}) collective-permute-start(f32[2,176,128]{2,1,0:T(8,128)S(1)} %pad_maximum_fusion.own), channel_id=1, source_target_pairs={{2,1},{4,3},{6,5},{8,7},{10,9},{12,11},{14,13},{16,15},{18,17},{20... | collective-permute-start | bytes 540680 | tf_op jit(solution)/shard_map/ppermute | solution.py:648
  64.6 3.6 %collective-permute-start.15 = (f32[16,128]{1,0:T(8,128)S(1)}, f32[16,128]{1,0:T(8,128)S(1)}, u32[]{:S(2)}, u32[]{:S(2)}) collective-permute-start(f32[16,128]{1,0:T(8,128)S(1)} %get-tuple-element.70), channel_id=1, source_target_pairs={{6,1},{8,3},{10,5},{12,7},{14,9},{16,11},{18,13},{20,15},{22,17},{... | collective-permute-start | bytes 24584 | tf_op jit(solution)/shard_map/ppermute | solution.py:649
  68.3 2.8 %collective-permute-done.17.far = f32[2,176,128]{2,1,0:T(8,128)S(1)} collective-permute-done((f32[2,176,128]{2,1,0:T(8,128)S(1)}, f32[2,176,128]{2,1,0:T(8,128)S(1)}, u32[]{:S(2)}, u32[]{:S(2)}) %collective-permute-start.17) | collective-permute-done | bytes 180256 | tf_op jit(solution)/shard_map/ppermute | solution.py:648
  71.1 1.0 %level.1 = f32[4,32,1024]{2,1,0:T(8,128)} custom-call(s32[6]{0:T(128)S(4)} %get-tuple-element.40.scalars, f32[1024,128]{1,0:T(8,128)S(1)} %get-tuple-element.72.v), custom_call_target="tpu_custom_call" | custom-call | tf_op jit(solution)/shard_map/level/pallas_call | solution.py:551
  72.1 7.7 %collective-permute-start.18 = (f32[2,176,128]{2,1,0:T(8,128)S(1)}, f32[2,176,128]{2,1,0:T(8,128)S(1)}, u32[]{:S(2)}, u32[]{:S(2)}) collective-permute-start(f32[2,176,128]{2,1,0:T(8,128)S(1)} %collective-permute-done.17.far), channel_id=1, source_target_pairs={{0,1},{1,0},{2,3},{3,2},{4,5},{5,4},{6,7},{7,6},{8,9},{9,8},{10,11... | collective-permute-start | bytes 540680 | tf_op jit(solution)/shard_map/ppermute | solution.py:660
  79.8 0.0 collective-permute-start.19
  79.8 1.2 %collective-permute-done.19.side_post = f32[16,128]{1,0:T(8,128)S(1)} collective-permute-done((f32[16,128]{1,0:T(8,128)S(1)}, f32[16,128]{1,0:T(8,128)S(1)}, u32[]{:S(2)}, u32[]{:S(2)}) %collective-permute-start.19) | collective-permute-done | bytes 8224 | tf_op jit(solution)/shard_map/ppermute | solution.py:661
  81.0 2.0 %coarse.1 = f32[1,32,1024]{2,1,0:T(8,128)} custom-call(s32[6]{0:T(128)S(4)} %get-tuple-element.40.scalars, f32[2,176,128]{2,1,0:T(8,128)S(1)} %pad_maximum_fusion.own, f32[2,176,128]{2,1,0:T(8,128)S(1)} %collective-permute-done.17.far, f32[2,176,128]{2,1,0:T(8,128)S(1)} %collective-permute-done.18.post, f32[16,128]{1,0:T(8,128)S(1)} %collective-permute-done.15.side, ...), custom_call_target="tpu_custom_call" | custom-call | tf_op jit(solution)/shard_map/coarse/pallas_call | solution.py:551
  (4 shorter events, 0.0 us)
Async XLA Ops:
  2.9 2.2 %collective-permute-start = (f32[12,32,128]{2,1,0:T(8,128)S(1)}, f32[12,32,128]{2,1,0:T(8,128)S(1)}, u32[]{:S(2)}, u32[]{:S(2)}) collective-permute-start(f32[12,32,128]{2,1,0:T(8,128)S(1)} %get-tuple-element.41.own), channel_id=1, source_target_pairs={{0,1},{1,0},{2,3},{3,2},{4,5},{5,4},{6,7},{7,6},{8,9},{9,8},{10,11... | collective-permute-start | bytes 589832 | tf_op jit(solution)/shard_map/ppermute | solution.py:604
  5.4 5.0 %collective-permute-start.2 = (f32[3,1024,128]{2,1,0:T(8,128)S(1)}, f32[3,1024,128]{2,1,0:T(8,128)S(1)}, u32[]{:S(2)}, u32[]{:S(2)}) collective-permute-start(f32[3,1024,128]{2,1,0:T(8,128)S(1)} %get-tuple-element.47.own), channel_id=1, source_target_pairs={{0,1},{1,0},{2,3},{3,2},{4,5},{5,4},{6,7},{7,6},{8,9},{9,8},{10,11... | collective-permute-start | bytes 4718600 | tf_op jit(solution)/shard_map/ppermute | solution.py:617
  5.5 4.9 %collective-permute-start.3 = (f32[2,1024,128]{2,1,0:T(8,128)S(1)}, f32[2,1024,128]{2,1,0:T(8,128)S(1)}, u32[]{:S(2)}, u32[]{:S(2)}) collective-permute-start(f32[2,1024,128]{2,1,0:T(8,128)S(1)} %collect_rest.1.own_rest), channel_id=1, source_target_pairs={{0,1},{1,0},{2,3},{3,2},{4,5},{5,4},{6,7},{7,6},{8,9},{9,8},{10,11... | collective-permute-start | bytes 3145736 | tf_op jit(solution)/shard_map/ppermute | solution.py:617
  6.0 11.7 %collective-permute-start.4 = (f32[12,32,128]{2,1,0:T(8,128)S(1)}, f32[12,32,128]{2,1,0:T(8,128)S(1)}, u32[]{:S(2)}, u32[]{:S(2)}) collective-permute-start(f32[12,32,128]{2,1,0:T(8,128)S(1)} %get-tuple-element.53.own), channel_id=1, source_target_pairs={{0,1},{1,0},{2,3},{3,2},{4,5},{5,4},{6,7},{7,6},{8,9},{9,8},{10,11... | collective-permute-start | bytes 589832 | tf_op jit(solution)/shard_map/ppermute | solution.py:613
  6.1 8.5 %collective-permute-start.1 = (f32[5,32,128]{2,1,0:T(8,128)S(1)}, f32[5,32,128]{2,1,0:T(8,128)S(1)}, u32[]{:S(2)}, u32[]{:S(2)}) collective-permute-start(f32[5,32,128]{2,1,0:T(8,128)S(1)} %get-tuple-element.46), channel_id=1, source_target_pairs={{1,2},{3,4},{5,6},{7,8},{9,10},{11,12},{13,14},{15,16},{17,18},{19... | collective-permute-start | bytes 245768 | tf_op jit(solution)/shard_map/ppermute | solution.py:612
  14.6 4.0 %collective-permute-start.5 = (f32[5,32,128]{2,1,0:T(8,128)S(1)}, f32[5,32,128]{2,1,0:T(8,128)S(1)}, u32[]{:S(2)}, u32[]{:S(2)}) collective-permute-start(f32[5,32,128]{2,1,0:T(8,128)S(1)} %collective-permute-done.1.far), channel_id=1, source_target_pairs={{0,1},{1,0},{2,3},{3,2},{4,5},{5,4},{6,7},{7,6},{8,9},{9,8},{10,11... | collective-permute-start | bytes 245768 | tf_op jit(solution)/shard_map/ppermute | solution.py:621
  20.5 11.9 %collective-permute-start.6 = (f32[4,32,128]{2,1,0:T(8,128)S(1)}, f32[4,32,128]{2,1,0:T(8,128)S(1)}, u32[]{:S(2)}, u32[]{:S(2)}) collective-permute-start(f32[4,32,128]{2,1,0:T(8,128)S(1)} %get-tuple-element.58.own), channel_id=1, source_target_pairs={{0,1},{1,0},{2,3},{3,2},{4,5},{5,4},{6,7},{7,6},{8,9},{9,8},{10,11... | collective-permute-start | bytes 196616 | tf_op jit(solution)/shard_map/ppermute | solution.py:571
  20.9 5.0 %collective-permute-start.7 = (f32[32,128]{1,0:T(8,128)S(1)}, f32[32,128]{1,0:T(8,128)S(1)}, u32[]{:S(2)}, u32[]{:S(2)}) collective-permute-start(f32[32,128]{1,0:T(8,128)S(1)} %get-tuple-element.59), channel_id=1, source_target_pairs={{1,2},{3,4},{5,6},{7,8},{9,10},{11,12},{13,14},{15,16},{17,18},{19... | collective-permute-start | bytes 49160 | tf_op jit(solution)/shard_map/ppermute | solution.py:570
  25.9 6.4 %collective-permute-start.8 = (f32[32,128]{1,0:T(8,128)S(1)}, f32[32,128]{1,0:T(8,128)S(1)}, u32[]{:S(2)}, u32[]{:S(2)}) collective-permute-start(f32[32,128]{1,0:T(8,128)S(1)} %collective-permute-done.7.far), channel_id=1, source_target_pairs={{0,1},{1,0},{2,3},{3,2},{4,5},{5,4},{6,7},{7,6},{8,9},{9,8},{10,11... | collective-permute-start | bytes 49160 | tf_op jit(solution)/shard_map/ppermute | solution.py:572
  33.4 11.9 %collective-permute-start.9 = (f32[4,32,128]{2,1,0:T(8,128)S(1)}, f32[4,32,128]{2,1,0:T(8,128)S(1)}, u32[]{:S(2)}, u32[]{:S(2)}) collective-permute-start(f32[4,32,128]{2,1,0:T(8,128)S(1)} %get-tuple-element.61.own), channel_id=1, source_target_pairs={{0,1},{1,0},{2,3},{3,2},{4,5},{5,4},{6,7},{7,6},{8,9},{9,8},{10,11... | collective-permute-start | bytes 196616 | tf_op jit(solution)/shard_map/ppermute | solution.py:571
  33.8 5.0 %collective-permute-start.10 = (f32[32,128]{1,0:T(8,128)S(1)}, f32[32,128]{1,0:T(8,128)S(1)}, u32[]{:S(2)}, u32[]{:S(2)}) collective-permute-start(f32[32,128]{1,0:T(8,128)S(1)} %get-tuple-element.62), channel_id=1, source_target_pairs={{1,2},{3,4},{5,6},{7,8},{9,10},{11,12},{13,14},{15,16},{17,18},{19... | collective-permute-start | bytes 49160 | tf_op jit(solution)/shard_map/ppermute | solution.py:570
  38.9 6.4 %collective-permute-start.11 = (f32[32,128]{1,0:T(8,128)S(1)}, f32[32,128]{1,0:T(8,128)S(1)}, u32[]{:S(2)}, u32[]{:S(2)}) collective-permute-start(f32[32,128]{1,0:T(8,128)S(1)} %collective-permute-done.10.far), channel_id=1, source_target_pairs={{0,1},{1,0},{2,3},{3,2},{4,5},{5,4},{6,7},{7,6},{8,9},{9,8},{10,11... | collective-permute-start | bytes 49160 | tf_op jit(solution)/shard_map/ppermute | solution.py:572
  46.4 11.9 %collective-permute-start.12 = (f32[4,32,128]{2,1,0:T(8,128)S(1)}, f32[4,32,128]{2,1,0:T(8,128)S(1)}, u32[]{:S(2)}, u32[]{:S(2)}) collective-permute-start(f32[4,32,128]{2,1,0:T(8,128)S(1)} %get-tuple-element.64.own), channel_id=1, source_target_pairs={{0,1},{1,0},{2,3},{3,2},{4,5},{5,4},{6,7},{7,6},{8,9},{9,8},{10,11... | collective-permute-start | bytes 196616 | tf_op jit(solution)/shard_map/ppermute | solution.py:571
  46.8 5.0 %collective-permute-start.13 = (f32[32,128]{1,0:T(8,128)S(1)}, f32[32,128]{1,0:T(8,128)S(1)}, u32[]{:S(2)}, u32[]{:S(2)}) collective-permute-start(f32[32,128]{1,0:T(8,128)S(1)} %get-tuple-element.65), channel_id=1, source_target_pairs={{1,2},{3,4},{5,6},{7,8},{9,10},{11,12},{13,14},{15,16},{17,18},{19... | collective-permute-start | bytes 49160 | tf_op jit(solution)/shard_map/ppermute | solution.py:570
  51.8 6.4 %collective-permute-start.14 = (f32[32,128]{1,0:T(8,128)S(1)}, f32[32,128]{1,0:T(8,128)S(1)}, u32[]{:S(2)}, u32[]{:S(2)}) collective-permute-start(f32[32,128]{1,0:T(8,128)S(1)} %collective-permute-done.13.far), channel_id=1, source_target_pairs={{0,1},{1,0},{2,3},{3,2},{4,5},{5,4},{6,7},{7,6},{8,9},{9,8},{10,11... | collective-permute-start | bytes 49160 | tf_op jit(solution)/shard_map/ppermute | solution.py:572
  61.1 1.6 %collective-permute-start.16 = (f32[176,128]{1,0:T(8,128)S(1)}, f32[176,128]{1,0:T(8,128)S(1)}, u32[]{:S(2)}, u32[]{:S(2)}) collective-permute-start(f32[176,128]{1,0:T(8,128)S(1)} %get-tuple-element.71), channel_id=1, source_target_pairs={{0,1},{1,0},{2,3},{3,2},{4,5},{5,4},{6,7},{7,6},{8,9},{9,8},{10,11... | collective-permute-start | bytes 270344 | tf_op jit(solution)/shard_map/ppermute | solution.py:646
  62.7 8.4 %collective-permute-start.17 = (f32[2,176,128]{2,1,0:T(8,128)S(1)}, f32[2,176,128]{2,1,0:T(8,128)S(1)}, u32[]{:S(2)}, u32[]{:S(2)}) collective-permute-start(f32[2,176,128]{2,1,0:T(8,128)S(1)} %pad_maximum_fusion.own), channel_id=1, source_target_pairs={{2,1},{4,3},{6,5},{8,7},{10,9},{12,11},{14,13},{16,15},{18,17},{20... | collective-permute-start | bytes 540680 | tf_op jit(solution)/shard_map/ppermute | solution.py:648
  64.6 7.5 %collective-permute-start.15 = (f32[16,128]{1,0:T(8,128)S(1)}, f32[16,128]{1,0:T(8,128)S(1)}, u32[]{:S(2)}, u32[]{:S(2)}) collective-permute-start(f32[16,128]{1,0:T(8,128)S(1)} %get-tuple-element.70), channel_id=1, source_target_pairs={{6,1},{8,3},{10,5},{12,7},{14,9},{16,11},{18,13},{20,15},{22,17},{... | collective-permute-start | bytes 24584 | tf_op jit(solution)/shard_map/ppermute | solution.py:649
  72.1 8.9 %collective-permute-start.18 = (f32[2,176,128]{2,1,0:T(8,128)S(1)}, f32[2,176,128]{2,1,0:T(8,128)S(1)}, u32[]{:S(2)}, u32[]{:S(2)}) collective-permute-start(f32[2,176,128]{2,1,0:T(8,128)S(1)} %collective-permute-done.17.far), channel_id=1, source_target_pairs={{0,1},{1,0},{2,3},{3,2},{4,5},{5,4},{6,7},{7,6},{8,9},{9,8},{10,11... | collective-permute-start | bytes 540680 | tf_op jit(solution)/shard_map/ppermute | solution.py:660
  79.8 1.2 %collective-permute-start.19 = (f32[16,128]{1,0:T(8,128)S(1)}, f32[16,128]{1,0:T(8,128)S(1)}, u32[]{:S(2)}, u32[]{:S(2)}) collective-permute-start(f32[16,128]{1,0:T(8,128)S(1)} %collective-permute-done.15.side), channel_id=1, source_target_pairs={{0,1},{1,0},{2,3},{3,2},{4,5},{5,4},{6,7},{7,6},{8,9},{9,8},{10,11... | collective-permute-start | bytes 24584 | tf_op jit(solution)/shard_map/ppermute | solution.py:661
